TPU v7x, 32 devices: a whole 2x2x4 slice. The times are simulated.
32 devices in a mesh: tile: 16 (over z, x, core), grp: 2 (over y).
Axes of the slice: x: 2, y: 2, z: 4, core: 2. Of those that a mesh axis runs over, the one named last changes fastest.
Arguments:
- traces: float32 [128, 16, 1500], P(('tile', 'grp')), may hold values from -6 to 6
- validity: int32 [128, 16], P(('tile', 'grp')), may hold values 0 or 1
- boundary_rows: int32 [32, 2, 4], P(('tile', 'grp')), may hold values from 0 to 3, as said below
- boundary_count: int32 [32, 2], P(('tile', 'grp')), may hold values from 1 to 4, as said below
- pair_mask: int32 [128, 24], P(('tile', 'grp')), may hold values from 0 to 1, as said below
Outputs:
- correlations: bfloat16 [128, 24, 2001], P(('tile', 'grp'))
Inputs may be any that keep to these rules, and one draw needn't show every extreme that they name: `boundary_rows`: each device's list in each direction orders all of its 4 local stations, each once. `boundary_count`: in every draw some device sends all 4 of its stations in each direction. `pair_mask`: a station's column for itself is 0.
All inputs are finite; a program needn't handle non-finite values. No bound on the sum of `validity` on one device may be relied on, other than what follows from the above.
Results may differ from a plain program's by a relative error of at most 0.008.
Values may be sent and summed in bfloat16 or wider, within the bound.
No kernel may reach another device: no remote copies, remote signals or barrier semaphores. Data moves between devices by JAX's collectives and lax.ppermute only.
A program may use at most 64 MiB of HBM per device.

v0:
```python
import math

import jax
import jax.numpy as jnp
from jax import lax
from jax.sharding import PartitionSpec as P

SAMP = 1500
NBIN = 144
MAXLAG = 1000
LAGS = 2001


def passed_along(array, axis, by):
    count = lax.axis_size(axis)
    pairs = [(i, i + by) for i in range(count) if 0 <= i + by < count]
    return lax.ppermute(array, axis, pairs)


def fourier_table(samples):
    points = 2 * samples
    sample_number = jnp.arange(samples, dtype=jnp.int32)[:, None]
    freq_number = jnp.arange(1, NBIN + 1, dtype=jnp.int32)[None, :]
    angles = jnp.mod(sample_number * freq_number, points).astype(jnp.float32) * (
        2.0 * jnp.pi / points
    )
    return jnp.concatenate([jnp.cos(angles), -jnp.sin(angles)], axis=1)


def lag_basis():
    points = 2 * SAMP
    freq_number = jnp.arange(1, NBIN + 1, dtype=jnp.int32)[:, None]
    lag_number = jnp.arange(LAGS, dtype=jnp.int32)[None, :] - MAXLAG
    angles = jnp.mod(freq_number * lag_number, points).astype(jnp.float32) * (2.0 * jnp.pi / points)
    return jnp.concatenate([jnp.cos(angles), -jnp.sin(angles)], axis=0)


def whitened(traces, valid_float):
    stations, segments, samples = traces.shape
    sample_number = jnp.arange(samples, dtype=jnp.float32)
    hann_taper = 0.5 - 0.5 * jnp.cos(sample_number * (2.0 * jnp.pi / samples))
    flat_traces = (traces * hann_taper).reshape(stations * segments, samples)
    spectrum = jnp.dot(
        flat_traces,
        fourier_table(samples),
        precision=lax.Precision.HIGHEST,
        preferred_element_type=jnp.float32,
    )
    spectrum = spectrum.reshape(stations, segments, 2, NBIN)
    real_part = spectrum[:, :, 0]
    imag_part = spectrum[:, :, 1]
    power_bins = real_part * real_part + imag_part * imag_part
    padded = jnp.pad(power_bins, ((0, 0), (0, 0), (4, 4)))
    smooth = sum((padded[:, :, offset : offset + NBIN] for offset in range(9))) / 9.0
    mean_power = jnp.mean(power_bins, axis=2, keepdims=True)
    factor = valid_float[:, :, None] / jnp.sqrt(0.5 * smooth + 0.5 * mean_power + 1e-06)
    return jnp.stack([real_part * factor, imag_part * factor], axis=2).astype(jnp.bfloat16)


def stacked(left_spec, left_mask, right_spec, right_mask):
    left_both = jnp.concatenate([left_spec[:, :, 0], left_spec[:, :, 1]], axis=1)
    right_real = right_spec[:, :, 0]
    right_imag = right_spec[:, :, 1]
    right_both = jnp.stack(
        [
            jnp.concatenate([right_real, right_imag], axis=1),
            jnp.concatenate([-right_imag, right_real], axis=1),
        ],
        axis=1,
    )
    product = jnp.einsum(
        "iqf,jcqf->ijcf", left_both, right_both, preferred_element_type=jnp.float32
    )
    pair_count = jnp.einsum("iq,jq->ij", left_mask, right_mask, preferred_element_type=jnp.float32)
    return (product / jnp.maximum(pair_count, 1.0)[:, :, None, None]).astype(jnp.bfloat16)


def on_device(traces, validity, boundary_rows, boundary_count, pair_mask):
    per_device = traces.shape[0]
    valid_float = validity.astype(jnp.float32)
    valid_half = validity.astype(jnp.bfloat16)
    own_spec = whitened(traces, valid_float)
    slot_number = jnp.arange(per_device, dtype=jnp.int32)
    live_up = (slot_number < boundary_count[0, 0]).astype(jnp.float32)
    live_down = (slot_number < boundary_count[0, 1]).astype(jnp.float32)
    picks_up = boundary_rows[0, 0]
    picks_down = boundary_rows[0, 1]
    below_traces, below_mask = passed_along(
        (
            jnp.take(traces, picks_up, axis=0) * live_up[:, None, None],
            jnp.take(valid_float, picks_up, axis=0) * live_up[:, None],
        ),
        "tile",
        1,
    )
    above_traces, above_mask = passed_along(
        (
            jnp.take(traces, picks_down, axis=0) * live_down[:, None, None],
            jnp.take(valid_float, picks_down, axis=0) * live_down[:, None],
        ),
        "tile",
        -1,
    )
    recv_spec = whitened(
        jnp.concatenate([below_traces, above_traces], axis=0),
        jnp.concatenate([below_mask, above_mask], axis=0),
    )
    recv_mask = jnp.concatenate([below_mask, above_mask], axis=0).astype(jnp.bfloat16)
    local_spec = jnp.concatenate([own_spec, recv_spec], axis=0)
    local_mask = jnp.concatenate([valid_half, recv_mask], axis=0)
    all_spec, all_mask = (
        lax.all_gather(local_spec, "grp", axis=0, tiled=True),
        lax.all_gather(local_mask, "grp", axis=0, tiled=True),
    )
    cross_spec = stacked(own_spec, valid_half, all_spec, all_mask)
    columns = cross_spec.shape[1]
    basis = lag_basis()
    basis_high = basis.astype(jnp.bfloat16)
    basis_low = (basis - basis_high.astype(jnp.float32)).astype(jnp.bfloat16)
    flat_cross = cross_spec.reshape(per_device * columns, 2 * NBIN)
    series = jnp.dot(flat_cross, basis_high, preferred_element_type=jnp.float32)
    series = series + jnp.dot(flat_cross, basis_low, preferred_element_type=jnp.float32)
    series = series.reshape(per_device, columns, -1)
    scaled = series * (pair_mask.astype(jnp.float32) / math.sqrt(NBIN))[:, :, None]
    return scaled.astype(jnp.bfloat16)


def solution(mesh):
    return jax.shard_map(
        on_device,
        mesh=mesh,
        in_specs=(
            P(("tile", "grp"), None, None),
            P(("tile", "grp"), None),
            P(("tile", "grp"), None, None),
            P(("tile", "grp"), None),
            P(("tile", "grp"), None),
        ),
        out_specs=P(("tile", "grp"), None, None),
        check_vma=False,
    )
```

profile of v0, /device:TPU:3, one launch (start us, length us, event | category | flops | bytes accessed | tf_op | source)
XLA Modules:
  0.0 57.5 jit_solution(16336578575007352829)
XLA Ops:
  0.0 1.3 %fusion.41 = (s32[1,1]{1,0:T(1,128)}, s32[1,1]{1,0:T(1,128)}) fusion(s32[1,2]{1,0:T(1,128)} %param.12), kind=kLoop, calls=%fused_computation.102 | loop fusion | bytes 16 | tf_op jit(solution)/shard_map/slice | solution.py:84
  1.3 1.3 %compare_and_fusion.1 = (pred[4]{0:T(512)(128)(4,1)S(1)}, s32[4]{0:T(128)S(1)}, pred[4]{0:T(512)(128)(4,1)S(1)}, s32[4]{0:T(128)S(1)}, f32[4]{0:T(128)S(1)}) fusion(s32[1,2,4]{2,1,0:T(2,128)} %param.11, s32[]{:T(128)} %bitcast.12), kind=kLoop, calls=%fused_computation.89 | loop fusion | flops 56 | bytes 92 | tf_op jit(solution)/shard_map/jit(_take)/and | solution.py:90
  2.6 1.6 %gather_fusion.1 = f32[4,16,1500]{2,1,0:T(8,128)S(1)} fusion(f32[4,16,1500]{2,1,0:T(8,128)} %param.9, s32[1024]{0:T(1024)S(1)} %pad_clamp_fusion), kind=kCustom, calls=%fused_computation.2.clone | custom fusion | bytes 768016 | tf_op jit(solution)/shard_map/jit(_take)/gather | solution.py:98
  4.3 2.6 %collective-permute-start.1 = (f32[4,16,1500]{2,1,0:T(8,128)S(1)}, f32[4,16,1500]{2,1,0:T(8,128)}, u32[]{:S(2)}, u32[]{:S(2)}) collective-permute-start(f32[4,16,1500]{2,1,0:T(8,128)S(1)} %select_multiply_fusion), channel_id=1, source_target_pairs={{2,0},{4,2},{6,4},{8,6},{10,8},{12,10},{14,12},{16,14},{18,16},{20... | collective-permute-start | bytes 1152008 | tf_op jit(solution)/shard_map/ppermute | solution.py:17
  7.0 0.6 gather_fusion
  7.5 0.7 %compare_convert_fusion.1 = f32[4]{0:T(128)S(1)} fusion(s32[]{:T(128)} %bitcast.10), kind=kLoop, calls=%fused_computation.91 | loop fusion | flops 8 | bytes 20 | tf_op jit(solution)/shard_map/convert_element_type | solution.py:84
  8.2 0.8 %select_multiply_fusion.1 = f32[4,16,1500]{2,1,0:T(8,128)} fusion(f32[4,16,1500]{2,1,0:T(8,128)S(1)} %gather_fusion, f32[4]{0:T(128)S(1)} %compare_convert_fusion.1, pred[4]{0:T(512)(128)(4,1)S(1)} %get-tuple-element.15), kind=kLoop, calls=%fused_computation.42 | loop fusion | flops 192000 | bytes 768020 | tf_op jit(solution)/shard_map/mul | solution.py:90
  9.0 3.9 %collective-permute-start = (f32[4,16,1500]{2,1,0:T(8,128)}, f32[4,16,1500]{2,1,0:T(8,128)}, u32[]{:S(2)}, u32[]{:S(2)}) collective-permute-start(f32[4,16,1500]{2,1,0:T(8,128)} %select_multiply_fusion.1), channel_id=1, source_target_pairs={{0,2},{2,4},{4,6},{6,8},{8,10},{10,12},{12,14},{14,16},{16,18},{18... | collective-permute-start | bytes 1152008 | tf_op jit(solution)/shard_map/ppermute | solution.py:17
  12.9 0.6 gather_fusion.3
  13.6 1.9 %collective-permute-start.3 = (f32[4,16]{1,0:T(4,128)S(1)}, f32[4,16]{1,0:T(4,128)S(1)}, u32[]{:S(2)}, u32[]{:S(2)}) collective-permute-start(f32[4,16]{1,0:T(4,128)S(1)} %select_multiply_fusion.2), channel_id=1, source_target_pairs={{2,0},{4,2},{6,4},{8,6},{10,8},{12,10},{14,12},{16,14},{18,16},{20... | collective-permute-start | bytes 776 | tf_op jit(solution)/shard_map/ppermute | solution.py:17
  15.5 0.6 gather_fusion.2
  16.1 4.5 %collective-permute-start.2 = (f32[4,16]{1,0:T(4,128)S(1)}, f32[4,16]{1,0:T(4,128)S(1)}, u32[]{:S(2)}, u32[]{:S(2)}) collective-permute-start(f32[4,16]{1,0:T(4,128)S(1)} %select_multiply_fusion.3), channel_id=1, source_target_pairs={{0,2},{2,4},{4,6},{6,8},{8,10},{10,12},{12,14},{14,16},{16,18},{18... | collective-permute-start | bytes 776 | tf_op jit(solution)/shard_map/ppermute | solution.py:17
  20.8 3.7 %fusion.14 = (f32[1500,144]{0,1:T(8,128)S(1)}, f32[1500,144]{0,1:T(8,128)S(1)}) fusion(s32[144]{0:T(256)S(1)} %iota_add_fusion.1), kind=kLoop, calls=%fused_computation.28 | loop fusion | flops 2160000 | bytes 1728576 | tf_op jit(solution)/shard_map/cos | solution.py:27
  24.5 1.9 %fusion.21 = f32[4,16,2,144]{3,1,2,0:T(8,128)S(1)} fusion(f32[2,144,1500,1]{2,1,0,3:T(8,128)S(1)} %bitcast.94, f32[4,16,1500]{2,1,0:T(8,128)S(1)} %copy-done.1, f32[1500]{0:T(1024)S(1)} %multiply_subtract_fusion), kind=kOutput, calls=%fused_computation.39 | convolution fusion | flops 331872000 | bytes 2191728 | tf_op jit(solution)/shard_map/dot_general | solution.py:43
  26.8 6.0 %fusion.7 = (f32[144,2001]{1,0:T(8,128)S(1)}, f32[144,2001]{1,0:T(8,128)}) fusion(s32[2001]{0:T(1024)S(1)} %iota_add_fusion, s32[144]{0:T(256)S(1)} %iota_add_fusion.1), kind=kLoop, calls=%fused_computation.18 | loop fusion | flops 2881440 | bytes 2313732 | tf_op jit(solution)/shard_map/cos | solution.py:35
  32.9 0.8 %copy.31 = bf16[4,32,144,1]{1,0,3,2:T(4,128)(2,1)} copy(bf16[4,32,144,1]{2,1,0,3:T(8,128)(2,1)S(1)} %maximum_bitcast_fusion.2) | data formatting | bytes 73728 | tf_op jit(solution)/shard_map/concatenate | solution.py:61
  33.7 3.2 %all-gather = bf16[2,12,16]{2,1,0:T(8,128)(2,1)S(1)} all-gather(bf16[1,12,16]{2,1,0:T(8,128)(2,1)S(1)} %maximum_bitcast_fusion.3), channel_id=1, replica_groups=mesh['tile'=16,'grp'=2] {'grp'}, dimensions={0}, use_global_device_ids=true | all-gather | bytes 1152 | tf_op jit(solution)/shard_map/all_gather | solution.py:113
  37.1 2.7 %fusion.17 = f32[8,16,2,144]{3,1,2,0:T(8,128)S(1)} fusion(f32[2,144,1500,1]{2,1,0,3:T(8,128)S(1)} %bitcast.95, f32[4,16,1500]{2,1,0:T(8,128)} %collective-permute-done.1, f32[4,16,1500]{2,1,0:T(8,128)} %collective-permute-done, f32[1500]{0:T(1024)S(1)} %multiply_subtract_fusion), kind=kOutput, calls=%fused_computation.32 | convolution fusion | flops 663936000 | bytes 2649456 | tf_op jit(solution)/shard_map/dot_general | solution.py:43
  40.4 7.0 %all_gather.6 = bf16[24,16,2,144]{3,1,0,2:T(8,128)(2,1)S(1)} all-gather(bf16[12,16,2,144]{3,1,0,2:T(8,128)(2,1)S(1)} %maximum_maximum_fusion), channel_id=1, replica_groups=mesh['tile'=16,'grp'=2] {'grp'}, dimensions={0}, use_global_device_ids=true | all-gather | bytes 331776 | tf_op jit(solution)/shard_map/all_gather | solution.py:112
  47.6 1.1 %pad_maximum_fusion.2 = bf16[24,2,32,144]{3,2,0,1:T(8,128)(2,1)} fusion(bf16[24,1,32,144]{3,2,0,1:T(8,128)(2,1)S(1)} %get-tuple-element.22, bf16[24,1,32,144]{3,2,0,1:T(8,128)(2,1)S(1)} %get-tuple-element.21), kind=kLoop, calls=%fused_computation.35 | loop fusion | flops 221184 | bytes 884736 | tf_op jit(solution)/shard_map/stack | solution.py:64
  48.6 2.0 %copy.24 = bf16[24,2,32,144]{2,0,1,3:T(8,128)(2,1)S(1)} copy(bf16[24,2,32,144]{3,2,0,1:T(8,128)(2,1)} %pad_maximum_fusion.2) | data formatting | bytes 884736 | tf_op jit(solution)/shard_map/stack | solution.py:64
  50.7 3.9 %fusion.42 = f32[144,24,2,4]{1,3,2,0:T(4,128)S(1)} fusion(bf16[24,2,32,144]{2,0,1,3:T(8,128)(2,1)S(1)} %copy.24, bf16[4,32,144,1]{1,0,3,2:T(4,128)(2,1)} %copy.31), kind=kOutput, calls=%fused_computation.103 | convolution fusion | flops 1769472 | bytes 589824 | tf_op jit(solution)/shard_map/iqf,jcqf->ijcf/dot_general | solution.py:71
  55.2 0.6 %copy-done = f32[144,2001]{1,0:T(8,128)S(1)} copy-done((f32[144,2001]{1,0:T(8,128)S(1)}, f32[144,2001]{1,0:T(8,128)}, u32[]{:S(2)}) %copy-start) | copy-done | bytes 1152600
  56.7 0.9 %multiply_convert_fusion = bf16[4,24,2001]{2,1,0:T(8,128)(2,1)} fusion(f32[4,24,2001]{2,1,0:T(8,128)S(1)} %bitcast.96, f32[4,24]{1,0:T(4,128)S(1)} %convert_multiply_fusion), kind=kLoop, calls=%fused_computation.36 | loop fusion | flops 384192 | bytes 1152960 | tf_op jit(solution)/shard_map/convert_element_type | solution.py:125
  (46 shorter events, 3.2 us)
Async XLA Ops:
  0.0 7.0 %copy-start.1 = (f32[4,16,1500]{2,1,0:T(8,128)S(1)}, f32[4,16,1500]{2,1,0:T(8,128)}, u32[]{:S(2)}) copy-start(f32[4,16,1500]{2,1,0:T(8,128)} %param.9) | copy-start | bytes 1152004
  4.2 8.7 %copy-start.2 = (s32[4,16]{1,0:T(4,128)S(1)}, s32[4,16]{1,0:T(4,128)}, u32[]{:S(2)}) copy-start(s32[4,16]{1,0:T(4,128)} %param.10) | copy-start | bytes 772
  4.3 32.7 %collective-permute-start.1 = (f32[4,16,1500]{2,1,0:T(8,128)S(1)}, f32[4,16,1500]{2,1,0:T(8,128)}, u32[]{:S(2)}, u32[]{:S(2)}) collective-permute-start(f32[4,16,1500]{2,1,0:T(8,128)S(1)} %select_multiply_fusion), channel_id=1, source_target_pairs={{2,0},{4,2},{6,4},{8,6},{10,8},{12,10},{14,12},{16,14},{18,16},{20... | collective-permute-start | bytes 1152008 | tf_op jit(solution)/shard_map/ppermute | solution.py:17
  9.0 28.0 %collective-permute-start = (f32[4,16,1500]{2,1,0:T(8,128)}, f32[4,16,1500]{2,1,0:T(8,128)}, u32[]{:S(2)}, u32[]{:S(2)}) collective-permute-start(f32[4,16,1500]{2,1,0:T(8,128)} %select_multiply_fusion.1), channel_id=1, source_target_pairs={{0,2},{2,4},{4,6},{6,8},{8,10},{10,12},{12,14},{14,16},{16,18},{18... | collective-permute-start | bytes 1152008 | tf_op jit(solution)/shard_map/ppermute | solution.py:17
  13.6 20.1 %collective-permute-start.3 = (f32[4,16]{1,0:T(4,128)S(1)}, f32[4,16]{1,0:T(4,128)S(1)}, u32[]{:S(2)}, u32[]{:S(2)}) collective-permute-start(f32[4,16]{1,0:T(4,128)S(1)} %select_multiply_fusion.2), channel_id=1, source_target_pairs={{2,0},{4,2},{6,4},{8,6},{10,8},{12,10},{14,12},{16,14},{18,16},{20... | collective-permute-start | bytes 776 | tf_op jit(solution)/shard_map/ppermute | solution.py:17
  16.1 17.6 %collective-permute-start.2 = (f32[4,16]{1,0:T(4,128)S(1)}, f32[4,16]{1,0:T(4,128)S(1)}, u32[]{:S(2)}, u32[]{:S(2)}) collective-permute-start(f32[4,16]{1,0:T(4,128)S(1)} %select_multiply_fusion.3), channel_id=1, source_target_pairs={{0,2},{2,4},{4,6},{6,8},{8,10},{10,12},{12,14},{14,16},{16,18},{18... | collective-permute-start | bytes 776 | tf_op jit(solution)/shard_map/ppermute | solution.py:17
  26.8 6.0 %copy-start.3 = (s32[4,24]{1,0:T(4,128)S(1)}, s32[4,24]{1,0:T(4,128)}, u32[]{:S(2)}) copy-start(s32[4,24]{1,0:T(4,128)} %param.13) | copy-start | bytes 1156
  54.5 1.3 %copy-start = (f32[144,2001]{1,0:T(8,128)S(1)}, f32[144,2001]{1,0:T(8,128)}, u32[]{:S(2)}) copy-start(f32[144,2001]{1,0:T(8,128)} %get-tuple-element.24) | copy-start | bytes 3457732
where the time goes:
time: 58.2 us; the launch traced here: 57.5 us
  other arithmetic  16 us (27%)
  starting transfers between devices  12.9 us (22%)
  blocking collectives  10.2 us (18%)
  matrix products  9.53 us (16%)
  local copies, waits for them, and re-layouts  8.62 us (15%)
    ppermute x4, starting transfers between devices, passed_along(): return lax.ppermute(array, axis, pairs)  12.9 us
    all_gather x1, blocking collectives, on_device(): lax.all_gather(local_spec, 'grp', axis=0, tiled=True)  6.97 us
    cos x1, other arithmetic, lag_basis(): return jnp.concatenate([jnp.cos(angles), -jnp.sin(angles)], axis=0)  6.02 us
    dot_general x2, matrix products, whitened(): jnp.dot(flat_traces, fourier_table(samples), precision=lax.Precision.HIGH...  4.67 us
    dot_general x1, matrix products, stacked(): jnp.einsum('iqf,jcqf->ijcf', left_both, right_both, preferred_element_typ...  3.88 us
    cos x1, other arithmetic, fourier_table(): return jnp.concatenate([jnp.cos(angles), -jnp.sin(angles)], axis=1)  3.66 us
    all_gather x1, blocking collectives, on_device(): lax.all_gather(local_mask, 'grp', axis=0, tiled=True)  3.19 us
    another operation x1, local copies, waits for them, and re-layouts, stacked(): jnp.stack([jnp.concatenate([right_real, right_imag], axis=1), jnp.concate...  2.01 us
  transfers between devices with their start and end apart: 4, of which 0 were waited for; matrix products, arithmetic and copies ran while one was open for 29% of the time, Pallas kernels for 0%

commit v1 on v0

v1 whole, which is shorter than its diff:
```python
import numpy as np
import ml_dtypes

import jax
import jax.numpy as jnp
from jax import lax
from jax.experimental import pallas as pl
from jax.experimental.pallas import tpu as pltpu
from jax.sharding import PartitionSpec as P

NBIN = 144
MAXLAG = 1000
LAGS = 2001
LANE = 128
TAIL = NBIN - LANE
HALF = 64
VALID = 16
WIDE = 3 * LANE
F32 = jnp.float32
BF16 = jnp.bfloat16


def split(table):
    high = table.astype(ml_dtypes.bfloat16)
    low = (table - high.astype(np.float64)).astype(ml_dtypes.bfloat16)
    return high, low


def in_lanes(real, imag):
    out = np.zeros((real.shape[0], WIDE))
    out[:, :LANE] = real[:, :LANE]
    out[:, LANE : 2 * LANE] = imag[:, :LANE]
    out[:, 2 * LANE : 2 * LANE + TAIL] = real[:, LANE:]
    out[:, 2 * LANE + HALF : 2 * LANE + HALF + TAIL] = imag[:, LANE:]
    return out


def fourier_table(samples):
    number = np.arange(samples)
    bins = np.arange(1, NBIN + 1)
    angle = np.mod(number[:, None] * bins[None, :], 2 * samples) * (np.pi / samples)
    taper = (0.5 - 0.5 * np.cos(number * (2.0 * np.pi / samples)))[:, None]
    table = in_lanes(taper * np.cos(angle), -taper * np.sin(angle))
    return split(np.pad(table, ((0, -samples % (2 * LANE)), (0, 0))))


def lag_table(samples):
    lags = np.arange(LAGS) - MAXLAG
    bins = np.arange(1, NBIN + 1)
    angle = np.mod(lags[:, None] * bins[None, :], 2 * samples) * (np.pi / samples)
    scale = 1.0 / np.sqrt(NBIN)
    high, low = split(in_lanes(scale * np.cos(angle), -scale * np.sin(angle)))
    return np.concatenate([high.T, low.T], axis=0)


def iota(shape, dim):
    return lax.broadcasted_iota(jnp.int32, shape, dim)


def spectra_kernel(
    per, seg, samples, rows_ref, count_ref, valid_ref, traces_hbm, high_hbm, low_hbm,
    own_ref, near_ref, far_ref, traces, high, low, sems,
):
    lines = per * seg
    step = 2 * LANE
    cuts = range(0, samples, step)
    copies = []
    first = pltpu.make_async_copy(traces_hbm, traces, sems.at[0])
    first.start()
    for i, at in enumerate(cuts):
        here = pl.ds(at, step)
        a = pltpu.make_async_copy(high_hbm.at[here], high.at[here], sems.at[1 + 2 * i])
        b = pltpu.make_async_copy(low_hbm.at[here], low.at[here], sems.at[2 + 2 * i])
        a.start()
        b.start()
        copies.append((a, b))

    odd = lax.rem(lax.axis_index("tile"), 2)
    col = iota((2 * LANE, 2 * LANE), 0)
    row = iota((2 * LANE, 2 * LANE), 1)

    def bin_of(lane):
        tail = lax.rem(lane, HALF)
        known = (lane < LANE) | (tail < TAIL)
        return known, jnp.where(lane < LANE, lane, LANE + tail)

    known_in, bin_in = bin_of(col)
    known_out, bin_out = bin_of(row)
    near_bins = jnp.abs(bin_in - bin_out) <= 4
    window = jnp.where(known_in & known_out, jnp.where(near_bins, 17.0, 1.0), 0.0).astype(BF16)

    target = iota((lines, lines), 0)
    source = iota((lines, lines), 1)
    slot = lax.rem(target, per)
    part = lax.div(target, per)

    def choice(station):
        return jnp.where(source == station * seg + part, 1.0, 0.0).astype(BF16)

    def listed(direction):
        station = jnp.full((lines, lines), -seg, jnp.int32)
        for j in range(per):
            live = j < count_ref[0, direction]
            pick = jnp.where(live, rows_ref[0, direction, j], -seg)
            station = jnp.where(slot == j, pick, station)
        return choice(station)

    picks = jnp.concatenate([choice(slot), listed(odd), listed(1 - odd)], axis=0)

    numbers = valid_ref[...].astype(F32)
    spread = jnp.concatenate(
        [jnp.broadcast_to(numbers[s : s + 1], (seg, seg)) for s in range(per)], axis=0
    )
    here = lax.rem(iota((lines, seg), 0), seg) == iota((lines, seg), 1)
    usable = jnp.sum(jnp.where(here, spread, 0.0), axis=1, keepdims=True)

    first.wait()
    total = jnp.zeros((lines, WIDE), F32)
    for at, (a, b) in zip(cuts, copies):
        x = traces[:, at : min(at + step, samples)]
        if at + step > samples:
            x = jnp.concatenate([x, jnp.zeros((lines, at + step - samples), F32)], axis=1)
        x_high = x.astype(BF16)
        x_low = (x - x_high.astype(F32)).astype(BF16)
        both = jnp.concatenate([x_high, x_low], axis=0)
        a.wait()
        wide = jnp.dot(both, high[at : at + step, :], preferred_element_type=F32)
        total = total + wide[:lines] + wide[lines:]
        b.wait()
        total = total + jnp.dot(x_high, low[at : at + step, :], preferred_element_type=F32)

    real, imag, tail = total[:, :LANE], total[:, LANE : 2 * LANE], total[:, 2 * LANE :]
    power = jnp.concatenate([real * real + imag * imag, tail * tail], axis=1)
    p_high = power.astype(BF16)
    p_low = (power - p_high.astype(F32)).astype(BF16)
    level = jnp.dot(p_high, window, preferred_element_type=F32)
    level = level + jnp.dot(p_low, window, preferred_element_type=F32)
    factor = usable / jnp.sqrt(level * (1.0 / (2 * NBIN)) + 1e-06)
    tail = tail * factor[:, LANE:]
    tail = jnp.where(iota((lines, LANE), 1) == VALID, usable, tail)
    white = jnp.concatenate([real * factor[:, :LANE], imag * factor[:, :LANE], tail], axis=1)
    chosen = jnp.dot(picks, white.astype(BF16), preferred_element_type=F32).astype(BF16)
    own_ref[...] = chosen[:lines]
    near_ref[...] = chosen[lines : 2 * lines]
    far_ref[...] = chosen[2 * lines :]


def lags_kernel(per, seg, grps, tiles, *refs):
    mask_ref, table_ref, own_ref = refs[:3]
    own_cols = [own_ref, *refs[3 : 2 + grps]]
    near_cols = refs[2 + grps : 2 + 2 * grps]
    far_cols = refs[2 + 2 * grps : 2 + 3 * grps]
    out_ref, spread, cross, result, sems = refs[2 + 3 * grps :]
    lines = per * seg
    columns = 3 * grps * per
    tile = lax.axis_index("tile")
    grp = lax.axis_index("grp")
    odd = lax.rem(tile, 2)
    inside = jnp.where(odd == 1, tile < tiles - 1, tile > 0)

    target = iota((per * lines, lines), 0)
    source = iota((per * lines, lines), 1)
    station = lax.div(target, lines)
    part = lax.div(lax.rem(target, lines), per)
    pick = jnp.where(source == part * per + station, 1.0, 0.0).astype(BF16)
    spread[...] = jnp.dot(pick, own_ref[...], preferred_element_type=F32)

    def stacked(ref):
        sums = [[None] * 4 for _ in range(per)]

        def add(s, i, value):
            sums[s][i] = value if sums[s][i] is None else sums[s][i] + value

        for at in range(0, lines, 16):
            both = ref[at : at + 16, :].astype(F32)
            for half in range(2):
                one = both[8 * half : 8 * half + 8]
                c_re, c_im, c_tail = one[:, :LANE], one[:, LANE : 2 * LANE], one[:, 2 * LANE :]
                c_turn = pltpu.roll(c_tail, HALF, 1)
                for s in range(per):
                    first = s * lines + at + 8 * half
                    left = spread[first : first + 8, :]
                    l_re, l_im, l_tail = left[:, :LANE], left[:, LANE : 2 * LANE], left[:, 2 * LANE :]
                    add(s, 0, l_re * c_re + l_im * c_im)
                    add(s, 1, l_im * c_re - l_re * c_im)
                    add(s, 2, l_tail * c_tail)
                    add(s, 3, l_tail * c_turn)
        low_lanes = iota((8, LANE), 1) < HALF
        out = []
        for s in range(per):
            straight, turned = sums[s][2], sums[s][3]
            straight = straight + pltpu.roll(straight, HALF, 1)
            turned = turned - pltpu.roll(turned, HALF, 1)
            all_lanes = [sums[s][0], sums[s][1], jnp.where(low_lanes, straight, turned)]
            out.append([v + pltpu.roll(v, 4, 0) for v in all_lanes])
        return out

    def by_place(pieces):
        places = []
        for g in range(grps):
            value = pieces[0]
            for d in range(1, grps):
                here = lax.rem(grp + (grps - d), grps) == g
                value = [[jnp.where(here, p, v) for p, v in zip(ps, vs)] for ps, vs in zip(pieces[d], value)]
            places.append(value)
        return places

    def of(cols):
        return by_place([stacked(c) for c in cols])

    own, near, far = of(own_cols), of(near_cols), of(far_cols)
    upper = iota((8, LANE), 0) < 4
    for s in range(per):
        slots = []
        for g in range(grps):
            n = near[g][s]
            f = [jnp.where(inside, v, 0.0) for v in far[g][s]]
            below = [jnp.where(odd == 1, a, b) for a, b in zip(n, f)]
            above = [jnp.where(odd == 1, b, a) for a, b in zip(n, f)]
            slots += [own[g][s], below, above]
        for i in range(0, len(slots), 2):
            rows = [jnp.where(upper, a, b) for a, b in zip(slots[i], slots[i + 1])]
            count = jnp.maximum(rows[2][:, VALID : VALID + 1], 1.0)
            at = s * columns + 4 * i
            for j in range(3):
                cross[at : at + 8, j * LANE : (j + 1) * LANE] = rows[j] / count

    masks = mask_ref[...].astype(F32)
    spread_mask = jnp.concatenate(
        [jnp.broadcast_to(masks[s : s + 1], (columns, columns)) for s in range(per)], axis=0
    )
    here = lax.rem(iota((per * columns, columns), 0), columns) == iota((per * columns, columns), 1)
    keep = jnp.sum(jnp.where(here, spread_mask, 0.0), axis=1, keepdims=True)
    left = (cross[...] * keep).astype(BF16)
    left = jnp.concatenate([left, left], axis=1)
    step = 4 * LANE
    for lo in range(0, LAGS, step):
        hi = min(lo + step, LAGS)
        series = jnp.dot(left, table_ref[:, lo:hi], preferred_element_type=F32).astype(BF16)
        for s in range(per):
            result[s, :, lo:hi] = series[s * columns : (s + 1) * columns]
    copy = pltpu.make_async_copy(result, out_ref, sems.at[0])
    copy.start()
    copy.wait()


def solution(mesh):
    tiles, grps = mesh.shape["tile"], mesh.shape["grp"]
    axes = ("tile", "grp")
    vmem = pl.BlockSpec(memory_space=pltpu.VMEM)
    smem = pl.BlockSpec(memory_space=pltpu.SMEM)
    hbm = pl.BlockSpec(memory_space=pl.ANY)

    def exchange(array, way, by):
        pairs = []
        for t in range(tiles):
            to = (t, t ^ 1, ((t + 1) ^ 1) - 1)[way]
            for g in range(grps):
                if 0 <= to < tiles:
                    goal = to * grps + (g + by) % grps
                else:
                    goal = t * grps + (g + max(by, 1)) % grps
                pairs.append((t * grps + g, goal))
        return lax.ppermute(array, axes, pairs)

    def on_device(traces, validity, boundary_rows, boundary_count, pair_mask):
        per, seg, samples = traces.shape
        lines = per * seg
        columns = pair_mask.shape[1]
        high, low = fourier_table(samples)
        table = lag_table(samples)
        payload = pltpu.VMEM((lines, WIDE), BF16)
        cuts = pl.cdiv(samples, 2 * LANE)
        own, near, far = pl.pallas_call(
            lambda *refs: spectra_kernel(per, seg, samples, *refs),
            out_shape=(payload, payload, payload),
            in_specs=[smem, smem, vmem, hbm, hbm, hbm],
            out_specs=(vmem, vmem, vmem),
            scratch_shapes=[
                pltpu.VMEM((lines, samples), F32),
                pltpu.VMEM(high.shape, BF16),
                pltpu.VMEM(low.shape, BF16),
                pltpu.SemaphoreType.DMA((1 + 2 * cuts,)),
            ],
            compiler_params=pltpu.CompilerParams(vmem_limit_bytes=32 << 20),
            name="spectra",
        )(boundary_rows, boundary_count, validity, traces.reshape(lines, samples), jnp.asarray(high), jnp.asarray(low))
        own_cols = [exchange(own, 0, d) for d in range(1, grps)]
        near_cols = [exchange(near, 1, d) for d in range(grps)]
        far_cols = [exchange(far, 2, d) for d in range(grps)]
        inputs = [jnp.asarray(table), own, *own_cols, *near_cols, *far_cols]
        inputs = [pltpu.with_memory_space_constraint(x, pltpu.VMEM) for x in inputs]
        return pl.pallas_call(
            lambda *refs: lags_kernel(per, seg, grps, tiles, *refs),
            out_shape=jax.ShapeDtypeStruct((per, columns, LAGS), BF16),
            in_specs=[vmem] * (1 + len(inputs)),
            out_specs=hbm,
            scratch_shapes=[
                pltpu.VMEM((per * lines, WIDE), F32),
                pltpu.VMEM((per * columns, WIDE), F32),
                pltpu.VMEM((per, columns, LAGS), BF16),
                pltpu.SemaphoreType.DMA((1,)),
            ],
            compiler_params=pltpu.CompilerParams(vmem_limit_bytes=48 << 20),
            name="lags",
        )(pair_mask, *inputs)

    return jax.shard_map(
        on_device,
        mesh=mesh,
        in_specs=(P(axes, None, None), P(axes, None), P(axes, None, None), P(axes, None), P(axes, None)),
        out_specs=P(axes, None, None),
        check_vma=False,
    )
```

time: 58.2 us -> 25.4 us (0.44)
  other arithmetic: 16 us -> 0 us
  blocking collectives: 10.2 us -> 0 us
  matrix products: 9.53 us -> 0 us
  Pallas kernels: 0 us -> 8.27 us
  starting transfers between devices: 12.9 us -> 5.98 us
  waiting for transfers between devices: 0.01 us -> 3.42 us
  local copies, waits for them, and re-layouts: 8.62 us -> 7.44 us
    all_gather x2 -> x0, blocking collectives: 10.2 us -> none  [the longest x1 6.97 us: on_device(): lax.all_gather(local_spec, 'grp', axis=0, tiled=True)]
    cos x2 -> x0, other arithmetic: 9.68 us -> none  [the longest x1 6.02 us: lag_basis(): return jnp.concatenate([jnp.cos(angles), -jnp.sin(angles)], axis=0)]
    dot_general x6 -> x0, matrix products: 9.53 us -> none  [the longest x2 4.67 us: whitened(): jnp.dot(flat_traces, fourier_table(samples), precision=lax.Precision.HIGH...]
    pallas_call x0 -> x2, Pallas kernels: none -> 8.27 us  [the longest x1 6.35 us: on_device(): pl.pallas_call(lambda *refs: spectra_kernel(per, seg, samples, *refs), ou...]
    ppermute x4 -> x5, starting transfers between devices: 12.9 us -> 5.98 us  [exchange(): return lax.ppermute(array, axes, pairs)]
    unnamed x9 -> x16, local copies, waits for them, and re-layouts: 0.63 us -> 7.44 us
    ppermute x4 -> x5, waiting for transfers between devices: 0.01 us -> 3.42 us  [exchange(): return lax.ppermute(array, axes, pairs)]
    gather x4 -> x0, local copies, waits for them, and re-layouts: 3.26 us -> none  [the longest x1 1.57 us: on_device(): jnp.take(traces, picks_down, axis=0) * live_down[:, None, None]]
  transfers between devices with their start and end apart: 4 -> 5, of which waited for: 0 -> 2; matrix products, arithmetic and copies ran while one was open for 29% -> 0% of each run, Pallas kernels for 0% -> 0%
where the time goes in v1:
time: 25.4 us; the launch traced here: 25.1 us
  Pallas kernels  8.27 us (33%)
  local copies, waits for them, and re-layouts  7.44 us (29%)
  starting transfers between devices  5.98 us (24%)
  waiting for transfers between devices  3.42 us (13%)
    unnamed x16, local copies, waits for them, and re-layouts  7.44 us
    pallas_call x1, Pallas kernels, on_device(): pl.pallas_call(lambda *refs: spectra_kernel(per, seg, samples, *refs), ou...  6.35 us
    ppermute x5, starting transfers between devices, exchange(): return lax.ppermute(array, axes, pairs)  5.98 us
    ppermute x5, waiting for transfers between devices, exchange(): return lax.ppermute(array, axes, pairs)  3.42 us
    pallas_call x1, Pallas kernels, on_device(): pl.pallas_call(lambda *refs: lags_kernel(per, seg, grps, tiles, *refs), o...  1.92 us
  transfers between devices with their start and end apart: 5, of which 2 were waited for; matrix products, arithmetic and copies ran while one was open for 0% of the time, Pallas kernels for 0%

profile of v1, /device:TPU:3, one launch (start us, length us, event | category | flops | bytes accessed | tf_op | source)
XLA Modules:
  0.0 25.1 jit_solution(13295126769041190585)
XLA Ops:
  0.0 0.0 copy-start.1
  0.0 1.3 %copy-done.1 = bf16[1536,384]{1,0:T(8,128)(2,1)S(1)} copy-done((bf16[1536,384]{1,0:T(8,128)(2,1)S(1)}, bf16[1536,384]{1,0:T(8,128)(2,1)}, u32[]{:S(2)}) %copy-start.1) | copy-done | bytes 1179672
  1.3 0.0 copy-start.2
  1.3 1.3 %copy-done.2 = bf16[1536,384]{1,0:T(8,128)(2,1)S(1)} copy-done((bf16[1536,384]{1,0:T(8,128)(2,1)S(1)}, bf16[1536,384]{1,0:T(8,128)(2,1)}, u32[]{:S(2)}) %copy-start.2) | copy-done | bytes 1179672
  2.5 0.0 copy-start.3
  2.5 1.0 %copy-done.3 = f32[4,16,1500]{2,1,0:T(8,128)S(1)} copy-done((f32[4,16,1500]{2,1,0:T(8,128)S(1)}, f32[4,16,1500]{2,1,0:T(8,128)}, u32[]{:S(2)}) %copy-start.3) | copy-done | bytes 384024
  3.5 0.0 copy-start.5
  3.5 0.7 %copy-done.5 = s32[4,16]{1,0:T(4,128)S(1)} copy-done((s32[4,16]{1,0:T(4,128)S(1)}, s32[4,16]{1,0:T(4,128)}, u32[]{:S(2)}) %copy-start.5) | copy-done | bytes 280
  4.2 0.7 %copy-done.6 = s32[1,2,4]{2,1,0:T(2,128)S(1)} copy-done((s32[1,2,4]{2,1,0:T(2,128)S(1)}, s32[1,2,4]{2,1,0:T(2,128)}, u32[]{:S(2)}) %copy-start.6) | copy-done | bytes 56
  4.9 0.7 %copy-done.7 = s32[1,2]{1,0:T(1,128)S(1)} copy-done((s32[1,2]{1,0:T(1,128)S(1)}, s32[1,2]{1,0:T(1,128)}, u32[]{:S(2)}) %copy-start.7) | copy-done | bytes 32
  5.6 6.4 %spectra.1 = (bf16[64,384]{1,0:T(8,128)(2,1)S(1)}, bf16[64,384]{1,0:T(8,128)(2,1)S(1)}, bf16[64,384]{1,0:T(8,128)(2,1)S(1)}) custom-call(s32[1,2,4]{2,1,0:T(2,128)S(1)} %copy-done.6, s32[1,2]{1,0:T(1,128)S(1)} %copy-done.7, s32[4,16]{1,0:T(4,128)S(1)} %copy-done.5, f32[64,1500]{1,0:T(8,128)S(1)} %bitcast.1, bf16[1536,384]{1,0:T(8,128)(2,1)S(1)} %copy-done.2, ...), custom_call_target="tpu_custom_call" | custom-call | tf_op jit(solution)/shard_map/spectra/pallas_call | solution.py:274
  11.9 1.3 %collective-permute-start = (bf16[64,384]{1,0:T(8,128)(2,1)S(1)}, bf16[64,384]{1,0:T(8,128)(2,1)S(1)}, u32[]{:S(2)}, u32[]{:S(2)}) collective-permute-start(bf16[64,384]{1,0:T(8,128)(2,1)S(1)} %get-tuple-element.8.refs_2_), channel_id=1, source_target_pairs={{0,1},{1,0},{2,3},{3,2},{4,5},{5,4},{6,7},{7,6},{8,9},{9,8},{10,11... | collective-permute-start | bytes 147464 | tf_op jit(solution)/shard_map/ppermute | solution.py:264
  13.2 1.1 %collective-permute-start.2 = (bf16[64,384]{1,0:T(8,128)(2,1)S(1)}, bf16[64,384]{1,0:T(8,128)(2,1)S(1)}, u32[]{:S(2)}, u32[]{:S(2)}) collective-permute-start(bf16[64,384]{1,0:T(8,128)(2,1)S(1)} %get-tuple-element.9), channel_id=1, source_target_pairs={{0,3},{1,2},{2,1},{3,0},{4,7},{5,6},{6,5},{7,4},{8,11},{9,10},{10,... | collective-permute-start | bytes 147464 | tf_op jit(solution)/shard_map/ppermute | solution.py:264
  14.3 0.0 collective-permute-start.1
  14.3 2.6 %collective-permute-start.4 = (bf16[64,384]{1,0:T(8,128)(2,1)S(1)}, bf16[64,384]{1,0:T(8,128)(2,1)S(1)}, u32[]{:S(2)}, u32[]{:S(2)}) collective-permute-start(bf16[64,384]{1,0:T(8,128)(2,1)S(1)} %get-tuple-element.10), channel_id=1, source_target_pairs={{0,1},{1,0},{2,5},{3,4},{4,3},{5,2},{6,9},{7,8},{8,7},{9,6},{10,13... | collective-permute-start | bytes 147464 | tf_op jit(solution)/shard_map/ppermute | solution.py:264
  16.9 1.0 %collective-permute-start.3 = (bf16[64,384]{1,0:T(8,128)(2,1)S(1)}, bf16[64,384]{1,0:T(8,128)(2,1)S(1)}, u32[]{:S(2)}, u32[]{:S(2)}) collective-permute-start(bf16[64,384]{1,0:T(8,128)(2,1)S(1)} %get-tuple-element.10), channel_id=1, source_target_pairs={{0,1},{1,0},{2,4},{3,5},{4,2},{5,3},{6,8},{7,9},{8,6},{9,7},{10,12... | collective-permute-start | bytes 147464 | tf_op jit(solution)/shard_map/ppermute | solution.py:264
  17.9 0.0 collective-permute-done.refs_3_
  17.9 0.0 collective-permute-done.2.refs_5_
  17.9 0.0 collective-permute-done.1.refs_4_
  17.9 1.7 %collective-permute-done.4.refs_7_ = bf16[64,384]{1,0:T(8,128)(2,1)S(1)} collective-permute-done((bf16[64,384]{1,0:T(8,128)(2,1)S(1)}, bf16[64,384]{1,0:T(8,128)(2,1)S(1)}, u32[]{:S(2)}, u32[]{:S(2)}) %collective-permute-start.4) | collective-permute-done | bytes 49184 | tf_op jit(solution)/shard_map/ppermute | solution.py:264
  19.6 1.7 %collective-permute-done.3.refs_6_ = bf16[64,384]{1,0:T(8,128)(2,1)S(1)} collective-permute-done((bf16[64,384]{1,0:T(8,128)(2,1)S(1)}, bf16[64,384]{1,0:T(8,128)(2,1)S(1)}, u32[]{:S(2)}, u32[]{:S(2)}) %collective-permute-start.3) | collective-permute-done | bytes 49184 | tf_op jit(solution)/shard_map/ppermute | solution.py:264
  21.3 0.0 copy-done.4
  21.3 1.9 %copy-done = bf16[768,2001]{1,0:T(8,128)(2,1)S(1)} copy-done((bf16[768,2001]{1,0:T(8,128)(2,1)S(1)}, bf16[768,2001]{1,0:T(8,128)(2,1)}, u32[]{:S(2)}) %copy-start) | copy-done | bytes 3073560
  23.2 1.9 %lags.1 = bf16[4,24,2001]{2,1,0:T(8,128)(2,1)} custom-call(s32[4,24]{1,0:T(4,128)S(1)} %copy-done.4, bf16[768,2001]{1,0:T(8,128)(2,1)S(1)} %copy-done, bf16[64,384]{1,0:T(8,128)(2,1)S(1)} %get-tuple-element.8.refs_2_, bf16[64,384]{1,0:T(8,128)(2,1)S(1)} %collective-permute-done.refs_3_, bf16[64,384]{1,0:T(8,128)(2,1)S(1)} %collective-permute-done.1.refs_4_, ...), custom_call_target="tpu_custom_call" | custom-call | tf_op jit(solution)/shard_map/lags/pallas_call | solution.py:293
  (4 shorter events, 0.0 us)
Async XLA Ops:
  0.0 1.3 %copy-start.1 = (bf16[1536,384]{1,0:T(8,128)(2,1)S(1)}, bf16[1536,384]{1,0:T(8,128)(2,1)}, u32[]{:S(2)}) copy-start(bf16[1536,384]{1,0:T(8,128)(2,1)} %constant.7.clone.refs_5_) | copy-start | bytes 3538948
  1.3 1.3 %copy-start.2 = (bf16[1536,384]{1,0:T(8,128)(2,1)S(1)}, bf16[1536,384]{1,0:T(8,128)(2,1)}, u32[]{:S(2)}) copy-start(bf16[1536,384]{1,0:T(8,128)(2,1)} %constant.6.clone.refs_4_) | copy-start | bytes 3538948
  2.5 1.0 %copy-start.3 = (f32[4,16,1500]{2,1,0:T(8,128)S(1)}, f32[4,16,1500]{2,1,0:T(8,128)}, u32[]{:S(2)}) copy-start(f32[4,16,1500]{2,1,0:T(8,128)} %param.8) | copy-start | bytes 1152004
  3.5 0.7 %copy-start.5 = (s32[4,16]{1,0:T(4,128)S(1)}, s32[4,16]{1,0:T(4,128)}, u32[]{:S(2)}) copy-start(s32[4,16]{1,0:T(4,128)} %refs_2_.1) | copy-start | bytes 772
  4.2 0.7 %copy-start.6 = (s32[1,2,4]{2,1,0:T(2,128)S(1)}, s32[1,2,4]{2,1,0:T(2,128)}, u32[]{:S(2)}) copy-start(s32[1,2,4]{2,1,0:T(2,128)} %refs_0_.2) | copy-start | bytes 100
  4.9 0.7 %copy-start.7 = (s32[1,2]{1,0:T(1,128)S(1)}, s32[1,2]{1,0:T(1,128)}, u32[]{:S(2)}) copy-start(s32[1,2]{1,0:T(1,128)} %refs_1_.2) | copy-start | bytes 28
  5.6 15.8 %copy-start.4 = (s32[4,24]{1,0:T(4,128)S(1)}, s32[4,24]{1,0:T(4,128)}, u32[]{:S(2)}) copy-start(s32[4,24]{1,0:T(4,128)} %refs_0_.3) | copy-start | bytes 1156
  11.9 6.0 %collective-permute-start = (bf16[64,384]{1,0:T(8,128)(2,1)S(1)}, bf16[64,384]{1,0:T(8,128)(2,1)S(1)}, u32[]{:S(2)}, u32[]{:S(2)}) collective-permute-start(bf16[64,384]{1,0:T(8,128)(2,1)S(1)} %get-tuple-element.8.refs_2_), channel_id=1, source_target_pairs={{0,1},{1,0},{2,3},{3,2},{4,5},{5,4},{6,7},{7,6},{8,9},{9,8},{10,11... | collective-permute-start | bytes 147464 | tf_op jit(solution)/shard_map/ppermute | solution.py:264
  13.2 4.7 %collective-permute-start.2 = (bf16[64,384]{1,0:T(8,128)(2,1)S(1)}, bf16[64,384]{1,0:T(8,128)(2,1)S(1)}, u32[]{:S(2)}, u32[]{:S(2)}) collective-permute-start(bf16[64,384]{1,0:T(8,128)(2,1)S(1)} %get-tuple-element.9), channel_id=1, source_target_pairs={{0,3},{1,2},{2,1},{3,0},{4,7},{5,6},{6,5},{7,4},{8,11},{9,10},{10,... | collective-permute-start | bytes 147464 | tf_op jit(solution)/shard_map/ppermute | solution.py:264
  14.3 3.6 %collective-permute-start.1 = (bf16[64,384]{1,0:T(8,128)(2,1)S(1)}, bf16[64,384]{1,0:T(8,128)(2,1)S(1)}, u32[]{:S(2)}, u32[]{:S(2)}) collective-permute-start(bf16[64,384]{1,0:T(8,128)(2,1)S(1)} %get-tuple-element.9), channel_id=1, source_target_pairs={{0,2},{1,3},{2,0},{3,1},{4,6},{5,7},{6,4},{7,5},{8,10},{9,11},{10,... | collective-permute-start | bytes 147464 | tf_op jit(solution)/shard_map/ppermute | solution.py:264
  14.3 5.3 %collective-permute-start.4 = (bf16[64,384]{1,0:T(8,128)(2,1)S(1)}, bf16[64,384]{1,0:T(8,128)(2,1)S(1)}, u32[]{:S(2)}, u32[]{:S(2)}) collective-permute-start(bf16[64,384]{1,0:T(8,128)(2,1)S(1)} %get-tuple-element.10), channel_id=1, source_target_pairs={{0,1},{1,0},{2,5},{3,4},{4,3},{5,2},{6,9},{7,8},{8,7},{9,6},{10,13... | collective-permute-start | bytes 147464 | tf_op jit(solution)/shard_map/ppermute | solution.py:264
  16.9 4.4 %collective-permute-start.3 = (bf16[64,384]{1,0:T(8,128)(2,1)S(1)}, bf16[64,384]{1,0:T(8,128)(2,1)S(1)}, u32[]{:S(2)}, u32[]{:S(2)}) collective-permute-start(bf16[64,384]{1,0:T(8,128)(2,1)S(1)} %get-tuple-element.10), channel_id=1, source_target_pairs={{0,1},{1,0},{2,4},{3,5},{4,2},{5,3},{6,8},{7,9},{8,6},{9,7},{10,12... | collective-permute-start | bytes 147464 | tf_op jit(solution)/shard_map/ppermute | solution.py:264
  21.3 1.9 %copy-start = (bf16[768,2001]{1,0:T(8,128)(2,1)S(1)}, bf16[768,2001]{1,0:T(8,128)(2,1)}, u32[]{:S(2)}) copy-start(bf16[768,2001]{1,0:T(8,128)(2,1)} %constant.8.clone.refs_1_) | copy-start | bytes 9220612

commit v2 on v1

--- a/solution.py
+++ b/solution.py
@@ -57,14 +57,35 @@
     return lax.broadcasted_iota(jnp.int32, shape, dim)
 
 
+def divided(value, by):
+    if by & (by - 1) == 0:
+        return value >> (by.bit_length() - 1), value & (by - 1)
+    return lax.div(value, by), lax.rem(value, by)
+
+
+def column_of(rows):
+    n, m = rows.shape
+    diagonal = iota((m, m), 0) == iota((m, m), 1)
+    return [
+        jnp.sum(jnp.where(diagonal, jnp.broadcast_to(rows[i : i + 1], (m, m)), 0.0), axis=1, keepdims=True)
+        for i in range(n)
+    ]
+
+
 def spectra_kernel(
-    per, seg, samples, rows_ref, count_ref, valid_ref, traces_hbm, high_hbm, low_hbm,
-    own_ref, near_ref, far_ref, traces, high, low, sems,
+    per, seg, samples, rows_hbm, count_hbm, valid_hbm, traces_hbm, high_hbm, low_hbm,
+    own_ref, near_ref, far_ref, rows_ref, count_ref, valid_ref, traces, high, low, sems, small_sems,
 ):
     lines = per * seg
     step = 2 * LANE
     cuts = range(0, samples, step)
     copies = []
+    small = [
+        pltpu.make_async_copy(src, dst, small_sems.at[i])
+        for i, (src, dst) in enumerate(((rows_hbm, rows_ref), (count_hbm, count_ref), (valid_hbm, valid_ref)))
+    ]
+    for copy in small:
+        copy.start()
     first = pltpu.make_async_copy(traces_hbm, traces, sems.at[0])
     first.start()
     for i, at in enumerate(cuts):
@@ -80,7 +101,7 @@
     row = iota((2 * LANE, 2 * LANE), 1)
 
     def bin_of(lane):
-        tail = lax.rem(lane, HALF)
+        tail = lane & (HALF - 1)
         known = (lane < LANE) | (tail < TAIL)
         return known, jnp.where(lane < LANE, lane, LANE + tail)
 
@@ -91,8 +112,9 @@
 
     target = iota((lines, lines), 0)
     source = iota((lines, lines), 1)
-    slot = lax.rem(target, per)
-    part = lax.div(target, per)
+    part, slot = divided(target, per)
+    for copy in small:
+        copy.wait()
 
     def choice(station):
         return jnp.where(source == station * seg + part, 1.0, 0.0).astype(BF16)
@@ -107,12 +129,7 @@
 
     picks = jnp.concatenate([choice(slot), listed(odd), listed(1 - odd)], axis=0)
 
-    numbers = valid_ref[...].astype(F32)
-    spread = jnp.concatenate(
-        [jnp.broadcast_to(numbers[s : s + 1], (seg, seg)) for s in range(per)], axis=0
-    )
-    here = lax.rem(iota((lines, seg), 0), seg) == iota((lines, seg), 1)
-    usable = jnp.sum(jnp.where(here, spread, 0.0), axis=1, keepdims=True)
+    usable = jnp.concatenate(column_of(valid_ref[...].astype(F32)), axis=0)
 
     first.wait()
     total = jnp.zeros((lines, WIDE), F32)
@@ -145,25 +162,33 @@
     far_ref[...] = chosen[2 * lines :]
 
 
+def ready_kernel(per, seg, mask_hbm, table_hbm, own_ref, mask_ref, table_ref, spread_ref, sems):
+    copies = [
+        pltpu.make_async_copy(table_hbm, table_ref, sems.at[0]),
+        pltpu.make_async_copy(mask_hbm, mask_ref, sems.at[1]),
+    ]
+    for copy in copies:
+        copy.start()
+    lines = per * seg
+    part, _ = divided(iota((lines, lines), 0), per)
+    source = iota((lines, lines), 1)
+    pick = [jnp.where(source == part * per + s, 1.0, 0.0).astype(BF16) for s in range(per)]
+    spread_ref[...] = jnp.dot(jnp.concatenate(pick, axis=0), own_ref[...], preferred_element_type=F32)
+    for copy in copies:
+        copy.wait()
+
+
 def lags_kernel(per, seg, grps, tiles, *refs):
-    mask_ref, table_ref, own_ref = refs[:3]
-    own_cols = [own_ref, *refs[3 : 2 + grps]]
-    near_cols = refs[2 + grps : 2 + 2 * grps]
-    far_cols = refs[2 + 2 * grps : 2 + 3 * grps]
-    out_ref, spread, cross, result, sems = refs[2 + 3 * grps :]
+    mask_ref, table_ref, spread = refs[:3]
+    refs = refs[3:]
+    own_cols, near_cols, far_cols = (refs[i * grps : (i + 1) * grps] for i in range(3))
+    out_ref, cross, result, sems = refs[3 * grps :]
     lines = per * seg
     columns = 3 * grps * per
     tile = lax.axis_index("tile")
     grp = lax.axis_index("grp")
     odd = lax.rem(tile, 2)
     inside = jnp.where(odd == 1, tile < tiles - 1, tile > 0)
-
-    target = iota((per * lines, lines), 0)
-    source = iota((per * lines, lines), 1)
-    station = lax.div(target, lines)
-    part = lax.div(lax.rem(target, lines), per)
-    pick = jnp.where(source == part * per + station, 1.0, 0.0).astype(BF16)
-    spread[...] = jnp.dot(pick, own_ref[...], preferred_element_type=F32)
 
     def stacked(ref):
         sums = [[None] * 4 for _ in range(per)]
@@ -225,12 +250,7 @@
             for j in range(3):
                 cross[at : at + 8, j * LANE : (j + 1) * LANE] = rows[j] / count
 
-    masks = mask_ref[...].astype(F32)
-    spread_mask = jnp.concatenate(
-        [jnp.broadcast_to(masks[s : s + 1], (columns, columns)) for s in range(per)], axis=0
-    )
-    here = lax.rem(iota((per * columns, columns), 0), columns) == iota((per * columns, columns), 1)
-    keep = jnp.sum(jnp.where(here, spread_mask, 0.0), axis=1, keepdims=True)
+    keep = jnp.concatenate(column_of(mask_ref[...].astype(F32)), axis=0)
     left = (cross[...] * keep).astype(BF16)
     left = jnp.concatenate([left, left], axis=1)
     step = 4 * LANE
@@ -248,8 +268,8 @@
     tiles, grps = mesh.shape["tile"], mesh.shape["grp"]
     axes = ("tile", "grp")
     vmem = pl.BlockSpec(memory_space=pltpu.VMEM)
-    smem = pl.BlockSpec(memory_space=pltpu.SMEM)
-    hbm = pl.BlockSpec(memory_space=pl.ANY)
+    hbm = pl.BlockSpec(memory_space=pltpu.HBM)
+    placed = pltpu.with_memory_space_constraint
 
     def exchange(array, way, by):
         pairs = []
@@ -267,43 +287,59 @@
         per, seg, samples = traces.shape
         lines = per * seg
         columns = pair_mask.shape[1]
-        high, low = fourier_table(samples)
-        table = lag_table(samples)
+        high, low = map(jnp.asarray, fourier_table(samples))
+        table = jnp.asarray(lag_table(samples))
         payload = pltpu.VMEM((lines, WIDE), BF16)
         cuts = pl.cdiv(samples, 2 * LANE)
+        inputs = [boundary_rows, boundary_count, validity, traces.reshape(lines, samples), high, low]
         own, near, far = pl.pallas_call(
             lambda *refs: spectra_kernel(per, seg, samples, *refs),
             out_shape=(payload, payload, payload),
-            in_specs=[smem, smem, vmem, hbm, hbm, hbm],
+            in_specs=[hbm] * len(inputs),
             out_specs=(vmem, vmem, vmem),
             scratch_shapes=[
+                pltpu.SMEM(boundary_rows.shape, jnp.int32),
+                pltpu.SMEM(boundary_count.shape, jnp.int32),
+                pltpu.VMEM(validity.shape, jnp.int32),
                 pltpu.VMEM((lines, samples), F32),
                 pltpu.VMEM(high.shape, BF16),
                 pltpu.VMEM(low.shape, BF16),
                 pltpu.SemaphoreType.DMA((1 + 2 * cuts,)),
+                pltpu.SemaphoreType.DMA((3,)),
             ],
             compiler_params=pltpu.CompilerParams(vmem_limit_bytes=32 << 20),
             name="spectra",
-        )(boundary_rows, boundary_count, validity, traces.reshape(lines, samples), jnp.asarray(high), jnp.asarray(low))
+        )(*[placed(x, pltpu.HBM) for x in inputs])
         own_cols = [exchange(own, 0, d) for d in range(1, grps)]
         near_cols = [exchange(near, 1, d) for d in range(grps)]
         far_cols = [exchange(far, 2, d) for d in range(grps)]
-        inputs = [jnp.asarray(table), own, *own_cols, *near_cols, *far_cols]
-        inputs = [pltpu.with_memory_space_constraint(x, pltpu.VMEM) for x in inputs]
+        mask, table, spread = pl.pallas_call(
+            lambda *refs: ready_kernel(per, seg, *refs),
+            out_shape=(
+                pltpu.VMEM(pair_mask.shape, jnp.int32),
+                pltpu.VMEM(table.shape, BF16),
+                pltpu.VMEM((per * lines, WIDE), F32),
+            ),
+            in_specs=[hbm, hbm, vmem],
+            out_specs=(vmem, vmem, vmem),
+            scratch_shapes=[pltpu.SemaphoreType.DMA((2,))],
+            compiler_params=pltpu.CompilerParams(vmem_limit_bytes=32 << 20),
+            name="ready",
+        )(placed(pair_mask, pltpu.HBM), placed(table, pltpu.HBM), placed(own, pltpu.VMEM))
+        inputs = [mask, table, spread, own, *own_cols, *near_cols, *far_cols]
         return pl.pallas_call(
             lambda *refs: lags_kernel(per, seg, grps, tiles, *refs),
             out_shape=jax.ShapeDtypeStruct((per, columns, LAGS), BF16),
-            in_specs=[vmem] * (1 + len(inputs)),
+            in_specs=[vmem] * len(inputs),
             out_specs=hbm,
             scratch_shapes=[
-                pltpu.VMEM((per * lines, WIDE), F32),
                 pltpu.VMEM((per * columns, WIDE), F32),
                 pltpu.VMEM((per, columns, LAGS), BF16),
                 pltpu.SemaphoreType.DMA((1,)),
             ],
-            compiler_params=pltpu.CompilerParams(vmem_limit_bytes=48 << 20),
+            compiler_params=pltpu.CompilerParams(vmem_limit_bytes=32 << 20),
             name="lags",
-        )(pair_mask, *inputs)
+        )(*[placed(x, pltpu.VMEM) for x in inputs])
 
     return jax.shard_map(
         on_device,

time: 25.4 us -> 15.4 us (0.61)
  the two profiles are of different devices: /device:TPU:3 before, /device:TPU:0 now
where the time goes in v2:
time: 15.4 us; the launch traced here: 15.2 us
  Pallas kernels  7.81 us (51%)
  starting transfers between devices  5.21 us (34%)
  waiting for transfers between devices  2.19 us (14%)
    ppermute x5, starting transfers between devices, exchange(): return lax.ppermute(array, axes, pairs)  5.21 us
    pallas_call x1, Pallas kernels, on_device(): pl.pallas_call(lambda *refs: spectra_kernel(per, seg, samples, *refs), ou...  4.04 us
    ppermute x5, waiting for transfers between devices, exchange(): return lax.ppermute(array, axes, pairs)  2.19 us
    pallas_call x1, Pallas kernels, on_device(): pl.pallas_call(lambda *refs: ready_kernel(per, seg, *refs), out_shape=(pl...  1.91 us
    pallas_call x1, Pallas kernels, on_device(): pl.pallas_call(lambda *refs: lags_kernel(per, seg, grps, tiles, *refs), o...  1.86 us
  transfers between devices with their start and end apart: 5, of which 3 were waited for; matrix products, arithmetic and copies ran while one was open for 0% of the time, Pallas kernels for 13%

profile of v2, /device:TPU:0, one launch (start us, length us, event | category | flops | bytes accessed | tf_op | source)
XLA Modules:
  0.0 15.2 jit_solution(3240383211772400088)
XLA Ops:
  0.0 4.0 %spectra.1 = (bf16[64,384]{1,0:T(8,128)(2,1)S(1)}, bf16[64,384]{1,0:T(8,128)(2,1)S(1)}, bf16[64,384]{1,0:T(8,128)(2,1)S(1)}) custom-call(s32[1,2,4]{2,1,0:T(2,128)} %refs_0_.2, s32[1,2]{1,0:T(1,128)} %refs_1_.2, s32[4,16]{1,0:T(4,128)} %refs_2_.1, f32[64,1500]{1,0:T(8,128)} %bitcast.1, bf16[1536,384]{1,0:T(8,128)(2,1)} %constant.6.clone.refs_4_, ...), custom_call_target="tpu_custom_call" | custom-call | tf_op jit(solution)/shard_map/spectra/pallas_call | solution.py:295
  4.0 2.5 %collective-permute-start.2 = (bf16[64,384]{1,0:T(8,128)(2,1)S(1)}, bf16[64,384]{1,0:T(8,128)(2,1)S(1)}, u32[]{:S(2)}, u32[]{:S(2)}) collective-permute-start(bf16[64,384]{1,0:T(8,128)(2,1)S(1)} %get-tuple-element.15), channel_id=1, source_target_pairs={{0,3},{1,2},{2,1},{3,0},{4,7},{5,6},{6,5},{7,4},{8,11},{9,10},{10,... | collective-permute-start | bytes 147464 | tf_op jit(solution)/shard_map/ppermute | solution.py:284
  6.5 0.7 %collective-permute-start.1 = (bf16[64,384]{1,0:T(8,128)(2,1)S(1)}, bf16[64,384]{1,0:T(8,128)(2,1)S(1)}, u32[]{:S(2)}, u32[]{:S(2)}) collective-permute-start(bf16[64,384]{1,0:T(8,128)(2,1)S(1)} %get-tuple-element.15), channel_id=1, source_target_pairs={{0,2},{1,3},{2,0},{3,1},{4,6},{5,7},{6,4},{7,5},{8,10},{9,11},{10,... | collective-permute-start | bytes 147464 | tf_op jit(solution)/shard_map/ppermute | solution.py:284
  7.2 0.0 collective-permute-start.4
  7.2 2.0 %collective-permute-start.3 = (bf16[64,384]{1,0:T(8,128)(2,1)S(1)}, bf16[64,384]{1,0:T(8,128)(2,1)S(1)}, u32[]{:S(2)}, u32[]{:S(2)}) collective-permute-start(bf16[64,384]{1,0:T(8,128)(2,1)S(1)} %get-tuple-element.16), channel_id=1, source_target_pairs={{0,1},{1,0},{2,4},{3,5},{4,2},{5,3},{6,8},{7,9},{8,6},{9,7},{10,12... | collective-permute-start | bytes 147464 | tf_op jit(solution)/shard_map/ppermute | solution.py:284
  9.2 0.0 collective-permute-start
  9.3 1.9 %ready.1 = (s32[4,24]{1,0:T(4,128)S(1)}, bf16[768,2001]{1,0:T(8,128)(2,1)S(1)}, f32[256,384]{1,0:T(8,128)S(1)}) custom-call(s32[4,24]{1,0:T(4,128)} %refs_0_.3, bf16[768,2001]{1,0:T(8,128)(2,1)} %constant.8.clone.refs_1_, bf16[64,384]{1,0:T(8,128)(2,1)S(1)} %get-tuple-element.11.refs_2_.refs_3_), custom_call_target="tpu_custom_call" | custom-call | tf_op jit(solution)/shard_map/ready/pallas_call | solution.py:316
  11.2 0.0 collective-permute-done.2.refs_6_
  11.2 0.0 collective-permute-done.1.refs_5_
  11.2 0.1 collective-permute-done.4.refs_8_
  11.3 1.5 %collective-permute-done.3.refs_7_ = bf16[64,384]{1,0:T(8,128)(2,1)S(1)} collective-permute-done((bf16[64,384]{1,0:T(8,128)(2,1)S(1)}, bf16[64,384]{1,0:T(8,128)(2,1)S(1)}, u32[]{:S(2)}, u32[]{:S(2)}) %collective-permute-start.3) | collective-permute-done | bytes 49184 | tf_op jit(solution)/shard_map/ppermute | solution.py:284
  12.8 0.6 %collective-permute-done.refs_4_ = bf16[64,384]{1,0:T(8,128)(2,1)S(1)} collective-permute-done((bf16[64,384]{1,0:T(8,128)(2,1)S(1)}, bf16[64,384]{1,0:T(8,128)(2,1)S(1)}, u32[]{:S(2)}, u32[]{:S(2)}) %collective-permute-start) | collective-permute-done | bytes 49184 | tf_op jit(solution)/shard_map/ppermute | solution.py:284
  13.4 1.9 %lags.1 = bf16[4,24,2001]{2,1,0:T(8,128)(2,1)} custom-call(s32[4,24]{1,0:T(4,128)S(1)} %get-tuple-element.12.refs_0_, bf16[768,2001]{1,0:T(8,128)(2,1)S(1)} %get-tuple-element.13.refs_1_, f32[256,384]{1,0:T(8,128)S(1)} %get-tuple-element.14.refs_2_, bf16[64,384]{1,0:T(8,128)(2,1)S(1)} %get-tuple-element.11.refs_2_.refs_3_, ...), custom_call_target="tpu_custom_call" | custom-call | tf_op jit(solution)/shard_map/lags/pallas_call | solution.py:330
Async XLA Ops:
  4.0 7.1 %collective-permute-start.2 = (bf16[64,384]{1,0:T(8,128)(2,1)S(1)}, bf16[64,384]{1,0:T(8,128)(2,1)S(1)}, u32[]{:S(2)}, u32[]{:S(2)}) collective-permute-start(bf16[64,384]{1,0:T(8,128)(2,1)S(1)} %get-tuple-element.15), channel_id=1, source_target_pairs={{0,3},{1,2},{2,1},{3,0},{4,7},{5,6},{6,5},{7,4},{8,11},{9,10},{10,... | collective-permute-start | bytes 147464 | tf_op jit(solution)/shard_map/ppermute | solution.py:284
  6.5 4.7 %collective-permute-start.1 = (bf16[64,384]{1,0:T(8,128)(2,1)S(1)}, bf16[64,384]{1,0:T(8,128)(2,1)S(1)}, u32[]{:S(2)}, u32[]{:S(2)}) collective-permute-start(bf16[64,384]{1,0:T(8,128)(2,1)S(1)} %get-tuple-element.15), channel_id=1, source_target_pairs={{0,2},{1,3},{2,0},{3,1},{4,6},{5,7},{6,4},{7,5},{8,10},{9,11},{10,... | collective-permute-start | bytes 147464 | tf_op jit(solution)/shard_map/ppermute | solution.py:284
  7.2 4.1 %collective-permute-start.4 = (bf16[64,384]{1,0:T(8,128)(2,1)S(1)}, bf16[64,384]{1,0:T(8,128)(2,1)S(1)}, u32[]{:S(2)}, u32[]{:S(2)}) collective-permute-start(bf16[64,384]{1,0:T(8,128)(2,1)S(1)} %get-tuple-element.16), channel_id=1, source_target_pairs={{0,1},{1,0},{2,5},{3,4},{4,3},{5,2},{6,9},{7,8},{8,7},{9,6},{10,13... | collective-permute-start | bytes 147464 | tf_op jit(solution)/shard_map/ppermute | solution.py:284
  7.2 5.6 %collective-permute-start.3 = (bf16[64,384]{1,0:T(8,128)(2,1)S(1)}, bf16[64,384]{1,0:T(8,128)(2,1)S(1)}, u32[]{:S(2)}, u32[]{:S(2)}) collective-permute-start(bf16[64,384]{1,0:T(8,128)(2,1)S(1)} %get-tuple-element.16), channel_id=1, source_target_pairs={{0,1},{1,0},{2,4},{3,5},{4,2},{5,3},{6,8},{7,9},{8,6},{9,7},{10,12... | collective-permute-start | bytes 147464 | tf_op jit(solution)/shard_map/ppermute | solution.py:284
  9.2 4.2 %collective-permute-start = (bf16[64,384]{1,0:T(8,128)(2,1)S(1)}, bf16[64,384]{1,0:T(8,128)(2,1)S(1)}, u32[]{:S(2)}, u32[]{:S(2)}) collective-permute-start(bf16[64,384]{1,0:T(8,128)(2,1)S(1)} %get-tuple-element.11.refs_2_.refs_3_), channel_id=1, source_target_pairs={{0,1},{1,0},{2,3},{3,2},{4,5},{5,4},{6,7},{7,6},{8,9},{9,8},{10,11... | collective-permute-start | bytes 147464 | tf_op jit(solution)/shard_map/ppermute | solution.py:284

commit v3 on v2

--- a/solution.py
+++ b/solution.py
@@ -16,6 +16,8 @@
 HALF = 64
 VALID = 16
 WIDE = 3 * LANE
+LAG_STEP = 4 * LANE
+STEP = 2 * LANE
 F32 = jnp.float32
 BF16 = jnp.bfloat16
 
@@ -35,13 +37,19 @@
     return out
 
 
-def fourier_table(samples):
-    number = np.arange(samples)
+def fourier_tables(samples):
     bins = np.arange(1, NBIN + 1)
-    angle = np.mod(number[:, None] * bins[None, :], 2 * samples) * (np.pi / samples)
-    taper = (0.5 - 0.5 * np.cos(number * (2.0 * np.pi / samples)))[:, None]
-    table = in_lanes(taper * np.cos(angle), -taper * np.sin(angle))
-    return split(np.pad(table, ((0, -samples % (2 * LANE)), (0, 0))))
+    turn = np.pi / samples
+    angle = np.mod(np.arange(STEP)[:, None] * bins[None, :], 2 * samples) * turn
+    high, low = split(in_lanes(np.cos(angle), -np.sin(angle)))
+    stretches = -(-samples // STEP)
+    angle = np.mod(np.arange(stretches)[:, None] * STEP * bins[None, :], 2 * samples) * turn
+    turns = np.stack([in_lanes(np.cos(angle), np.cos(angle)), in_lanes(np.sin(angle), -np.sin(angle))])
+    number = np.arange(stretches * STEP)
+    taper = np.where(number < samples, 0.5 - 0.5 * np.cos(number * (2.0 * np.pi / samples)), 0.0)
+    rows = np.concatenate([taper.reshape(stretches, STEP), np.zeros((stretches, WIDE - STEP))], axis=1)
+    factors = np.concatenate([rows[None], turns]).astype(np.float32)
+    return np.concatenate([high, high, low]), factors
 
 
 def lag_table(samples):
@@ -73,32 +81,21 @@
 
 
 def spectra_kernel(
-    per, seg, samples, rows_hbm, count_hbm, valid_hbm, traces_hbm, high_hbm, low_hbm,
-    own_ref, near_ref, far_ref, rows_ref, count_ref, valid_ref, traces, high, low, sems, small_sems,
+    per, seg, samples, rows_hbm, count_hbm, valid_hbm, traces_hbm, table_hbm, factors_hbm,
+    own_ref, near_ref, far_ref, rows_ref, count_ref, valid_ref, traces, table, factors, sems,
 ):
     lines = per * seg
-    step = 2 * LANE
-    cuts = range(0, samples, step)
-    copies = []
-    small = [
-        pltpu.make_async_copy(src, dst, small_sems.at[i])
-        for i, (src, dst) in enumerate(((rows_hbm, rows_ref), (count_hbm, count_ref), (valid_hbm, valid_ref)))
+    pairs = [
+        (traces_hbm, traces), (table_hbm, table), (factors_hbm, factors),
+        (rows_hbm, rows_ref), (count_hbm, count_ref), (valid_hbm, valid_ref),
     ]
-    for copy in small:
+    copies = [pltpu.make_async_copy(src, dst, sems.at[i]) for i, (src, dst) in enumerate(pairs)]
+    for copy in copies:
         copy.start()
-    first = pltpu.make_async_copy(traces_hbm, traces, sems.at[0])
-    first.start()
-    for i, at in enumerate(cuts):
-        here = pl.ds(at, step)
-        a = pltpu.make_async_copy(high_hbm.at[here], high.at[here], sems.at[1 + 2 * i])
-        b = pltpu.make_async_copy(low_hbm.at[here], low.at[here], sems.at[2 + 2 * i])
-        a.start()
-        b.start()
-        copies.append((a, b))
 
     odd = lax.rem(lax.axis_index("tile"), 2)
-    col = iota((2 * LANE, 2 * LANE), 0)
-    row = iota((2 * LANE, 2 * LANE), 1)
+    col = iota((STEP, STEP), 0)
+    row = iota((STEP, STEP), 1)
 
     def bin_of(lane):
         tail = lane & (HALF - 1)
@@ -113,7 +110,7 @@
     target = iota((lines, lines), 0)
     source = iota((lines, lines), 1)
     part, slot = divided(target, per)
-    for copy in small:
+    for copy in copies[-3:]:
         copy.wait()
 
     def choice(station):
@@ -131,22 +128,29 @@
 
     usable = jnp.concatenate(column_of(valid_ref[...].astype(F32)), axis=0)
 
-    first.wait()
-    total = jnp.zeros((lines, WIDE), F32)
-    for at, (a, b) in zip(cuts, copies):
-        x = traces[:, at : min(at + step, samples)]
-        if at + step > samples:
-            x = jnp.concatenate([x, jnp.zeros((lines, at + step - samples), F32)], axis=1)
+    for copy in copies[:3]:
+        copy.wait()
+    stretches = factors.shape[1]
+    left = []
+    for j in range(stretches):
+        at = j * STEP
+        x = traces[:, at : min(at + STEP, samples)]
+        if at + STEP > samples:
+            x = jnp.concatenate([x, jnp.zeros((lines, at + STEP - samples), F32)], axis=1)
+        x = x * factors[0, j : j + 1, :STEP]
         x_high = x.astype(BF16)
         x_low = (x - x_high.astype(F32)).astype(BF16)
-        both = jnp.concatenate([x_high, x_low], axis=0)
-        a.wait()
-        wide = jnp.dot(both, high[at : at + step, :], preferred_element_type=F32)
-        total = total + wide[:lines] + wide[lines:]
-        b.wait()
-        total = total + jnp.dot(x_high, low[at : at + step, :], preferred_element_type=F32)
-
-    real, imag, tail = total[:, :LANE], total[:, LANE : 2 * LANE], total[:, 2 * LANE :]
+        left.append(jnp.concatenate([x_high, x_low, x_high], axis=1))
+    parts = jnp.dot(jnp.concatenate(left, axis=0), table[...], preferred_element_type=F32)
+    real, imag, tail = (parts[:lines, k * LANE : (k + 1) * LANE] for k in range(3))
+    for j in range(1, stretches):
+        p_re, p_im, p_tail = (parts[j * lines : (j + 1) * lines, k * LANE : (k + 1) * LANE] for k in range(3))
+        turn = factors[1, j : j + 1, :]
+        swap = factors[2, j : j + 1, :]
+        real = real + p_re * turn[:, :LANE] + p_im * swap[:, :LANE]
+        imag = imag + p_im * turn[:, LANE : 2 * LANE] + p_re * swap[:, LANE : 2 * LANE]
+        tail = tail + p_tail * turn[:, 2 * LANE :] + pltpu.roll(p_tail, HALF, 1) * swap[:, 2 * LANE :]
+
     power = jnp.concatenate([real * real + imag * imag, tail * tail], axis=1)
     p_high = power.astype(BF16)
     p_low = (power - p_high.astype(F32)).astype(BF16)
@@ -253,15 +257,17 @@
     keep = jnp.concatenate(column_of(mask_ref[...].astype(F32)), axis=0)
     left = (cross[...] * keep).astype(BF16)
     left = jnp.concatenate([left, left], axis=1)
-    step = 4 * LANE
-    for lo in range(0, LAGS, step):
-        hi = min(lo + step, LAGS)
+    copies = []
+    for i, lo in enumerate(range(0, LAGS, LAG_STEP)):
+        hi = min(lo + LAG_STEP, LAGS)
         series = jnp.dot(left, table_ref[:, lo:hi], preferred_element_type=F32).astype(BF16)
         for s in range(per):
             result[s, :, lo:hi] = series[s * columns : (s + 1) * columns]
-    copy = pltpu.make_async_copy(result, out_ref, sems.at[0])
-    copy.start()
-    copy.wait()
+        here = (slice(None), slice(None), slice(lo, hi))
+        copies.append(pltpu.make_async_copy(result.at[here], out_ref.at[here], sems.at[i]))
+        copies[-1].start()
+    for copy in copies:
+        copy.wait()
 
 
 def solution(mesh):
@@ -287,11 +293,10 @@
         per, seg, samples = traces.shape
         lines = per * seg
         columns = pair_mask.shape[1]
-        high, low = map(jnp.asarray, fourier_table(samples))
-        table = jnp.asarray(lag_table(samples))
+        table, factors = map(jnp.asarray, fourier_tables(samples))
+        lag_basis = jnp.asarray(lag_table(samples))
         payload = pltpu.VMEM((lines, WIDE), BF16)
-        cuts = pl.cdiv(samples, 2 * LANE)
-        inputs = [boundary_rows, boundary_count, validity, traces.reshape(lines, samples), high, low]
+        inputs = [boundary_rows, boundary_count, validity, traces.reshape(lines, samples), table, factors]
         own, near, far = pl.pallas_call(
             lambda *refs: spectra_kernel(per, seg, samples, *refs),
             out_shape=(payload, payload, payload),
@@ -302,10 +307,9 @@
                 pltpu.SMEM(boundary_count.shape, jnp.int32),
                 pltpu.VMEM(validity.shape, jnp.int32),
                 pltpu.VMEM((lines, samples), F32),
-                pltpu.VMEM(high.shape, BF16),
-                pltpu.VMEM(low.shape, BF16),
-                pltpu.SemaphoreType.DMA((1 + 2 * cuts,)),
-                pltpu.SemaphoreType.DMA((3,)),
+                pltpu.VMEM(table.shape, BF16),
+                pltpu.VMEM(factors.shape, F32),
+                pltpu.SemaphoreType.DMA((6,)),
             ],
             compiler_params=pltpu.CompilerParams(vmem_limit_bytes=32 << 20),
             name="spectra",
@@ -313,11 +317,11 @@
         own_cols = [exchange(own, 0, d) for d in range(1, grps)]
         near_cols = [exchange(near, 1, d) for d in range(grps)]
         far_cols = [exchange(far, 2, d) for d in range(grps)]
-        mask, table, spread = pl.pallas_call(
+        mask, basis, spread = pl.pallas_call(
             lambda *refs: ready_kernel(per, seg, *refs),
             out_shape=(
                 pltpu.VMEM(pair_mask.shape, jnp.int32),
-                pltpu.VMEM(table.shape, BF16),
+                pltpu.VMEM(lag_basis.shape, BF16),
                 pltpu.VMEM((per * lines, WIDE), F32),
             ),
             in_specs=[hbm, hbm, vmem],
@@ -325,8 +329,8 @@
             scratch_shapes=[pltpu.SemaphoreType.DMA((2,))],
             compiler_params=pltpu.CompilerParams(vmem_limit_bytes=32 << 20),
             name="ready",
-        )(placed(pair_mask, pltpu.HBM), placed(table, pltpu.HBM), placed(own, pltpu.VMEM))
-        inputs = [mask, table, spread, own, *own_cols, *near_cols, *far_cols]
+        )(placed(pair_mask, pltpu.HBM), placed(lag_basis, pltpu.HBM), placed(own, pltpu.VMEM))
+        inputs = [mask, basis, spread, own, *own_cols, *near_cols, *far_cols]
         return pl.pallas_call(
             lambda *refs: lags_kernel(per, seg, grps, tiles, *refs),
             out_shape=jax.ShapeDtypeStruct((per, columns, LAGS), BF16),
@@ -335,7 +339,7 @@
             scratch_shapes=[
                 pltpu.VMEM((per * columns, WIDE), F32),
                 pltpu.VMEM((per, columns, LAGS), BF16),
-                pltpu.SemaphoreType.DMA((1,)),
+                pltpu.SemaphoreType.DMA((pl.cdiv(LAGS, LAG_STEP),)),
             ],
             compiler_params=pltpu.CompilerParams(vmem_limit_bytes=32 << 20),
             name="lags",

time: 15.4 us -> 13.4 us (0.87)
  Pallas kernels: 7.81 us -> 5.81 us
    pallas_call x1, Pallas kernels: 4.04 us -> 2.12 us  [on_device(): pl.pallas_call(lambda *refs: spectra_kernel(per, seg, samples, *refs), ou...]
  transfers between devices with their start and end apart: 5 -> 5, of which waited for: 3 -> 3; matrix products, arithmetic and copies ran while one was open for 0% -> 0% of each run, Pallas kernels for 13% -> 14%
where the time goes in v3:
time: 13.4 us; the launch traced here: 13.3 us
  Pallas kernels  5.81 us (43%)
  starting transfers between devices  5.21 us (39%)
  waiting for transfers between devices  2.19 us (16%)
    ppermute x5, starting transfers between devices, exchange(): return lax.ppermute(array, axes, pairs)  5.21 us
    ppermute x5, waiting for transfers between devices, exchange(): return lax.ppermute(array, axes, pairs)  2.19 us
    pallas_call x1, Pallas kernels, on_device(): pl.pallas_call(lambda *refs: spectra_kernel(per, seg, samples, *refs), ou...  2.12 us
    pallas_call x1, Pallas kernels, on_device(): pl.pallas_call(lambda *refs: ready_kernel(per, seg, *refs), out_shape=(pl...  1.91 us
    pallas_call x1, Pallas kernels, on_device(): pl.pallas_call(lambda *refs: lags_kernel(per, seg, grps, tiles, *refs), o...  1.78 us
  transfers between devices with their start and end apart: 5, of which 3 were waited for; matrix products, arithmetic and copies ran while one was open for 0% of the time, Pallas kernels for 14%

profile of v3, /device:TPU:0, one launch (start us, length us, event | category | flops | bytes accessed | tf_op | source)
XLA Modules:
  0.0 13.3 jit_solution(2271188951844973190)
XLA Ops:
  0.0 2.1 %spectra.1 = (bf16[64,384]{1,0:T(8,128)(2,1)S(1)}, bf16[64,384]{1,0:T(8,128)(2,1)S(1)}, bf16[64,384]{1,0:T(8,128)(2,1)S(1)}) custom-call(s32[1,2,4]{2,1,0:T(2,128)} %refs_0_.2, s32[1,2]{1,0:T(1,128)} %refs_1_.2, s32[4,16]{1,0:T(4,128)} %refs_2_.1, f32[64,1500]{1,0:T(8,128)} %bitcast.1, bf16[768,384]{1,0:T(8,128)(2,1)} %constant.6.clone.refs_4_, ...), custom_call_target="tpu_custom_call" | custom-call | tf_op jit(solution)/shard_map/spectra/pallas_call | solution.py:300
  2.1 2.5 %collective-permute-start.2 = (bf16[64,384]{1,0:T(8,128)(2,1)S(1)}, bf16[64,384]{1,0:T(8,128)(2,1)S(1)}, u32[]{:S(2)}, u32[]{:S(2)}) collective-permute-start(bf16[64,384]{1,0:T(8,128)(2,1)S(1)} %get-tuple-element.15), channel_id=1, source_target_pairs={{0,3},{1,2},{2,1},{3,0},{4,7},{5,6},{6,5},{7,4},{8,11},{9,10},{10,... | collective-permute-start | bytes 147464 | tf_op jit(solution)/shard_map/ppermute | solution.py:290
  4.6 0.7 %collective-permute-start.1 = (bf16[64,384]{1,0:T(8,128)(2,1)S(1)}, bf16[64,384]{1,0:T(8,128)(2,1)S(1)}, u32[]{:S(2)}, u32[]{:S(2)}) collective-permute-start(bf16[64,384]{1,0:T(8,128)(2,1)S(1)} %get-tuple-element.15), channel_id=1, source_target_pairs={{0,2},{1,3},{2,0},{3,1},{4,6},{5,7},{6,4},{7,5},{8,10},{9,11},{10,... | collective-permute-start | bytes 147464 | tf_op jit(solution)/shard_map/ppermute | solution.py:290
  5.3 0.0 collective-permute-start.4
  5.3 2.0 %collective-permute-start.3 = (bf16[64,384]{1,0:T(8,128)(2,1)S(1)}, bf16[64,384]{1,0:T(8,128)(2,1)S(1)}, u32[]{:S(2)}, u32[]{:S(2)}) collective-permute-start(bf16[64,384]{1,0:T(8,128)(2,1)S(1)} %get-tuple-element.16), channel_id=1, source_target_pairs={{0,1},{1,0},{2,4},{3,5},{4,2},{5,3},{6,8},{7,9},{8,6},{9,7},{10,12... | collective-permute-start | bytes 147464 | tf_op jit(solution)/shard_map/ppermute | solution.py:290
  7.3 0.0 collective-permute-start
  7.3 1.9 %ready.1 = (s32[4,24]{1,0:T(4,128)S(1)}, bf16[768,2001]{1,0:T(8,128)(2,1)S(1)}, f32[256,384]{1,0:T(8,128)S(1)}) custom-call(s32[4,24]{1,0:T(4,128)} %refs_0_.3, bf16[768,2001]{1,0:T(8,128)(2,1)} %constant.8.clone.refs_1_, bf16[64,384]{1,0:T(8,128)(2,1)S(1)} %get-tuple-element.11.refs_2_.refs_3_), custom_call_target="tpu_custom_call" | custom-call | tf_op jit(solution)/shard_map/ready/pallas_call | solution.py:320
  9.3 0.0 collective-permute-done.2.refs_6_
  9.3 0.0 collective-permute-done.1.refs_5_
  9.3 0.1 collective-permute-done.4.refs_8_
  9.4 1.5 %collective-permute-done.3.refs_7_ = bf16[64,384]{1,0:T(8,128)(2,1)S(1)} collective-permute-done((bf16[64,384]{1,0:T(8,128)(2,1)S(1)}, bf16[64,384]{1,0:T(8,128)(2,1)S(1)}, u32[]{:S(2)}, u32[]{:S(2)}) %collective-permute-start.3) | collective-permute-done | bytes 49184 | tf_op jit(solution)/shard_map/ppermute | solution.py:290
  10.9 0.6 %collective-permute-done.refs_4_ = bf16[64,384]{1,0:T(8,128)(2,1)S(1)} collective-permute-done((bf16[64,384]{1,0:T(8,128)(2,1)S(1)}, bf16[64,384]{1,0:T(8,128)(2,1)S(1)}, u32[]{:S(2)}, u32[]{:S(2)}) %collective-permute-start) | collective-permute-done | bytes 49184 | tf_op jit(solution)/shard_map/ppermute | solution.py:290
  11.5 1.8 %lags.1 = bf16[4,24,2001]{2,1,0:T(8,128)(2,1)} custom-call(s32[4,24]{1,0:T(4,128)S(1)} %get-tuple-element.12.refs_0_, bf16[768,2001]{1,0:T(8,128)(2,1)S(1)} %get-tuple-element.13.refs_1_, f32[256,384]{1,0:T(8,128)S(1)} %get-tuple-element.14.refs_2_, bf16[64,384]{1,0:T(8,128)(2,1)S(1)} %get-tuple-element.11.refs_2_.refs_3_, ...), custom_call_target="tpu_custom_call" | custom-call | tf_op jit(solution)/shard_map/lags/pallas_call | solution.py:334
Async XLA Ops:
  2.1 7.1 %collective-permute-start.2 = (bf16[64,384]{1,0:T(8,128)(2,1)S(1)}, bf16[64,384]{1,0:T(8,128)(2,1)S(1)}, u32[]{:S(2)}, u32[]{:S(2)}) collective-permute-start(bf16[64,384]{1,0:T(8,128)(2,1)S(1)} %get-tuple-element.15), channel_id=1, source_target_pairs={{0,3},{1,2},{2,1},{3,0},{4,7},{5,6},{6,5},{7,4},{8,11},{9,10},{10,... | collective-permute-start | bytes 147464 | tf_op jit(solution)/shard_map/ppermute | solution.py:290
  4.6 4.7 %collective-permute-start.1 = (bf16[64,384]{1,0:T(8,128)(2,1)S(1)}, bf16[64,384]{1,0:T(8,128)(2,1)S(1)}, u32[]{:S(2)}, u32[]{:S(2)}) collective-permute-start(bf16[64,384]{1,0:T(8,128)(2,1)S(1)} %get-tuple-element.15), channel_id=1, source_target_pairs={{0,2},{1,3},{2,0},{3,1},{4,6},{5,7},{6,4},{7,5},{8,10},{9,11},{10,... | collective-permute-start | bytes 147464 | tf_op jit(solution)/shard_map/ppermute | solution.py:290
  5.3 4.1 %collective-permute-start.4 = (bf16[64,384]{1,0:T(8,128)(2,1)S(1)}, bf16[64,384]{1,0:T(8,128)(2,1)S(1)}, u32[]{:S(2)}, u32[]{:S(2)}) collective-permute-start(bf16[64,384]{1,0:T(8,128)(2,1)S(1)} %get-tuple-element.16), channel_id=1, source_target_pairs={{0,1},{1,0},{2,5},{3,4},{4,3},{5,2},{6,9},{7,8},{8,7},{9,6},{10,13... | collective-permute-start | bytes 147464 | tf_op jit(solution)/shard_map/ppermute | solution.py:290
  5.3 5.6 %collective-permute-start.3 = (bf16[64,384]{1,0:T(8,128)(2,1)S(1)}, bf16[64,384]{1,0:T(8,128)(2,1)S(1)}, u32[]{:S(2)}, u32[]{:S(2)}) collective-permute-start(bf16[64,384]{1,0:T(8,128)(2,1)S(1)} %get-tuple-element.16), channel_id=1, source_target_pairs={{0,1},{1,0},{2,4},{3,5},{4,2},{5,3},{6,8},{7,9},{8,6},{9,7},{10,12... | collective-permute-start | bytes 147464 | tf_op jit(solution)/shard_map/ppermute | solution.py:290
  7.3 4.2 %collective-permute-start = (bf16[64,384]{1,0:T(8,128)(2,1)S(1)}, bf16[64,384]{1,0:T(8,128)(2,1)S(1)}, u32[]{:S(2)}, u32[]{:S(2)}) collective-permute-start(bf16[64,384]{1,0:T(8,128)(2,1)S(1)} %get-tuple-element.11.refs_2_.refs_3_), channel_id=1, source_target_pairs={{0,1},{1,0},{2,3},{3,2},{4,5},{5,4},{6,7},{7,6},{8,9},{9,8},{10,11... | collective-permute-start | bytes 147464 | tf_op jit(solution)/shard_map/ppermute | solution.py:290

commit v4 on v3

--- a/solution.py
+++ b/solution.py
@@ -14,6 +14,7 @@
 LANE = 128
 TAIL = NBIN - LANE
 HALF = 64
+LAST = ((0, 1), (1, 0))
 VALID = 16
 WIDE = 3 * LANE
 LAG_STEP = 4 * LANE
@@ -81,9 +82,10 @@
 
 
 def spectra_kernel(
-    per, seg, samples, rows_hbm, count_hbm, valid_hbm, traces_hbm, table_hbm, factors_hbm,
-    own_ref, near_ref, far_ref, rows_ref, count_ref, valid_ref, traces, table, factors, sems,
+    per, seg, samples, ways, rows_hbm, count_hbm, valid_hbm, traces_hbm, table_hbm, factors_hbm,
+    *refs,
 ):
+    mine_ref, *outs, rows_ref, count_ref, valid_ref, traces, table, factors, sems = refs
     lines = per * seg
     pairs = [
         (traces_hbm, traces), (table_hbm, table), (factors_hbm, factors),
@@ -161,14 +163,57 @@
     tail = jnp.where(iota((lines, LANE), 1) == VALID, usable, tail)
     white = jnp.concatenate([real * factor[:, :LANE], imag * factor[:, :LANE], tail], axis=1)
     chosen = jnp.dot(picks, white.astype(BF16), preferred_element_type=F32).astype(BF16)
-    own_ref[...] = chosen[:lines]
-    near_ref[...] = chosen[lines : 2 * lines]
-    far_ref[...] = chosen[2 * lines :]
-
-
-def ready_kernel(per, seg, mask_hbm, table_hbm, own_ref, mask_ref, table_ref, spread_ref, sems):
+    mine_ref[...] = chosen[:lines]
+    for ref, way in zip(outs, ways):
+        ref[...] = chosen[way * lines : (way + 1) * lines]
+
+
+def stacked(per, lines, spread, ref):
+    sums = [[None] * 4 for _ in range(per)]
+
+    def add(s, i, value):
+        sums[s][i] = value if sums[s][i] is None else sums[s][i] + value
+
+    for at in range(0, lines, 16):
+        both = ref[at : at + 16, :].astype(F32)
+        for half in range(2):
+            one = both[8 * half : 8 * half + 8]
+            c_re, c_im, c_tail = one[:, :LANE], one[:, LANE : 2 * LANE], one[:, 2 * LANE :]
+            c_turn = pltpu.roll(c_tail, HALF, 1)
+            for s in range(per):
+                here = s * lines + at + 8 * half
+                left = spread[here : here + 8, :]
+                l_re, l_im, l_tail = left[:, :LANE], left[:, LANE : 2 * LANE], left[:, 2 * LANE :]
+                add(s, 0, l_re * c_re + l_im * c_im)
+                add(s, 1, l_im * c_re - l_re * c_im)
+                add(s, 2, l_tail * c_tail)
+                add(s, 3, l_tail * c_turn)
+    low_lanes = iota((8, LANE), 1) < HALF
+    out = []
+    for s in range(per):
+        straight, turned = sums[s][2], sums[s][3]
+        straight = straight + pltpu.roll(straight, HALF, 1)
+        turned = turned - pltpu.roll(turned, HALF, 1)
+        all_lanes = [sums[s][0], sums[s][1], jnp.where(low_lanes, straight, turned)]
+        out.append([v + pltpu.roll(v, 4, 0) for v in all_lanes])
+    return out
+
+
+def store_sums(per, ref, i, pieces):
+    for s, sums in enumerate(pieces):
+        at = (i * per + s) * 8
+        for k in range(3):
+            ref[at : at + 8, k * LANE : (k + 1) * LANE] = sums[k]
+
+
+def load_sums(per, ref, i):
+    rows = [ref[(i * per + s) * 8 : (i * per + s) * 8 + 8, :] for s in range(per)]
+    return [[row[:, k * LANE : (k + 1) * LANE] for k in range(3)] for row in rows]
+
+
+def ready_kernel(per, seg, mask_hbm, basis_hbm, mine_ref, mask_ref, basis_ref, spread_ref, sums_ref, sems):
     copies = [
-        pltpu.make_async_copy(table_hbm, table_ref, sems.at[0]),
+        pltpu.make_async_copy(basis_hbm, basis_ref, sems.at[0]),
         pltpu.make_async_copy(mask_hbm, mask_ref, sems.at[1]),
     ]
     for copy in copies:
@@ -177,52 +222,26 @@
     part, _ = divided(iota((lines, lines), 0), per)
     source = iota((lines, lines), 1)
     pick = [jnp.where(source == part * per + s, 1.0, 0.0).astype(BF16) for s in range(per)]
-    spread_ref[...] = jnp.dot(jnp.concatenate(pick, axis=0), own_ref[...], preferred_element_type=F32)
+    spread_ref[...] = jnp.dot(jnp.concatenate(pick, axis=0), mine_ref[...], preferred_element_type=F32)
+    store_sums(per, sums_ref, 0, stacked(per, lines, spread_ref, mine_ref))
     for copy in copies:
         copy.wait()
 
 
-def lags_kernel(per, seg, grps, tiles, *refs):
-    mask_ref, table_ref, spread = refs[:3]
-    refs = refs[3:]
-    own_cols, near_cols, far_cols = (refs[i * grps : (i + 1) * grps] for i in range(3))
-    out_ref, cross, result, sems = refs[3 * grps :]
+def early_kernel(per, seg, spread_ref, *refs):
+    for i, ref in enumerate(refs[:-1]):
+        store_sums(per, refs[-1], i, stacked(per, per * seg, spread_ref, ref))
+
+
+def lags_kernel(per, seg, grps, tiles, order, *refs):
+    mask_ref, basis_ref, spread_ref, mine_ref, early_ref = refs[:5]
+    out_ref, cross, result, sems = refs[-4:]
     lines = per * seg
     columns = 3 * grps * per
     tile = lax.axis_index("tile")
     grp = lax.axis_index("grp")
     odd = lax.rem(tile, 2)
     inside = jnp.where(odd == 1, tile < tiles - 1, tile > 0)
-
-    def stacked(ref):
-        sums = [[None] * 4 for _ in range(per)]
-
-        def add(s, i, value):
-            sums[s][i] = value if sums[s][i] is None else sums[s][i] + value
-
-        for at in range(0, lines, 16):
-            both = ref[at : at + 16, :].astype(F32)
-            for half in range(2):
-                one = both[8 * half : 8 * half + 8]
-                c_re, c_im, c_tail = one[:, :LANE], one[:, LANE : 2 * LANE], one[:, 2 * LANE :]
-                c_turn = pltpu.roll(c_tail, HALF, 1)
-                for s in range(per):
-                    first = s * lines + at + 8 * half
-                    left = spread[first : first + 8, :]
-                    l_re, l_im, l_tail = left[:, :LANE], left[:, LANE : 2 * LANE], left[:, 2 * LANE :]
-                    add(s, 0, l_re * c_re + l_im * c_im)
-                    add(s, 1, l_im * c_re - l_re * c_im)
-                    add(s, 2, l_tail * c_tail)
-                    add(s, 3, l_tail * c_turn)
-        low_lanes = iota((8, LANE), 1) < HALF
-        out = []
-        for s in range(per):
-            straight, turned = sums[s][2], sums[s][3]
-            straight = straight + pltpu.roll(straight, HALF, 1)
-            turned = turned - pltpu.roll(turned, HALF, 1)
-            all_lanes = [sums[s][0], sums[s][1], jnp.where(low_lanes, straight, turned)]
-            out.append([v + pltpu.roll(v, 4, 0) for v in all_lanes])
-        return out
 
     def by_place(pieces):
         places = []
@@ -234,10 +253,14 @@
             places.append(value)
         return places
 
-    def of(cols):
-        return by_place([stacked(c) for c in cols])
-
-    own, near, far = of(own_cols), of(near_cols), of(far_cols)
+    soon, names = order
+    sums = {(0, 0): load_sums(per, mine_ref, 0)}
+    for i, name in enumerate(names):
+        if i < soon:
+            sums[name] = load_sums(per, early_ref, i)
+        else:
+            sums[name] = stacked(per, lines, spread_ref, refs[5 + i - soon])
+    own, near, far = (by_place([sums[way, d] for d in range(grps)]) for way in range(3))
     upper = iota((8, LANE), 0) < 4
     for s in range(per):
         slots = []
@@ -260,7 +283,7 @@
     copies = []
     for i, lo in enumerate(range(0, LAGS, LAG_STEP)):
         hi = min(lo + LAG_STEP, LAGS)
-        series = jnp.dot(left, table_ref[:, lo:hi], preferred_element_type=F32).astype(BF16)
+        series = jnp.dot(left, basis_ref[:, lo:hi], preferred_element_type=F32).astype(BF16)
         for s in range(per):
             result[s, :, lo:hi] = series[s * columns : (s + 1) * columns]
         here = (slice(None), slice(None), slice(lo, hi))
@@ -296,12 +319,16 @@
         table, factors = map(jnp.asarray, fourier_tables(samples))
         lag_basis = jnp.asarray(lag_table(samples))
         payload = pltpu.VMEM((lines, WIDE), BF16)
+        names = [(2, d) for d in reversed(range(grps))]
+        names += [(1, d) for d in range(1, grps)] + [(0, d) for d in range(1, grps)] + [(1, 0)]
+        soon = [name for name in names if name not in LAST]
+        late = [name for name in names if name in LAST]
         inputs = [boundary_rows, boundary_count, validity, traces.reshape(lines, samples), table, factors]
-        own, near, far = pl.pallas_call(
-            lambda *refs: spectra_kernel(per, seg, samples, *refs),
-            out_shape=(payload, payload, payload),
+        mine, *rest = pl.pallas_call(
+            lambda *refs: spectra_kernel(per, seg, samples, [way for way, _ in names], *refs),
+            out_shape=(payload,) * (1 + len(names)),
             in_specs=[hbm] * len(inputs),
-            out_specs=(vmem, vmem, vmem),
+            out_specs=(vmem,) * (1 + len(names)),
             scratch_shapes=[
                 pltpu.SMEM(boundary_rows.shape, jnp.int32),
                 pltpu.SMEM(boundary_count.shape, jnp.int32),
@@ -314,25 +341,34 @@
             compiler_params=pltpu.CompilerParams(vmem_limit_bytes=32 << 20),
             name="spectra",
         )(*[placed(x, pltpu.HBM) for x in inputs])
-        own_cols = [exchange(own, 0, d) for d in range(1, grps)]
-        near_cols = [exchange(near, 1, d) for d in range(grps)]
-        far_cols = [exchange(far, 2, d) for d in range(grps)]
-        mask, basis, spread = pl.pallas_call(
+        came = {name: exchange(array, *name) for name, array in zip(names, rest)}
+        mask, basis, spread, first = pl.pallas_call(
             lambda *refs: ready_kernel(per, seg, *refs),
             out_shape=(
                 pltpu.VMEM(pair_mask.shape, jnp.int32),
                 pltpu.VMEM(lag_basis.shape, BF16),
                 pltpu.VMEM((per * lines, WIDE), F32),
+                pltpu.VMEM((per * 8, WIDE), F32),
             ),
             in_specs=[hbm, hbm, vmem],
-            out_specs=(vmem, vmem, vmem),
+            out_specs=(vmem,) * 4,
             scratch_shapes=[pltpu.SemaphoreType.DMA((2,))],
             compiler_params=pltpu.CompilerParams(vmem_limit_bytes=32 << 20),
             name="ready",
-        )(placed(pair_mask, pltpu.HBM), placed(lag_basis, pltpu.HBM), placed(own, pltpu.VMEM))
-        inputs = [mask, basis, spread, own, *own_cols, *near_cols, *far_cols]
+        )(placed(pair_mask, pltpu.HBM), placed(lag_basis, pltpu.HBM), placed(mine, pltpu.VMEM))
+        inputs = [placed(x, pltpu.VMEM) for x in (spread, *(came[name] for name in soon))]
+        early = pl.pallas_call(
+            lambda *refs: early_kernel(per, seg, *refs),
+            out_shape=pltpu.VMEM((len(soon) * per * 8, WIDE), F32),
+            in_specs=[vmem] * len(inputs),
+            out_specs=vmem,
+            compiler_params=pltpu.CompilerParams(vmem_limit_bytes=32 << 20),
+            name="early",
+        )(*inputs)
+        order = len(soon), soon + late
+        inputs = [mask, basis, spread, first, early, *(came[name] for name in late)]
         return pl.pallas_call(
-            lambda *refs: lags_kernel(per, seg, grps, tiles, *refs),
+            lambda *refs: lags_kernel(per, seg, grps, tiles, order, *refs),
             out_shape=jax.ShapeDtypeStruct((per, columns, LAGS), BF16),
             in_specs=[vmem] * len(inputs),
             out_specs=hbm,

time: 13.4 us -> 12.7 us (0.948)
  waiting for transfers between devices: 2.19 us -> 0.88 us
  starting transfers between devices: 5.21 us -> 5.72 us
    ppermute x5, waiting for transfers between devices: 2.19 us -> 0.88 us  [exchange(): return lax.ppermute(array, axes, pairs)]
    ppermute x5, starting transfers between devices: 5.21 us -> 5.72 us  [exchange(): return lax.ppermute(array, axes, pairs)]
    pallas_call x2 -> x3, Pallas kernels: 3.9 us -> 3.96 us  [the longest x1 2.12 us: on_device(): pl.pallas_call(lambda *refs: spectra_kernel(per, seg, samples, [way for w...]
  transfers between devices with their start and end apart: 5 -> 5, of which waited for: 3 -> 1; matrix products, arithmetic and copies ran while one was open for 0% -> 0% of each run, Pallas kernels for 14% -> 18%
where the time goes in v4:
time: 12.7 us; the launch traced here: 12.5 us
  Pallas kernels  5.87 us (46%)
  starting transfers between devices  5.72 us (45%)
  waiting for transfers between devices  0.88 us (7%)
    ppermute x5, starting transfers between devices, exchange(): return lax.ppermute(array, axes, pairs)  5.72 us
    pallas_call x1, Pallas kernels, on_device(): pl.pallas_call(lambda *refs: spectra_kernel(per, seg, samples, [way for w...  2.12 us
    pallas_call x1, Pallas kernels, on_device(): pl.pallas_call(lambda *refs: ready_kernel(per, seg, *refs), out_shape=(pl...  1.91 us
    pallas_call x1, Pallas kernels, on_device(): pl.pallas_call(lambda *refs: lags_kernel(per, seg, grps, tiles, order, *r...  1.56 us
    ppermute x5, waiting for transfers between devices, exchange(): return lax.ppermute(array, axes, pairs)  0.88 us
    pallas_call x1, Pallas kernels, on_device(): pl.pallas_call(lambda *refs: early_kernel(per, seg, *refs), out_shape=plt...  0.29 us
  transfers between devices with their start and end apart: 5, of which 1 were waited for; matrix products, arithmetic and copies ran while one was open for 0% of the time, Pallas kernels for 18%

profile of v4, /device:TPU:0, one launch (start us, length us, event | category | flops | bytes accessed | tf_op | source)
XLA Modules:
  0.0 12.5 jit_solution(18306271461659053403)
XLA Ops:
  0.0 2.1 %spectra.1 = (bf16[64,384]{1,0:T(8,128)(2,1)S(1)}, bf16[64,384]{1,0:T(8,128)(2,1)S(1)}, bf16[64,384]{1,0:T(8,128)(2,1)S(1)}, bf16[64,384]{1,0:T(8,128)(2,1)S(1)}...) custom-call(s32[1,2,4]{2,1,0:T(2,128)} %refs_0_.2, s32[1,2]{1,0:T(1,128)} %refs_1_.2, s32[4,16]{1,0:T(4,128)} %refs_2_.1, ...), custom_call_target="tpu_custom_call" | custom-call | tf_op jit(solution)/shard_map/spectra/pallas_call | solution.py:327
  2.1 3.0 %collective-permute-start = (bf16[64,384]{1,0:T(8,128)(2,1)S(1)}, bf16[64,384]{1,0:T(8,128)(2,1)S(1)}, u32[]{:S(2)}, u32[]{:S(2)}) collective-permute-start(bf16[64,384]{1,0:T(8,128)(2,1)S(1)} %get-tuple-element.20), channel_id=1, source_target_pairs={{0,1},{1,0},{2,5},{3,4},{4,3},{5,2},{6,9},{7,8},{8,7},{9,6},{10,13... | collective-permute-start | bytes 147464 | tf_op jit(solution)/shard_map/ppermute | solution.py:313
  5.2 0.1 collective-permute-start.1
  5.2 1.2 %collective-permute-start.2 = (bf16[64,384]{1,0:T(8,128)(2,1)S(1)}, bf16[64,384]{1,0:T(8,128)(2,1)S(1)}, u32[]{:S(2)}, u32[]{:S(2)}) collective-permute-start(bf16[64,384]{1,0:T(8,128)(2,1)S(1)} %get-tuple-element.22), channel_id=1, source_target_pairs={{0,3},{1,2},{2,1},{3,0},{4,7},{5,6},{6,5},{7,4},{8,11},{9,10},{10,... | collective-permute-start | bytes 147464 | tf_op jit(solution)/shard_map/ppermute | solution.py:313
  6.5 1.4 %collective-permute-start.3 = (bf16[64,384]{1,0:T(8,128)(2,1)S(1)}, bf16[64,384]{1,0:T(8,128)(2,1)S(1)}, u32[]{:S(2)}, u32[]{:S(2)}) collective-permute-start(bf16[64,384]{1,0:T(8,128)(2,1)S(1)} %get-tuple-element.23), channel_id=1, source_target_pairs={{0,1},{1,0},{2,3},{3,2},{4,5},{5,4},{6,7},{7,6},{8,9},{9,8},{10,11... | collective-permute-start | bytes 147464 | tf_op jit(solution)/shard_map/ppermute | solution.py:313
  7.8 0.0 collective-permute-start.4
  7.8 1.9 %ready.1 = (s32[4,24]{1,0:T(4,128)S(1)}, bf16[768,2001]{1,0:T(8,128)(2,1)S(1)}, f32[256,384]{1,0:T(8,128)S(1)}, f32[32,384]{1,0:T(8,128)S(1)}) custom-call(s32[4,24]{1,0:T(4,128)} %refs_0_.3, bf16[768,2001]{1,0:T(8,128)(2,1)} %constant.8.clone.refs_1_, bf16[64,384]{1,0:T(8,128)(2,1)S(1)} %get-tuple-element.15.refs_2_), custom_call_target="tpu_custom_call" | custom-call | tf_op jit(solution)/shard_map/ready/pallas_call | solution.py:345
  9.8 0.0 collective-permute-done.refs_1_
  9.8 0.0 collective-permute-done.1.refs_2_
  9.8 0.0 collective-permute-done.2.refs_3_
  9.8 0.3 %early.1.refs_4_ = f32[96,384]{1,0:T(8,128)S(1)} custom-call(f32[256,384]{1,0:T(8,128)S(1)} %get-tuple-element.18.refs_0_.refs_2_, bf16[64,384]{1,0:T(8,128)(2,1)S(1)} %collective-permute-done.refs_1_, bf16[64,384]{1,0:T(8,128)(2,1)S(1)} %collective-permute-done.1.refs_2_, bf16[64,384]{1,0:T(8,128)(2,1)S(1)} %collective-permute-done.2.refs_3_), custom_call_target="tpu_custom_call" | custom-call | tf_op jit(solution)/shard_map/early/pallas_call | solution.py:360
  10.1 0.9 %collective-permute-done.3.refs_5_ = bf16[64,384]{1,0:T(8,128)(2,1)S(1)} collective-permute-done((bf16[64,384]{1,0:T(8,128)(2,1)S(1)}, bf16[64,384]{1,0:T(8,128)(2,1)S(1)}, u32[]{:S(2)}, u32[]{:S(2)}) %collective-permute-start.3) | collective-permute-done | bytes 49184 | tf_op jit(solution)/shard_map/ppermute | solution.py:313
  11.0 0.0 collective-permute-done.4.refs_6_
  11.0 1.6 %lags.1 = bf16[4,24,2001]{2,1,0:T(8,128)(2,1)} custom-call(s32[4,24]{1,0:T(4,128)S(1)} %get-tuple-element.16.refs_0_, bf16[768,2001]{1,0:T(8,128)(2,1)S(1)} %get-tuple-element.17.refs_1_, f32[256,384]{1,0:T(8,128)S(1)} %get-tuple-element.18.refs_0_.refs_2_, f32[32,384]{1,0:T(8,128)S(1)} %get-tuple-element.19.refs_3_, f32[96,384]{1,0:T(8,128)S(1)} %early.1.refs_4_, ...), custom_call_target="tpu_custom_call" | custom-call | tf_op jit(solution)/shard_map/lags/pallas_call | solution.py:370
Async XLA Ops:
  2.1 7.6 %collective-permute-start = (bf16[64,384]{1,0:T(8,128)(2,1)S(1)}, bf16[64,384]{1,0:T(8,128)(2,1)S(1)}, u32[]{:S(2)}, u32[]{:S(2)}) collective-permute-start(bf16[64,384]{1,0:T(8,128)(2,1)S(1)} %get-tuple-element.20), channel_id=1, source_target_pairs={{0,1},{1,0},{2,5},{3,4},{4,3},{5,2},{6,9},{7,8},{8,7},{9,6},{10,13... | collective-permute-start | bytes 147464 | tf_op jit(solution)/shard_map/ppermute | solution.py:313
  5.2 4.6 %collective-permute-start.1 = (bf16[64,384]{1,0:T(8,128)(2,1)S(1)}, bf16[64,384]{1,0:T(8,128)(2,1)S(1)}, u32[]{:S(2)}, u32[]{:S(2)}) collective-permute-start(bf16[64,384]{1,0:T(8,128)(2,1)S(1)} %get-tuple-element.21), channel_id=1, source_target_pairs={{0,1},{1,0},{2,4},{3,5},{4,2},{5,3},{6,8},{7,9},{8,6},{9,7},{10,12... | collective-permute-start | bytes 147464 | tf_op jit(solution)/shard_map/ppermute | solution.py:313
  5.2 4.5 %collective-permute-start.2 = (bf16[64,384]{1,0:T(8,128)(2,1)S(1)}, bf16[64,384]{1,0:T(8,128)(2,1)S(1)}, u32[]{:S(2)}, u32[]{:S(2)}) collective-permute-start(bf16[64,384]{1,0:T(8,128)(2,1)S(1)} %get-tuple-element.22), channel_id=1, source_target_pairs={{0,3},{1,2},{2,1},{3,0},{4,7},{5,6},{6,5},{7,4},{8,11},{9,10},{10,... | collective-permute-start | bytes 147464 | tf_op jit(solution)/shard_map/ppermute | solution.py:313
  6.5 4.5 %collective-permute-start.3 = (bf16[64,384]{1,0:T(8,128)(2,1)S(1)}, bf16[64,384]{1,0:T(8,128)(2,1)S(1)}, u32[]{:S(2)}, u32[]{:S(2)}) collective-permute-start(bf16[64,384]{1,0:T(8,128)(2,1)S(1)} %get-tuple-element.23), channel_id=1, source_target_pairs={{0,1},{1,0},{2,3},{3,2},{4,5},{5,4},{6,7},{7,6},{8,9},{9,8},{10,11... | collective-permute-start | bytes 147464 | tf_op jit(solution)/shard_map/ppermute | solution.py:313
  7.8 3.1 %collective-permute-start.4 = (bf16[64,384]{1,0:T(8,128)(2,1)S(1)}, bf16[64,384]{1,0:T(8,128)(2,1)S(1)}, u32[]{:S(2)}, u32[]{:S(2)}) collective-permute-start(bf16[64,384]{1,0:T(8,128)(2,1)S(1)} %get-tuple-element.24), channel_id=1, source_target_pairs={{0,2},{1,3},{2,0},{3,1},{4,6},{5,7},{6,4},{7,5},{8,10},{9,11},{10,... | collective-permute-start | bytes 147464 | tf_op jit(solution)/shard_map/ppermute | solution.py:313

commit v5 on v4

--- a/solution.py
+++ b/solution.py
@@ -58,8 +58,7 @@
     bins = np.arange(1, NBIN + 1)
     angle = np.mod(lags[:, None] * bins[None, :], 2 * samples) * (np.pi / samples)
     scale = 1.0 / np.sqrt(NBIN)
-    high, low = split(in_lanes(scale * np.cos(angle), -scale * np.sin(angle)))
-    return np.concatenate([high.T, low.T], axis=0)
+    return in_lanes(scale * np.cos(angle), -scale * np.sin(angle)).T.astype(ml_dtypes.bfloat16)
 
 
 def iota(shape, dim):
@@ -211,10 +210,10 @@
     return [[row[:, k * LANE : (k + 1) * LANE] for k in range(3)] for row in rows]
 
 
-def ready_kernel(per, seg, mask_hbm, basis_hbm, mine_ref, mask_ref, basis_ref, spread_ref, sums_ref, sems):
+def ready_kernel(per, seg, mask_hbm, basis_hbm, mine_ref, basis_ref, keep_ref, spread_ref, sums_ref, mask_ref, sems):
     copies = [
-        pltpu.make_async_copy(basis_hbm, basis_ref, sems.at[0]),
-        pltpu.make_async_copy(mask_hbm, mask_ref, sems.at[1]),
+        pltpu.make_async_copy(mask_hbm, mask_ref, sems.at[0]),
+        pltpu.make_async_copy(basis_hbm, basis_ref, sems.at[1]),
     ]
     for copy in copies:
         copy.start()
@@ -224,68 +223,74 @@
     pick = [jnp.where(source == part * per + s, 1.0, 0.0).astype(BF16) for s in range(per)]
     spread_ref[...] = jnp.dot(jnp.concatenate(pick, axis=0), mine_ref[...], preferred_element_type=F32)
     store_sums(per, sums_ref, 0, stacked(per, lines, spread_ref, mine_ref))
-    for copy in copies:
-        copy.wait()
-
-
-def early_kernel(per, seg, spread_ref, *refs):
-    for i, ref in enumerate(refs[:-1]):
-        store_sums(per, refs[-1], i, stacked(per, per * seg, spread_ref, ref))
-
-
-def lags_kernel(per, seg, grps, tiles, order, *refs):
-    mask_ref, basis_ref, spread_ref, mine_ref, early_ref = refs[:5]
-    out_ref, cross, result, sems = refs[-4:]
-    lines = per * seg
-    columns = 3 * grps * per
+    copies[0].wait()
+    keep = jnp.concatenate(column_of(mask_ref[...].astype(F32)), axis=0)
+    keep_ref[...] = jnp.broadcast_to(keep, keep_ref.shape)
+    copies[1].wait()
+
+
+def place_of(name, grps, tiles):
+    way, by = name
     tile = lax.axis_index("tile")
-    grp = lax.axis_index("grp")
     odd = lax.rem(tile, 2)
-    inside = jnp.where(odd == 1, tile < tiles - 1, tile > 0)
-
-    def by_place(pieces):
-        places = []
-        for g in range(grps):
-            value = pieces[0]
-            for d in range(1, grps):
-                here = lax.rem(grp + (grps - d), grps) == g
-                value = [[jnp.where(here, p, v) for p, v in zip(ps, vs)] for ps, vs in zip(pieces[d], value)]
-            places.append(value)
-        return places
-
-    soon, names = order
-    sums = {(0, 0): load_sums(per, mine_ref, 0)}
-    for i, name in enumerate(names):
-        if i < soon:
-            sums[name] = load_sums(per, early_ref, i)
-        else:
-            sums[name] = stacked(per, lines, spread_ref, refs[5 + i - soon])
-    own, near, far = (by_place([sums[way, d] for d in range(grps)]) for way in range(3))
-    upper = iota((8, LANE), 0) < 4
-    for s in range(per):
-        slots = []
-        for g in range(grps):
-            n = near[g][s]
-            f = [jnp.where(inside, v, 0.0) for v in far[g][s]]
-            below = [jnp.where(odd == 1, a, b) for a, b in zip(n, f)]
-            above = [jnp.where(odd == 1, b, a) for a, b in zip(n, f)]
-            slots += [own[g][s], below, above]
-        for i in range(0, len(slots), 2):
-            rows = [jnp.where(upper, a, b) for a, b in zip(slots[i], slots[i + 1])]
-            count = jnp.maximum(rows[2][:, VALID : VALID + 1], 1.0)
-            at = s * columns + 4 * i
-            for j in range(3):
-                cross[at : at + 8, j * LANE : (j + 1) * LANE] = rows[j] / count
-
-    keep = jnp.concatenate(column_of(mask_ref[...].astype(F32)), axis=0)
-    left = (cross[...] * keep).astype(BF16)
-    left = jnp.concatenate([left, left], axis=1)
+    source = lax.rem(lax.axis_index("grp") + (grps - by), grps)
+    kind = (0, 2 - odd, 1 + odd)[way]
+    there = jnp.where(odd == 1, tile < tiles - 1, tile > 0) if way == 2 else None
+    return 3 * source + kind, there
+
+
+def over_count(rows):
+    scale = 1.0 / jnp.maximum(rows[2][:, VALID : VALID + 1], 1.0)
+    return jnp.concatenate([row * scale for row in rows], axis=1).astype(BF16)
+
+
+def early_kernel(per, seg, grps, tiles, names, basis_ref, spread_ref, mine_ref, *refs):
+    series_ref, left = refs[-2:]
+    sums = [load_sums(per, mine_ref, 0)]
+    sums += [stacked(per, per * seg, spread_ref, ref) for ref in refs[:-2]]
+    places = [place_of(name, grps, tiles) for name in ((0, 0), *names)]
+    half = iota((8, LANE), 0) >> 2
+    blocks = 3 * grps // 2
+    for b in range(blocks):
+        fits = []
+        for place, there in places:
+            fit = (half + 2 * b) == place
+            fits.append(fit if there is None else fit & there)
+        for s in range(per):
+            rows = [jnp.zeros((8, LANE), F32)] * 3
+            for fit, piece in zip(fits, sums):
+                rows = [jnp.where(fit, new, row) for new, row in zip(piece[s], rows)]
+            at = (s * blocks + b) * 8
+            scale = 1.0 / jnp.maximum(rows[2][:, VALID : VALID + 1], 1.0)
+            for k in range(3):
+                left[at : at + 8, k * LANE : (k + 1) * LANE] = rows[k] * scale
+    series_ref[...] = jnp.dot(left[...].astype(BF16), basis_ref[...], preferred_element_type=F32)
+
+
+def lags_kernel(per, seg, grps, tiles, names, basis_ref, keep_ref, spread_ref, series_ref, *refs):
+    out_ref, result, sems = refs[-3:]
+    left = []
+    for ref in refs[:-3]:
+        left += [over_count(rows) for rows in stacked(per, per * seg, spread_ref, ref)]
+    left = jnp.concatenate(left, axis=0)
+    places = [place_of(name, grps, tiles) for name in names]
+    blocks = 3 * grps // 2
     copies = []
     for i, lo in enumerate(range(0, LAGS, LAG_STEP)):
         hi = min(lo + LAG_STEP, LAGS)
-        series = jnp.dot(left, basis_ref[:, lo:hi], preferred_element_type=F32).astype(BF16)
+        late = jnp.dot(left, basis_ref[:, lo:hi], preferred_element_type=F32)
+        half = iota((8, hi - lo), 0) >> 2
         for s in range(per):
-            result[s, :, lo:hi] = series[s * columns : (s + 1) * columns]
+            rows = []
+            for b in range(blocks):
+                at = (s * blocks + b) * 8
+                row = series_ref[at : at + 8, lo:hi]
+                for p, (place, there) in enumerate(places):
+                    fit = (half + 2 * b) == place
+                    fit = fit if there is None else fit & there
+                    row = jnp.where(fit, late[(p * per + s) * 8 : (p * per + s) * 8 + 8], row)
+                rows.append(row * keep_ref[at : at + 8, :1])
+            result[s, :, lo:hi] = jnp.concatenate(rows, axis=0).astype(BF16)
         here = (slice(None), slice(None), slice(lo, hi))
         copies.append(pltpu.make_async_copy(result.at[here], out_ref.at[here], sems.at[i]))
         copies[-1].start()
@@ -342,44 +347,44 @@
             name="spectra",
         )(*[placed(x, pltpu.HBM) for x in inputs])
         came = {name: exchange(array, *name) for name, array in zip(names, rest)}
-        mask, basis, spread, first = pl.pallas_call(
+        rows = per * columns
+        basis, keep, spread, first = pl.pallas_call(
             lambda *refs: ready_kernel(per, seg, *refs),
             out_shape=(
-                pltpu.VMEM(pair_mask.shape, jnp.int32),
                 pltpu.VMEM(lag_basis.shape, BF16),
+                pltpu.VMEM((rows, LANE), F32),
                 pltpu.VMEM((per * lines, WIDE), F32),
                 pltpu.VMEM((per * 8, WIDE), F32),
             ),
             in_specs=[hbm, hbm, vmem],
             out_specs=(vmem,) * 4,
-            scratch_shapes=[pltpu.SemaphoreType.DMA((2,))],
+            scratch_shapes=[pltpu.VMEM(pair_mask.shape, jnp.int32), pltpu.SemaphoreType.DMA((2,))],
             compiler_params=pltpu.CompilerParams(vmem_limit_bytes=32 << 20),
             name="ready",
         )(placed(pair_mask, pltpu.HBM), placed(lag_basis, pltpu.HBM), placed(mine, pltpu.VMEM))
-        inputs = [placed(x, pltpu.VMEM) for x in (spread, *(came[name] for name in soon))]
-        early = pl.pallas_call(
-            lambda *refs: early_kernel(per, seg, *refs),
-            out_shape=pltpu.VMEM((len(soon) * per * 8, WIDE), F32),
+        inputs = [placed(x, pltpu.VMEM) for x in (basis, spread, first, *(came[name] for name in soon))]
+        series = pl.pallas_call(
+            lambda *refs: early_kernel(per, seg, grps, tiles, soon, *refs),
+            out_shape=pltpu.VMEM((rows, LAGS), F32),
             in_specs=[vmem] * len(inputs),
             out_specs=vmem,
+            scratch_shapes=[pltpu.VMEM((rows, WIDE), F32)],
             compiler_params=pltpu.CompilerParams(vmem_limit_bytes=32 << 20),
             name="early",
         )(*inputs)
-        order = len(soon), soon + late
-        inputs = [mask, basis, spread, first, early, *(came[name] for name in late)]
+        inputs = [placed(x, pltpu.VMEM) for x in (basis, keep, spread, series, *(came[name] for name in late))]
         return pl.pallas_call(
-            lambda *refs: lags_kernel(per, seg, grps, tiles, order, *refs),
+            lambda *refs: lags_kernel(per, seg, grps, tiles, late, *refs),
             out_shape=jax.ShapeDtypeStruct((per, columns, LAGS), BF16),
             in_specs=[vmem] * len(inputs),
             out_specs=hbm,
             scratch_shapes=[
-                pltpu.VMEM((per * columns, WIDE), F32),
                 pltpu.VMEM((per, columns, LAGS), BF16),
                 pltpu.SemaphoreType.DMA((pl.cdiv(LAGS, LAG_STEP),)),
             ],
             compiler_params=pltpu.CompilerParams(vmem_limit_bytes=32 << 20),
             name="lags",
-        )(*[placed(x, pltpu.VMEM) for x in inputs])
+        )(*inputs)
 
     return jax.shard_map(
         on_device,

time: 12.7 us -> 12.5 us (0.984)
  Pallas kernels: 5.87 us -> 5.73 us
    pallas_call x1, Pallas kernels: 1.91 us -> 1.63 us  [on_device(): pl.pallas_call(lambda *refs: ready_kernel(per, seg, *refs), out_shape=(pl...]
    pallas_call x2, Pallas kernels: 1.84 us -> 1.98 us  [the longest x1 1.3 us: on_device(): pl.pallas_call(lambda *refs: lags_kernel(per, seg, grps, tiles, late, *re...]
  transfers between devices with their start and end apart: 5 -> 5, of which waited for: 1 -> 1; matrix products, arithmetic and copies ran while one was open for 0% -> 0% of each run, Pallas kernels for 18% -> 19%
where the time goes in v5:
time: 12.5 us; the launch traced here: 12.3 us
  Pallas kernels  5.73 us (46%)
  starting transfers between devices  5.72 us (46%)
  waiting for transfers between devices  0.77 us (6%)
    ppermute x5, starting transfers between devices, exchange(): return lax.ppermute(array, axes, pairs)  5.72 us
    pallas_call x1, Pallas kernels, on_device(): pl.pallas_call(lambda *refs: spectra_kernel(per, seg, samples, [way for w...  2.12 us
    pallas_call x1, Pallas kernels, on_device(): pl.pallas_call(lambda *refs: ready_kernel(per, seg, *refs), out_shape=(pl...  1.63 us
    pallas_call x1, Pallas kernels, on_device(): pl.pallas_call(lambda *refs: lags_kernel(per, seg, grps, tiles, late, *re...  1.3 us
    ppermute x5, waiting for transfers between devices, exchange(): return lax.ppermute(array, axes, pairs)  0.77 us
    pallas_call x1, Pallas kernels, on_device(): pl.pallas_call(lambda *refs: early_kernel(per, seg, grps, tiles, soon, *r...  0.68 us
  transfers between devices with their start and end apart: 5, of which 1 were waited for; matrix products, arithmetic and copies ran while one was open for 0% of the time, Pallas kernels for 19%

profile of v5, /device:TPU:0, one launch (start us, length us, event | category | flops | bytes accessed | tf_op | source)
XLA Modules:
  0.0 12.3 jit_solution(10351822267474977609)
XLA Ops:
  0.0 2.1 %spectra.1 = (bf16[64,384]{1,0:T(8,128)(2,1)S(1)}, bf16[64,384]{1,0:T(8,128)(2,1)S(1)}, bf16[64,384]{1,0:T(8,128)(2,1)S(1)}, bf16[64,384]{1,0:T(8,128)(2,1)S(1)}...) custom-call(s32[1,2,4]{2,1,0:T(2,128)} %refs_0_.2, s32[1,2]{1,0:T(1,128)} %refs_1_.2, s32[4,16]{1,0:T(4,128)} %refs_2_.1, ...), custom_call_target="tpu_custom_call" | custom-call | tf_op jit(solution)/shard_map/spectra/pallas_call | solution.py:332
  2.1 3.0 %collective-permute-start = (bf16[64,384]{1,0:T(8,128)(2,1)S(1)}, bf16[64,384]{1,0:T(8,128)(2,1)S(1)}, u32[]{:S(2)}, u32[]{:S(2)}) collective-permute-start(bf16[64,384]{1,0:T(8,128)(2,1)S(1)} %get-tuple-element.20), channel_id=1, source_target_pairs={{0,1},{1,0},{2,5},{3,4},{4,3},{5,2},{6,9},{7,8},{8,7},{9,6},{10,13... | collective-permute-start | bytes 147464 | tf_op jit(solution)/shard_map/ppermute | solution.py:318
  5.2 0.1 collective-permute-start.1
  5.2 1.2 %collective-permute-start.2 = (bf16[64,384]{1,0:T(8,128)(2,1)S(1)}, bf16[64,384]{1,0:T(8,128)(2,1)S(1)}, u32[]{:S(2)}, u32[]{:S(2)}) collective-permute-start(bf16[64,384]{1,0:T(8,128)(2,1)S(1)} %get-tuple-element.22), channel_id=1, source_target_pairs={{0,3},{1,2},{2,1},{3,0},{4,7},{5,6},{6,5},{7,4},{8,11},{9,10},{10,... | collective-permute-start | bytes 147464 | tf_op jit(solution)/shard_map/ppermute | solution.py:318
  6.5 1.4 %collective-permute-start.3 = (bf16[64,384]{1,0:T(8,128)(2,1)S(1)}, bf16[64,384]{1,0:T(8,128)(2,1)S(1)}, u32[]{:S(2)}, u32[]{:S(2)}) collective-permute-start(bf16[64,384]{1,0:T(8,128)(2,1)S(1)} %get-tuple-element.23), channel_id=1, source_target_pairs={{0,1},{1,0},{2,3},{3,2},{4,5},{5,4},{6,7},{7,6},{8,9},{9,8},{10,11... | collective-permute-start | bytes 147464 | tf_op jit(solution)/shard_map/ppermute | solution.py:318
  7.8 0.0 collective-permute-start.4
  7.8 1.6 %ready.1 = (bf16[384,2001]{1,0:T(8,128)(2,1)S(1)}, f32[96,128]{1,0:T(8,128)S(1)}, f32[256,384]{1,0:T(8,128)S(1)}, f32[32,384]{1,0:T(8,128)S(1)}) custom-call(s32[4,24]{1,0:T(4,128)} %refs_0_.3, bf16[384,2001]{1,0:T(8,128)(2,1)} %constant.8.clone.refs_1_, bf16[64,384]{1,0:T(8,128)(2,1)S(1)} %get-tuple-element.15.refs_2_), custom_call_target="tpu_custom_call" | custom-call | tf_op jit(solution)/shard_map/ready/pallas_call | solution.py:351
  9.5 0.0 collective-permute-done.refs_3_
  9.5 0.0 collective-permute-done.1.refs_4_
  9.5 0.0 collective-permute-done.2.refs_5_
  9.5 0.7 %early.1.refs_3_ = f32[96,2001]{1,0:T(8,128)S(1)} custom-call(bf16[384,2001]{1,0:T(8,128)(2,1)S(1)} %get-tuple-element.16.refs_0_, f32[256,384]{1,0:T(8,128)S(1)} %get-tuple-element.18.refs_1_.refs_2_, f32[32,384]{1,0:T(8,128)S(1)} %get-tuple-element.19.refs_2_, bf16[64,384]{1,0:T(8,128)(2,1)S(1)} %collective-permute-done.refs_3_, ...), custom_call_target="tpu_custom_call" | custom-call | tf_op jit(solution)/shard_map/early/pallas_call | solution.py:366
  10.2 0.8 %collective-permute-done.3.refs_4_ = bf16[64,384]{1,0:T(8,128)(2,1)S(1)} collective-permute-done((bf16[64,384]{1,0:T(8,128)(2,1)S(1)}, bf16[64,384]{1,0:T(8,128)(2,1)S(1)}, u32[]{:S(2)}, u32[]{:S(2)}) %collective-permute-start.3) | collective-permute-done | bytes 49184 | tf_op jit(solution)/shard_map/ppermute | solution.py:318
  11.0 0.0 collective-permute-done.4.refs_5_
  11.0 1.3 %lags.1 = bf16[4,24,2001]{2,1,0:T(8,128)(2,1)} custom-call(bf16[384,2001]{1,0:T(8,128)(2,1)S(1)} %get-tuple-element.16.refs_0_, f32[96,128]{1,0:T(8,128)S(1)} %get-tuple-element.17.refs_1_, f32[256,384]{1,0:T(8,128)S(1)} %get-tuple-element.18.refs_1_.refs_2_, f32[96,2001]{1,0:T(8,128)S(1)} %early.1.refs_3_, ...), custom_call_target="tpu_custom_call" | custom-call | tf_op jit(solution)/shard_map/lags/pallas_call | solution.py:376
Async XLA Ops:
  2.1 7.4 %collective-permute-start = (bf16[64,384]{1,0:T(8,128)(2,1)S(1)}, bf16[64,384]{1,0:T(8,128)(2,1)S(1)}, u32[]{:S(2)}, u32[]{:S(2)}) collective-permute-start(bf16[64,384]{1,0:T(8,128)(2,1)S(1)} %get-tuple-element.20), channel_id=1, source_target_pairs={{0,1},{1,0},{2,5},{3,4},{4,3},{5,2},{6,9},{7,8},{8,7},{9,6},{10,13... | collective-permute-start | bytes 147464 | tf_op jit(solution)/shard_map/ppermute | solution.py:318
  5.2 4.3 %collective-permute-start.1 = (bf16[64,384]{1,0:T(8,128)(2,1)S(1)}, bf16[64,384]{1,0:T(8,128)(2,1)S(1)}, u32[]{:S(2)}, u32[]{:S(2)}) collective-permute-start(bf16[64,384]{1,0:T(8,128)(2,1)S(1)} %get-tuple-element.21), channel_id=1, source_target_pairs={{0,1},{1,0},{2,4},{3,5},{4,2},{5,3},{6,8},{7,9},{8,6},{9,7},{10,12... | collective-permute-start | bytes 147464 | tf_op jit(solution)/shard_map/ppermute | solution.py:318
  5.2 4.3 %collective-permute-start.2 = (bf16[64,384]{1,0:T(8,128)(2,1)S(1)}, bf16[64,384]{1,0:T(8,128)(2,1)S(1)}, u32[]{:S(2)}, u32[]{:S(2)}) collective-permute-start(bf16[64,384]{1,0:T(8,128)(2,1)S(1)} %get-tuple-element.22), channel_id=1, source_target_pairs={{0,3},{1,2},{2,1},{3,0},{4,7},{5,6},{6,5},{7,4},{8,11},{9,10},{10,... | collective-permute-start | bytes 147464 | tf_op jit(solution)/shard_map/ppermute | solution.py:318
  6.5 4.5 %collective-permute-start.3 = (bf16[64,384]{1,0:T(8,128)(2,1)S(1)}, bf16[64,384]{1,0:T(8,128)(2,1)S(1)}, u32[]{:S(2)}, u32[]{:S(2)}) collective-permute-start(bf16[64,384]{1,0:T(8,128)(2,1)S(1)} %get-tuple-element.23), channel_id=1, source_target_pairs={{0,1},{1,0},{2,3},{3,2},{4,5},{5,4},{6,7},{7,6},{8,9},{9,8},{10,11... | collective-permute-start | bytes 147464 | tf_op jit(solution)/shard_map/ppermute | solution.py:318
  7.8 3.1 %collective-permute-start.4 = (bf16[64,384]{1,0:T(8,128)(2,1)S(1)}, bf16[64,384]{1,0:T(8,128)(2,1)S(1)}, u32[]{:S(2)}, u32[]{:S(2)}) collective-permute-start(bf16[64,384]{1,0:T(8,128)(2,1)S(1)} %get-tuple-element.24), channel_id=1, source_target_pairs={{0,2},{1,3},{2,0},{3,1},{4,6},{5,7},{6,4},{7,5},{8,10},{9,11},{10,... | collective-permute-start | bytes 147464 | tf_op jit(solution)/shard_map/ppermute | solution.py:318

commit v6 on v5

--- a/solution.py
+++ b/solution.py
@@ -19,6 +19,7 @@
 WIDE = 3 * LANE
 LAG_STEP = 4 * LANE
 STEP = 2 * LANE
+FINE = 16
 F32 = jnp.float32
 BF16 = jnp.bfloat16
 
@@ -41,16 +42,31 @@
 def fourier_tables(samples):
     bins = np.arange(1, NBIN + 1)
     turn = np.pi / samples
-    angle = np.mod(np.arange(STEP)[:, None] * bins[None, :], 2 * samples) * turn
-    high, low = split(in_lanes(np.cos(angle), -np.sin(angle)))
     stretches = -(-samples // STEP)
-    angle = np.mod(np.arange(stretches)[:, None] * STEP * bins[None, :], 2 * samples) * turn
-    turns = np.stack([in_lanes(np.cos(angle), np.cos(angle)), in_lanes(np.sin(angle), -np.sin(angle))])
+
+    def angles(number):
+        return np.mod(number[:, None] * bins[None, :], 2 * samples) * turn
+
+    whole = angles(np.arange(stretches) * STEP)
+    coarse = angles(np.arange(STEP // FINE) * FINE)
+    fine = angles(np.arange(FINE))
     number = np.arange(stretches * STEP)
     taper = np.where(number < samples, 0.5 - 0.5 * np.cos(number * (2.0 * np.pi / samples)), 0.0)
-    rows = np.concatenate([taper.reshape(stretches, STEP), np.zeros((stretches, WIDE - STEP))], axis=1)
-    factors = np.concatenate([rows[None], turns]).astype(np.float32)
-    return np.concatenate([high, high, low]), factors
+    parts = [
+        in_lanes(np.cos(whole), np.cos(whole)),
+        in_lanes(np.sin(whole), -np.sin(whole)),
+        np.pad(taper.reshape(stretches, STEP), ((0, 0), (0, WIDE - STEP))),
+        in_lanes(np.cos(coarse), -np.sin(coarse)),
+        in_lanes(-np.sin(coarse), -np.cos(coarse)),
+        in_lanes(np.cos(fine), np.cos(fine)),
+        in_lanes(np.sin(fine), np.sin(fine)),
+    ]
+    starts, rows = [], 0
+    for i, part in enumerate(parts):
+        parts[i] = np.pad(part, ((0, -len(part) % 8), (0, 0)))
+        starts.append(rows)
+        rows += len(parts[i])
+    return np.concatenate(parts).astype(np.float32), starts, stretches
 
 
 def lag_table(samples):
@@ -58,7 +74,18 @@
     bins = np.arange(1, NBIN + 1)
     angle = np.mod(lags[:, None] * bins[None, :], 2 * samples) * (np.pi / samples)
     scale = 1.0 / np.sqrt(NBIN)
-    return in_lanes(scale * np.cos(angle), -scale * np.sin(angle)).T.astype(ml_dtypes.bfloat16)
+    high, low = split(in_lanes(scale * np.cos(angle), -scale * np.sin(angle)).T)
+    lane = np.arange(LANE)
+    tail = np.where(holds_tail(lane)[:, None], high[2 * LANE :], low[LANE : 2 * LANE])
+    return np.concatenate([high[: 2 * LANE], tail])
+
+
+def holds_tail(lane):
+    return ((lane & (HALF - 1)) < TAIL) | (lane == VALID)
+
+
+def packed(real, imag, tail):
+    return jnp.concatenate([real, imag, jnp.where(holds_tail(iota(tail.shape, 1)), tail, imag)], axis=1)
 
 
 def iota(shape, dim):
@@ -81,13 +108,13 @@
 
 
 def spectra_kernel(
-    per, seg, samples, ways, rows_hbm, count_hbm, valid_hbm, traces_hbm, table_hbm, factors_hbm,
+    per, seg, samples, ways, starts, stretches, rows_hbm, count_hbm, valid_hbm, traces_hbm, factors_hbm,
     *refs,
 ):
-    mine_ref, *outs, rows_ref, count_ref, valid_ref, traces, table, factors, sems = refs
+    mine_ref, *outs, rows_ref, count_ref, valid_ref, traces, factors, white_ref, order_ref, sems = refs
     lines = per * seg
     pairs = [
-        (traces_hbm, traces), (table_hbm, table), (factors_hbm, factors),
+        (factors_hbm, factors), (traces_hbm, traces),
         (rows_hbm, rows_ref), (count_hbm, count_ref), (valid_hbm, valid_ref),
     ]
     copies = [pltpu.make_async_copy(src, dst, sems.at[i]) for i, (src, dst) in enumerate(pairs)]
@@ -108,46 +135,38 @@
     near_bins = jnp.abs(bin_in - bin_out) <= 4
     window = jnp.where(known_in & known_out, jnp.where(near_bins, 17.0, 1.0), 0.0).astype(BF16)
 
-    target = iota((lines, lines), 0)
-    source = iota((lines, lines), 1)
-    part, slot = divided(target, per)
-    for copy in copies[-3:]:
+    for copy in copies[2:]:
         copy.wait()
-
-    def choice(station):
-        return jnp.where(source == station * seg + part, 1.0, 0.0).astype(BF16)
-
-    def listed(direction):
-        station = jnp.full((lines, lines), -seg, jnp.int32)
-        for j in range(per):
-            live = j < count_ref[0, direction]
-            pick = jnp.where(live, rows_ref[0, direction, j], -seg)
-            station = jnp.where(slot == j, pick, station)
-        return choice(station)
-
-    picks = jnp.concatenate([choice(slot), listed(odd), listed(1 - odd)], axis=0)
-
     usable = jnp.concatenate(column_of(valid_ref[...].astype(F32)), axis=0)
 
-    for copy in copies[:3]:
-        copy.wait()
-    stretches = factors.shape[1]
+    copies[0].wait()
+    turn_at, swap_at, taper_at, coarse_at, cross_at, fine_at, other_at = starts
+    fine, other = factors[fine_at : fine_at + FINE, :], factors[other_at : other_at + FINE, :]
+    high, low = [], []
+    for i in range(STEP // FINE):
+        rows = factors[coarse_at + i : coarse_at + i + 1, :] * fine
+        rows = rows + factors[cross_at + i : cross_at + i + 1, :] * other
+        high.append(rows.astype(BF16))
+        low.append((rows - high[-1].astype(F32)).astype(BF16))
+    table = jnp.concatenate([*high, *high, *low], axis=0)
+
+    copies[1].wait()
     left = []
     for j in range(stretches):
         at = j * STEP
         x = traces[:, at : min(at + STEP, samples)]
         if at + STEP > samples:
             x = jnp.concatenate([x, jnp.zeros((lines, at + STEP - samples), F32)], axis=1)
-        x = x * factors[0, j : j + 1, :STEP]
+        x = x * factors[taper_at + j : taper_at + j + 1, :STEP]
         x_high = x.astype(BF16)
         x_low = (x - x_high.astype(F32)).astype(BF16)
         left.append(jnp.concatenate([x_high, x_low, x_high], axis=1))
-    parts = jnp.dot(jnp.concatenate(left, axis=0), table[...], preferred_element_type=F32)
+    parts = jnp.dot(jnp.concatenate(left, axis=0), table, preferred_element_type=F32)
     real, imag, tail = (parts[:lines, k * LANE : (k + 1) * LANE] for k in range(3))
     for j in range(1, stretches):
         p_re, p_im, p_tail = (parts[j * lines : (j + 1) * lines, k * LANE : (k + 1) * LANE] for k in range(3))
-        turn = factors[1, j : j + 1, :]
-        swap = factors[2, j : j + 1, :]
+        turn = factors[turn_at + j : turn_at + j + 1, :]
+        swap = factors[swap_at + j : swap_at + j + 1, :]
         real = real + p_re * turn[:, :LANE] + p_im * swap[:, :LANE]
         imag = imag + p_im * turn[:, LANE : 2 * LANE] + p_re * swap[:, LANE : 2 * LANE]
         tail = tail + p_tail * turn[:, 2 * LANE :] + pltpu.roll(p_tail, HALF, 1) * swap[:, 2 * LANE :]
@@ -161,10 +180,23 @@
     tail = tail * factor[:, LANE:]
     tail = jnp.where(iota((lines, LANE), 1) == VALID, usable, tail)
     white = jnp.concatenate([real * factor[:, :LANE], imag * factor[:, :LANE], tail], axis=1)
-    chosen = jnp.dot(picks, white.astype(BF16), preferred_element_type=F32).astype(BF16)
-    mine_ref[...] = chosen[:lines]
+    white_ref[...] = white.reshape(per, seg, WIDE)
+
+    def ordered(direction):
+        for j in range(per):
+            if direction is None:
+                rows = white_ref[j]
+            else:
+                rows = white_ref[rows_ref[0, direction, j]]
+                rows = jnp.where(j < count_ref[0, direction], rows, 0.0)
+            for k in range(3):
+                order_ref[k, pl.ds(j, seg, stride=per), :] = rows[:, k * LANE : (k + 1) * LANE]
+        return jnp.concatenate([order_ref[k] for k in range(3)], axis=1).astype(BF16)
+
+    own, near, far = ordered(None), ordered(odd), ordered(1 - odd)
+    mine_ref[...] = own
     for ref, way in zip(outs, ways):
-        ref[...] = chosen[way * lines : (way + 1) * lines]
+        ref[...] = (own, near, far)[way]
 
 
 def stacked(per, lines, spread, ref):
@@ -241,16 +273,17 @@
 
 def over_count(rows):
     scale = 1.0 / jnp.maximum(rows[2][:, VALID : VALID + 1], 1.0)
-    return jnp.concatenate([row * scale for row in rows], axis=1).astype(BF16)
+    return packed(*(row * scale for row in rows)).astype(BF16)
 
 
 def early_kernel(per, seg, grps, tiles, names, basis_ref, spread_ref, mine_ref, *refs):
-    series_ref, left = refs[-2:]
+    series_ref = refs[-1]
     sums = [load_sums(per, mine_ref, 0)]
-    sums += [stacked(per, per * seg, spread_ref, ref) for ref in refs[:-2]]
+    sums += [stacked(per, per * seg, spread_ref, ref) for ref in refs[:-1]]
     places = [place_of(name, grps, tiles) for name in ((0, 0), *names)]
     half = iota((8, LANE), 0) >> 2
     blocks = 3 * grps // 2
+    left = [None] * (per * blocks)
     for b in range(blocks):
         fits = []
         for place, there in places:
@@ -261,10 +294,8 @@
             for fit, piece in zip(fits, sums):
                 rows = [jnp.where(fit, new, row) for new, row in zip(piece[s], rows)]
             at = (s * blocks + b) * 8
-            scale = 1.0 / jnp.maximum(rows[2][:, VALID : VALID + 1], 1.0)
-            for k in range(3):
-                left[at : at + 8, k * LANE : (k + 1) * LANE] = rows[k] * scale
-    series_ref[...] = jnp.dot(left[...].astype(BF16), basis_ref[...], preferred_element_type=F32)
+            left[at // 8] = over_count(rows)
+    series_ref[...] = jnp.dot(jnp.concatenate(left, axis=0), basis_ref[...], preferred_element_type=F32)
 
 
 def lags_kernel(per, seg, grps, tiles, names, basis_ref, keep_ref, spread_ref, series_ref, *refs):
@@ -321,16 +352,18 @@
         per, seg, samples = traces.shape
         lines = per * seg
         columns = pair_mask.shape[1]
-        table, factors = map(jnp.asarray, fourier_tables(samples))
+        factors, starts, stretches = fourier_tables(samples)
         lag_basis = jnp.asarray(lag_table(samples))
         payload = pltpu.VMEM((lines, WIDE), BF16)
         names = [(2, d) for d in reversed(range(grps))]
         names += [(1, d) for d in range(1, grps)] + [(0, d) for d in range(1, grps)] + [(1, 0)]
         soon = [name for name in names if name not in LAST]
         late = [name for name in names if name in LAST]
-        inputs = [boundary_rows, boundary_count, validity, traces.reshape(lines, samples), table, factors]
+        inputs = [boundary_rows, boundary_count, validity, traces.reshape(lines, samples), jnp.asarray(factors)]
         mine, *rest = pl.pallas_call(
-            lambda *refs: spectra_kernel(per, seg, samples, [way for way, _ in names], *refs),
+            lambda *refs: spectra_kernel(
+                per, seg, samples, [way for way, _ in names], starts, stretches, *refs
+            ),
             out_shape=(payload,) * (1 + len(names)),
             in_specs=[hbm] * len(inputs),
             out_specs=(vmem,) * (1 + len(names)),
@@ -339,9 +372,10 @@
                 pltpu.SMEM(boundary_count.shape, jnp.int32),
                 pltpu.VMEM(validity.shape, jnp.int32),
                 pltpu.VMEM((lines, samples), F32),
-                pltpu.VMEM(table.shape, BF16),
                 pltpu.VMEM(factors.shape, F32),
-                pltpu.SemaphoreType.DMA((6,)),
+                pltpu.VMEM((per, seg, WIDE), F32),
+                pltpu.VMEM((3, lines, LANE), F32),
+                pltpu.SemaphoreType.DMA((5,)),
             ],
             compiler_params=pltpu.CompilerParams(vmem_limit_bytes=32 << 20),
             name="spectra",
@@ -368,7 +402,6 @@
             out_shape=pltpu.VMEM((rows, LAGS), F32),
             in_specs=[vmem] * len(inputs),
             out_specs=vmem,
-            scratch_shapes=[pltpu.VMEM((rows, WIDE), F32)],
             compiler_params=pltpu.CompilerParams(vmem_limit_bytes=32 << 20),
             name="early",
         )(*inputs)

time: 12.5 us -> 12.2 us (0.976)
  Pallas kernels: 5.73 us -> 5.5 us
    pallas_call x1, Pallas kernels: 2.12 us -> 1.88 us  [on_device(): pl.pallas_call(lambda *refs: spectra_kernel(per, seg, samples, [way for w...]
where the time goes in v6:
time: 12.2 us; the launch traced here: 12 us
  starting transfers between devices  5.71 us (47%)
  Pallas kernels  5.5 us (45%)
  waiting for transfers between devices  0.77 us (6%)
    ppermute x5, starting transfers between devices, exchange(): return lax.ppermute(array, axes, pairs)  5.71 us
    pallas_call x1, Pallas kernels, on_device(): pl.pallas_call(lambda *refs: spectra_kernel(per, seg, samples, [way for w...  1.88 us
    pallas_call x1, Pallas kernels, on_device(): pl.pallas_call(lambda *refs: ready_kernel(per, seg, *refs), out_shape=(pl...  1.63 us
    pallas_call x1, Pallas kernels, on_device(): pl.pallas_call(lambda *refs: lags_kernel(per, seg, grps, tiles, late, *re...  1.31 us
    ppermute x5, waiting for transfers between devices, exchange(): return lax.ppermute(array, axes, pairs)  0.77 us
    pallas_call x1, Pallas kernels, on_device(): pl.pallas_call(lambda *refs: early_kernel(per, seg, grps, tiles, soon, *r...  0.69 us
  transfers between devices with their start and end apart: 5, of which 1 were waited for; matrix products, arithmetic and copies ran while one was open for 0% of the time, Pallas kernels for 19%

profile of v6, /device:TPU:0, one launch (start us, length us, event | category | flops | bytes accessed | tf_op | source)
XLA Modules:
  0.0 12.0 jit_solution(626207534413016604)
XLA Ops:
  0.0 1.9 %spectra.1 = (bf16[64,384]{1,0:T(8,128)(2,1)S(1)}, bf16[64,384]{1,0:T(8,128)(2,1)S(1)}, bf16[64,384]{1,0:T(8,128)(2,1)S(1)}, bf16[64,384]{1,0:T(8,128)(2,1)S(1)}...) custom-call(s32[1,2,4]{2,1,0:T(2,128)} %refs_0_.2, s32[1,2]{1,0:T(1,128)} %refs_1_.2, s32[4,16]{1,0:T(4,128)} %refs_2_.1, ...), custom_call_target="tpu_custom_call" | custom-call | tf_op jit(solution)/shard_map/spectra/pallas_call | solution.py:363
  1.9 3.0 %collective-permute-start = (bf16[64,384]{1,0:T(8,128)(2,1)S(1)}, bf16[64,384]{1,0:T(8,128)(2,1)S(1)}, u32[]{:S(2)}, u32[]{:S(2)}) collective-permute-start(bf16[64,384]{1,0:T(8,128)(2,1)S(1)} %get-tuple-element.20), channel_id=1, source_target_pairs={{0,1},{1,0},{2,5},{3,4},{4,3},{5,2},{6,9},{7,8},{8,7},{9,6},{10,13... | collective-permute-start | bytes 147464 | tf_op jit(solution)/shard_map/ppermute | solution.py:349
  4.9 0.1 collective-permute-start.1
  5.0 1.2 %collective-permute-start.2 = (bf16[64,384]{1,0:T(8,128)(2,1)S(1)}, bf16[64,384]{1,0:T(8,128)(2,1)S(1)}, u32[]{:S(2)}, u32[]{:S(2)}) collective-permute-start(bf16[64,384]{1,0:T(8,128)(2,1)S(1)} %get-tuple-element.22), channel_id=1, source_target_pairs={{0,3},{1,2},{2,1},{3,0},{4,7},{5,6},{6,5},{7,4},{8,11},{9,10},{10,... | collective-permute-start | bytes 147464 | tf_op jit(solution)/shard_map/ppermute | solution.py:349
  6.2 1.4 %collective-permute-start.3 = (bf16[64,384]{1,0:T(8,128)(2,1)S(1)}, bf16[64,384]{1,0:T(8,128)(2,1)S(1)}, u32[]{:S(2)}, u32[]{:S(2)}) collective-permute-start(bf16[64,384]{1,0:T(8,128)(2,1)S(1)} %get-tuple-element.23), channel_id=1, source_target_pairs={{0,1},{1,0},{2,3},{3,2},{4,5},{5,4},{6,7},{7,6},{8,9},{9,8},{10,11... | collective-permute-start | bytes 147464 | tf_op jit(solution)/shard_map/ppermute | solution.py:349
  7.6 0.0 collective-permute-start.4
  7.6 1.6 %ready.1 = (bf16[384,2001]{1,0:T(8,128)(2,1)S(1)}, f32[96,128]{1,0:T(8,128)S(1)}, f32[256,384]{1,0:T(8,128)S(1)}, f32[32,384]{1,0:T(8,128)S(1)}) custom-call(s32[4,24]{1,0:T(4,128)} %refs_0_.3, bf16[384,2001]{1,0:T(8,128)(2,1)} %constant.4.clone.refs_1_, bf16[64,384]{1,0:T(8,128)(2,1)S(1)} %get-tuple-element.15.refs_2_), custom_call_target="tpu_custom_call" | custom-call | tf_op jit(solution)/shard_map/ready/pallas_call | solution.py:385
  9.2 0.0 collective-permute-done.refs_3_
  9.2 0.0 collective-permute-done.1.refs_4_
  9.3 0.0 collective-permute-done.2.refs_5_
  9.3 0.7 %early.1.refs_3_ = f32[96,2001]{1,0:T(8,128)S(1)} custom-call(bf16[384,2001]{1,0:T(8,128)(2,1)S(1)} %get-tuple-element.16.refs_0_, f32[256,384]{1,0:T(8,128)S(1)} %get-tuple-element.18.refs_1_.refs_2_, f32[32,384]{1,0:T(8,128)S(1)} %get-tuple-element.19.refs_2_, bf16[64,384]{1,0:T(8,128)(2,1)S(1)} %collective-permute-done.refs_3_, ...), custom_call_target="tpu_custom_call" | custom-call | tf_op jit(solution)/shard_map/early/pallas_call | solution.py:400
  10.0 0.8 %collective-permute-done.3.refs_4_ = bf16[64,384]{1,0:T(8,128)(2,1)S(1)} collective-permute-done((bf16[64,384]{1,0:T(8,128)(2,1)S(1)}, bf16[64,384]{1,0:T(8,128)(2,1)S(1)}, u32[]{:S(2)}, u32[]{:S(2)}) %collective-permute-start.3) | collective-permute-done | bytes 49184 | tf_op jit(solution)/shard_map/ppermute | solution.py:349
  10.7 0.0 collective-permute-done.4.refs_5_
  10.7 1.3 %lags.1 = bf16[4,24,2001]{2,1,0:T(8,128)(2,1)} custom-call(bf16[384,2001]{1,0:T(8,128)(2,1)S(1)} %get-tuple-element.16.refs_0_, f32[96,128]{1,0:T(8,128)S(1)} %get-tuple-element.17.refs_1_, f32[256,384]{1,0:T(8,128)S(1)} %get-tuple-element.18.refs_1_.refs_2_, f32[96,2001]{1,0:T(8,128)S(1)} %early.1.refs_3_, ...), custom_call_target="tpu_custom_call" | custom-call | tf_op jit(solution)/shard_map/lags/pallas_call | solution.py:409
Async XLA Ops:
  1.9 7.3 %collective-permute-start = (bf16[64,384]{1,0:T(8,128)(2,1)S(1)}, bf16[64,384]{1,0:T(8,128)(2,1)S(1)}, u32[]{:S(2)}, u32[]{:S(2)}) collective-permute-start(bf16[64,384]{1,0:T(8,128)(2,1)S(1)} %get-tuple-element.20), channel_id=1, source_target_pairs={{0,1},{1,0},{2,5},{3,4},{4,3},{5,2},{6,9},{7,8},{8,7},{9,6},{10,13... | collective-permute-start | bytes 147464 | tf_op jit(solution)/shard_map/ppermute | solution.py:349
  4.9 4.3 %collective-permute-start.1 = (bf16[64,384]{1,0:T(8,128)(2,1)S(1)}, bf16[64,384]{1,0:T(8,128)(2,1)S(1)}, u32[]{:S(2)}, u32[]{:S(2)}) collective-permute-start(bf16[64,384]{1,0:T(8,128)(2,1)S(1)} %get-tuple-element.21), channel_id=1, source_target_pairs={{0,1},{1,0},{2,4},{3,5},{4,2},{5,3},{6,8},{7,9},{8,6},{9,7},{10,12... | collective-permute-start | bytes 147464 | tf_op jit(solution)/shard_map/ppermute | solution.py:349
  5.0 4.3 %collective-permute-start.2 = (bf16[64,384]{1,0:T(8,128)(2,1)S(1)}, bf16[64,384]{1,0:T(8,128)(2,1)S(1)}, u32[]{:S(2)}, u32[]{:S(2)}) collective-permute-start(bf16[64,384]{1,0:T(8,128)(2,1)S(1)} %get-tuple-element.22), channel_id=1, source_target_pairs={{0,3},{1,2},{2,1},{3,0},{4,7},{5,6},{6,5},{7,4},{8,11},{9,10},{10,... | collective-permute-start | bytes 147464 | tf_op jit(solution)/shard_map/ppermute | solution.py:349
  6.2 4.5 %collective-permute-start.3 = (bf16[64,384]{1,0:T(8,128)(2,1)S(1)}, bf16[64,384]{1,0:T(8,128)(2,1)S(1)}, u32[]{:S(2)}, u32[]{:S(2)}) collective-permute-start(bf16[64,384]{1,0:T(8,128)(2,1)S(1)} %get-tuple-element.23), channel_id=1, source_target_pairs={{0,1},{1,0},{2,3},{3,2},{4,5},{5,4},{6,7},{7,6},{8,9},{9,8},{10,11... | collective-permute-start | bytes 147464 | tf_op jit(solution)/shard_map/ppermute | solution.py:349
  7.6 3.1 %collective-permute-start.4 = (bf16[64,384]{1,0:T(8,128)(2,1)S(1)}, bf16[64,384]{1,0:T(8,128)(2,1)S(1)}, u32[]{:S(2)}, u32[]{:S(2)}) collective-permute-start(bf16[64,384]{1,0:T(8,128)(2,1)S(1)} %get-tuple-element.24), channel_id=1, source_target_pairs={{0,2},{1,3},{2,0},{3,1},{4,6},{5,7},{6,4},{7,5},{8,10},{9,11},{10,... | collective-permute-start | bytes 147464 | tf_op jit(solution)/shard_map/ppermute | solution.py:349

commit v7 on v6

--- a/solution.py
+++ b/solution.py
@@ -196,7 +196,7 @@
     own, near, far = ordered(None), ordered(odd), ordered(1 - odd)
     mine_ref[...] = own
     for ref, way in zip(outs, ways):
-        ref[...] = (own, near, far)[way]
+        ref[...] = (own, near, far, jnp.concatenate([own, near], axis=0))[way]
 
 
 def stacked(per, lines, spread, ref):
@@ -259,6 +259,12 @@
     keep = jnp.concatenate(column_of(mask_ref[...].astype(F32)), axis=0)
     keep_ref[...] = jnp.broadcast_to(keep, keep_ref.shape)
     copies[1].wait()
+
+
+def pass_kernel(lines, *refs):
+    half = len(refs) // 2
+    for src, dst in zip(refs[:half], refs[half:]):
+        dst[...] = src[lines:, :]
 
 
 def place_of(name, grps, tiles):
@@ -355,18 +361,19 @@
         factors, starts, stretches = fourier_tables(samples)
         lag_basis = jnp.asarray(lag_table(samples))
         payload = pltpu.VMEM((lines, WIDE), BF16)
-        names = [(2, d) for d in reversed(range(grps))]
-        names += [(1, d) for d in range(1, grps)] + [(0, d) for d in range(1, grps)] + [(1, 0)]
-        soon = [name for name in names if name not in LAST]
-        late = [name for name in names if name in LAST]
+        sent = [(3, d) for d in range(1, grps)] + [(1, 0)] + [(2, d) for d in reversed(range(grps))]
+        soon = [(0, d) for d in range(1, grps)] + [(1, 0)] + [(2, d) for d in range(1, grps)]
+        late = [(2, 0)] + [(1, d) for d in range(1, grps)]
         inputs = [boundary_rows, boundary_count, validity, traces.reshape(lines, samples), jnp.asarray(factors)]
         mine, *rest = pl.pallas_call(
             lambda *refs: spectra_kernel(
-                per, seg, samples, [way for way, _ in names], starts, stretches, *refs
+                per, seg, samples, [way for way, _ in sent], starts, stretches, *refs
             ),
-            out_shape=(payload,) * (1 + len(names)),
+            out_shape=(payload,) + tuple(
+                pltpu.VMEM(((1 + way // 3) * lines, WIDE), BF16) for way, _ in sent
+            ),
             in_specs=[hbm] * len(inputs),
-            out_specs=(vmem,) * (1 + len(names)),
+            out_specs=(vmem,) * (1 + len(sent)),
             scratch_shapes=[
                 pltpu.SMEM(boundary_rows.shape, jnp.int32),
                 pltpu.SMEM(boundary_count.shape, jnp.int32),
@@ -380,7 +387,7 @@
             compiler_params=pltpu.CompilerParams(vmem_limit_bytes=32 << 20),
             name="spectra",
         )(*[placed(x, pltpu.HBM) for x in inputs])
-        came = {name: exchange(array, *name) for name, array in zip(names, rest)}
+        came = {(way, by): exchange(array, way % 3, by) for (way, by), array in zip(sent, rest)}
         rows = per * columns
         basis, keep, spread, first = pl.pallas_call(
             lambda *refs: ready_kernel(per, seg, *refs),
@@ -396,6 +403,19 @@
             compiler_params=pltpu.CompilerParams(vmem_limit_bytes=32 << 20),
             name="ready",
         )(placed(pair_mask, pltpu.HBM), placed(lag_basis, pltpu.HBM), placed(mine, pltpu.VMEM))
+        both = [came[3, d] for d in range(1, grps)]
+        for d in range(1, grps):
+            came[0, d] = came[3, d]
+        if both:
+            passed = pl.pallas_call(
+                lambda _, *refs: pass_kernel(lines, *refs),
+                out_shape=(payload,) * len(both),
+                in_specs=[vmem] * (1 + len(both)),
+                out_specs=(vmem,) * len(both),
+                name="pass",
+            )(*[placed(x, pltpu.VMEM) for x in (first, *both)])
+            for d, array in enumerate(passed):
+                came[1, d + 1] = exchange(array, 1, 0)
         inputs = [placed(x, pltpu.VMEM) for x in (basis, spread, first, *(came[name] for name in soon))]
         series = pl.pallas_call(
             lambda *refs: early_kernel(per, seg, grps, tiles, soon, *refs),

time: 12.2 us -> 11.7 us (0.959)
  the two profiles are of different devices: /device:TPU:0 before, /device:TPU:3 now
where the time goes in v7:
time: 11.7 us; the launch traced here: 11.5 us
  Pallas kernels  5.49 us (47%)
  starting transfers between devices  4.93 us (42%)
  waiting for transfers between devices  0.98 us (8%)
    ppermute x5, starting transfers between devices, exchange(): return lax.ppermute(array, axes, pairs)  4.93 us
    pallas_call x1, Pallas kernels, on_device(): pl.pallas_call(lambda *refs: spectra_kernel(per, seg, samples, [way for w...  1.87 us
    pallas_call x1, Pallas kernels, on_device(): pl.pallas_call(lambda *refs: ready_kernel(per, seg, *refs), out_shape=(pl...  1.63 us
    pallas_call x1, Pallas kernels, on_device(): pl.pallas_call(lambda *refs: lags_kernel(per, seg, grps, tiles, late, *re...  1.3 us
    ppermute x5, waiting for transfers between devices, exchange(): return lax.ppermute(array, axes, pairs)  0.98 us
    pallas_call x1, Pallas kernels, on_device(): pl.pallas_call(lambda *refs: early_kernel(per, seg, grps, tiles, soon, *r...  0.68 us
  transfers between devices with their start and end apart: 5, of which 1 were waited for; matrix products, arithmetic and copies ran while one was open for 0% of the time, Pallas kernels for 20%

profile of v7, /device:TPU:3, one launch (start us, length us, event | category | flops | bytes accessed | tf_op | source)
XLA Modules:
  0.0 11.5 jit_solution(7601405659617092247)
XLA Ops:
  0.0 1.9 %spectra.1 = (bf16[64,384]{1,0:T(8,128)(2,1)S(1)}, bf16[128,384]{1,0:T(8,128)(2,1)S(1)}, bf16[64,384]{1,0:T(8,128)(2,1)S(1)}, bf16[64,384]{1,0:T(8,128)(2,1)S(1)}, bf16[64,384]{1,0:T(8,128)(2,1)S(1)}) custom-call(s32[1,2,4]{2,1,0:T(2,128)} %refs_0_.2, s32[1,2]{1,0:T(1,128)} %refs_1_.2, s32[4,16]{1,0:T(4,128)} %refs_2_.1, f32[64,1500]{1,0:T(8,128)} %bitcast.1, ...), custom_call_target="tpu_custom_call" | custom-call | tf_op jit(solution)/shard_map/spectra/pallas_call | solution.py:368
  1.9 1.3 %collective-permute-start = (bf16[128,384]{1,0:T(8,128)(2,1)S(1)}, bf16[128,384]{1,0:T(8,128)(2,1)S(1)}, u32[]{:S(2)}, u32[]{:S(2)}) collective-permute-start(bf16[128,384]{1,0:T(8,128)(2,1)S(1)} %get-tuple-element.19), channel_id=1, source_target_pairs={{0,1},{1,0},{2,3},{3,2},{4,5},{5,4},{6,7},{7,6},{8,9},{9,8},{10,11... | collective-permute-start | bytes 294920 | tf_op jit(solution)/shard_map/ppermute | solution.py:355
  3.2 1.0 %collective-permute-start.1 = (bf16[64,384]{1,0:T(8,128)(2,1)S(1)}, bf16[64,384]{1,0:T(8,128)(2,1)S(1)}, u32[]{:S(2)}, u32[]{:S(2)}) collective-permute-start(bf16[64,384]{1,0:T(8,128)(2,1)S(1)} %get-tuple-element.20), channel_id=1, source_target_pairs={{0,2},{1,3},{2,0},{3,1},{4,6},{5,7},{6,4},{7,5},{8,10},{9,11},{10,... | collective-permute-start | bytes 147464 | tf_op jit(solution)/shard_map/ppermute | solution.py:355
  4.1 1.1 %collective-permute-start.2 = (bf16[64,384]{1,0:T(8,128)(2,1)S(1)}, bf16[64,384]{1,0:T(8,128)(2,1)S(1)}, u32[]{:S(2)}, u32[]{:S(2)}) collective-permute-start(bf16[64,384]{1,0:T(8,128)(2,1)S(1)} %get-tuple-element.21), channel_id=1, source_target_pairs={{0,1},{1,0},{2,5},{3,4},{4,3},{5,2},{6,9},{7,8},{8,7},{9,6},{10,13... | collective-permute-start | bytes 147464 | tf_op jit(solution)/shard_map/ppermute | solution.py:355
  5.2 1.5 %collective-permute-start.3 = (bf16[64,384]{1,0:T(8,128)(2,1)S(1)}, bf16[64,384]{1,0:T(8,128)(2,1)S(1)}, u32[]{:S(2)}, u32[]{:S(2)}) collective-permute-start(bf16[64,384]{1,0:T(8,128)(2,1)S(1)} %get-tuple-element.22), channel_id=1, source_target_pairs={{0,1},{1,0},{2,4},{3,5},{4,2},{5,3},{6,8},{7,9},{8,6},{9,7},{10,12... | collective-permute-start | bytes 147464 | tf_op jit(solution)/shard_map/ppermute | solution.py:355
  6.7 1.6 %ready.1 = (bf16[384,2001]{1,0:T(8,128)(2,1)S(1)}, f32[96,128]{1,0:T(8,128)S(1)}, f32[256,384]{1,0:T(8,128)S(1)}, f32[32,384]{1,0:T(8,128)S(1)}) custom-call(s32[4,24]{1,0:T(4,128)} %refs_0_.3, bf16[384,2001]{1,0:T(8,128)(2,1)} %constant.4.clone.refs_1_, bf16[64,384]{1,0:T(8,128)(2,1)S(1)} %get-tuple-element.14.refs_2_), custom_call_target="tpu_custom_call" | custom-call | tf_op jit(solution)/shard_map/ready/pallas_call | solution.py:392
  8.4 0.0 collective-permute-done.refs_3_.refs_0_
  8.4 0.1 collective-permute-start.4
  8.5 0.0 collective-permute-done.1.refs_4_
  8.5 1.0 %collective-permute-done.2.refs_5_ = bf16[64,384]{1,0:T(8,128)(2,1)S(1)} collective-permute-done((bf16[64,384]{1,0:T(8,128)(2,1)S(1)}, bf16[64,384]{1,0:T(8,128)(2,1)S(1)}, u32[]{:S(2)}, u32[]{:S(2)}) %collective-permute-start.2) | collective-permute-done | bytes 49184 | tf_op jit(solution)/shard_map/ppermute | solution.py:355
  9.5 0.7 %early.1.refs_3_ = f32[96,2001]{1,0:T(8,128)S(1)} custom-call(bf16[384,2001]{1,0:T(8,128)(2,1)S(1)} %get-tuple-element.15.refs_0_, f32[256,384]{1,0:T(8,128)S(1)} %get-tuple-element.17.refs_1_.refs_2_, f32[32,384]{1,0:T(8,128)S(1)} %get-tuple-element.18.refs_2_._, bf16[128,384]{1,0:T(8,128)(2,1)S(1)} %collective-permute-done.refs_3_.refs_0_, ...), custom_call_target="tpu_custom_call" | custom-call | tf_op jit(solution)/shard_map/early/pallas_call | solution.py:420
  10.2 0.0 collective-permute-done.3.refs_4_
  10.2 0.0 collective-permute-done.4.refs_5_
  10.2 1.3 %lags.1 = bf16[4,24,2001]{2,1,0:T(8,128)(2,1)} custom-call(bf16[384,2001]{1,0:T(8,128)(2,1)S(1)} %get-tuple-element.15.refs_0_, f32[96,128]{1,0:T(8,128)S(1)} %get-tuple-element.16.refs_1_, f32[256,384]{1,0:T(8,128)S(1)} %get-tuple-element.17.refs_1_.refs_2_, f32[96,2001]{1,0:T(8,128)S(1)} %early.1.refs_3_, ...), custom_call_target="tpu_custom_call" | custom-call | tf_op jit(solution)/shard_map/lags/pallas_call | solution.py:429
  (1 shorter events, 0.0 us)
Async XLA Ops:
  1.9 6.5 %collective-permute-start = (bf16[128,384]{1,0:T(8,128)(2,1)S(1)}, bf16[128,384]{1,0:T(8,128)(2,1)S(1)}, u32[]{:S(2)}, u32[]{:S(2)}) collective-permute-start(bf16[128,384]{1,0:T(8,128)(2,1)S(1)} %get-tuple-element.19), channel_id=1, source_target_pairs={{0,1},{1,0},{2,3},{3,2},{4,5},{5,4},{6,7},{7,6},{8,9},{9,8},{10,11... | collective-permute-start | bytes 294920 | tf_op jit(solution)/shard_map/ppermute | solution.py:355
  3.2 5.3 %collective-permute-start.1 = (bf16[64,384]{1,0:T(8,128)(2,1)S(1)}, bf16[64,384]{1,0:T(8,128)(2,1)S(1)}, u32[]{:S(2)}, u32[]{:S(2)}) collective-permute-start(bf16[64,384]{1,0:T(8,128)(2,1)S(1)} %get-tuple-element.20), channel_id=1, source_target_pairs={{0,2},{1,3},{2,0},{3,1},{4,6},{5,7},{6,4},{7,5},{8,10},{9,11},{10,... | collective-permute-start | bytes 147464 | tf_op jit(solution)/shard_map/ppermute | solution.py:355
  4.1 5.3 %collective-permute-start.2 = (bf16[64,384]{1,0:T(8,128)(2,1)S(1)}, bf16[64,384]{1,0:T(8,128)(2,1)S(1)}, u32[]{:S(2)}, u32[]{:S(2)}) collective-permute-start(bf16[64,384]{1,0:T(8,128)(2,1)S(1)} %get-tuple-element.21), channel_id=1, source_target_pairs={{0,1},{1,0},{2,5},{3,4},{4,3},{5,2},{6,9},{7,8},{8,7},{9,6},{10,13... | collective-permute-start | bytes 147464 | tf_op jit(solution)/shard_map/ppermute | solution.py:355
  5.2 4.9 %collective-permute-start.3 = (bf16[64,384]{1,0:T(8,128)(2,1)S(1)}, bf16[64,384]{1,0:T(8,128)(2,1)S(1)}, u32[]{:S(2)}, u32[]{:S(2)}) collective-permute-start(bf16[64,384]{1,0:T(8,128)(2,1)S(1)} %get-tuple-element.22), channel_id=1, source_target_pairs={{0,1},{1,0},{2,4},{3,5},{4,2},{5,3},{6,8},{7,9},{8,6},{9,7},{10,12... | collective-permute-start | bytes 147464 | tf_op jit(solution)/shard_map/ppermute | solution.py:355
  8.4 1.8 %collective-permute-start.4 = (bf16[64,384]{1,0:T(8,128)(2,1)S(1)}, bf16[64,384]{1,0:T(8,128)(2,1)S(1)}, u32[]{:S(2)}, u32[]{:S(2)}) collective-permute-start(bf16[64,384]{1,0:T(8,128)(2,1)S(1)} %pass.1), channel_id=1, source_target_pairs={{0,2},{1,3},{2,0},{3,1},{4,6},{5,7},{6,4},{7,5},{8,10},{9,11},{10,... | collective-permute-start | bytes 147464 | tf_op jit(solution)/shard_map/ppermute | solution.py:355

commit v8 on v7

--- a/solution.py
+++ b/solution.py
@@ -108,14 +108,14 @@
 
 
 def spectra_kernel(
-    per, seg, samples, ways, starts, stretches, rows_hbm, count_hbm, valid_hbm, traces_hbm, factors_hbm,
+    per, seg, samples, ways, starts, stretches, rows_hbm, count_hbm, valid_hbm, traces_hbm, factors_hbm, basis_hbm,
     *refs,
 ):
-    mine_ref, *outs, rows_ref, count_ref, valid_ref, traces, factors, white_ref, order_ref, sems = refs
+    mine_ref, *outs, basis_ref, rows_ref, count_ref, valid_ref, traces, factors, white_ref, order_ref, sems = refs
     lines = per * seg
     pairs = [
         (factors_hbm, factors), (traces_hbm, traces),
-        (rows_hbm, rows_ref), (count_hbm, count_ref), (valid_hbm, valid_ref),
+        (rows_hbm, rows_ref), (count_hbm, count_ref), (valid_hbm, valid_ref), (basis_hbm, basis_ref),
     ]
     copies = [pltpu.make_async_copy(src, dst, sems.at[i]) for i, (src, dst) in enumerate(pairs)]
     for copy in copies:
@@ -135,7 +135,7 @@
     near_bins = jnp.abs(bin_in - bin_out) <= 4
     window = jnp.where(known_in & known_out, jnp.where(near_bins, 17.0, 1.0), 0.0).astype(BF16)
 
-    for copy in copies[2:]:
+    for copy in copies[2:5]:
         copy.wait()
     usable = jnp.concatenate(column_of(valid_ref[...].astype(F32)), axis=0)
 
@@ -197,10 +197,11 @@
     mine_ref[...] = own
     for ref, way in zip(outs, ways):
         ref[...] = (own, near, far, jnp.concatenate([own, near], axis=0))[way]
+    copies[5].wait()
 
 
 def stacked(per, lines, spread, ref):
-    sums = [[None] * 4 for _ in range(per)]
+    sums = [[None] * 5 for _ in range(per)]
 
     def add(s, i, value):
         sums[s][i] = value if sums[s][i] is None else sums[s][i] + value
@@ -211,21 +212,23 @@
             one = both[8 * half : 8 * half + 8]
             c_re, c_im, c_tail = one[:, :LANE], one[:, LANE : 2 * LANE], one[:, 2 * LANE :]
             c_turn = pltpu.roll(c_tail, HALF, 1)
+            c_valid = jnp.broadcast_to(c_tail[:, VALID : VALID + 1], c_tail.shape)
             for s in range(per):
                 here = s * lines + at + 8 * half
                 left = spread[here : here + 8, :]
-                l_re, l_im, l_tail = left[:, :LANE], left[:, LANE : 2 * LANE], left[:, 2 * LANE :]
+                l_re, l_im, l_tail, l_valid = (left[:, k * LANE : (k + 1) * LANE] for k in range(4))
                 add(s, 0, l_re * c_re + l_im * c_im)
                 add(s, 1, l_im * c_re - l_re * c_im)
                 add(s, 2, l_tail * c_tail)
                 add(s, 3, l_tail * c_turn)
+                add(s, 4, l_valid * c_valid)
     low_lanes = iota((8, LANE), 1) < HALF
     out = []
     for s in range(per):
         straight, turned = sums[s][2], sums[s][3]
         straight = straight + pltpu.roll(straight, HALF, 1)
         turned = turned - pltpu.roll(turned, HALF, 1)
-        all_lanes = [sums[s][0], sums[s][1], jnp.where(low_lanes, straight, turned)]
+        all_lanes = [sums[s][0], sums[s][1], jnp.where(low_lanes, straight, turned), sums[s][4]]
         out.append([v + pltpu.roll(v, 4, 0) for v in all_lanes])
     return out
 
@@ -233,19 +236,18 @@
 def store_sums(per, ref, i, pieces):
     for s, sums in enumerate(pieces):
         at = (i * per + s) * 8
-        for k in range(3):
+        for k in range(4):
             ref[at : at + 8, k * LANE : (k + 1) * LANE] = sums[k]
 
 
 def load_sums(per, ref, i):
     rows = [ref[(i * per + s) * 8 : (i * per + s) * 8 + 8, :] for s in range(per)]
-    return [[row[:, k * LANE : (k + 1) * LANE] for k in range(3)] for row in rows]
-
-
-def ready_kernel(per, seg, mask_hbm, basis_hbm, mine_ref, basis_ref, keep_ref, spread_ref, sums_ref, mask_ref, sems):
+    return [[row[:, k * LANE : (k + 1) * LANE] for k in range(4)] for row in rows]
+
+
+def ready_kernel(per, seg, mask_hbm, mine_ref, keep_ref, spread_ref, sums_ref, mask_ref, sems):
     copies = [
         pltpu.make_async_copy(mask_hbm, mask_ref, sems.at[0]),
-        pltpu.make_async_copy(basis_hbm, basis_ref, sems.at[1]),
     ]
     for copy in copies:
         copy.start()
@@ -253,12 +255,14 @@
     part, _ = divided(iota((lines, lines), 0), per)
     source = iota((lines, lines), 1)
     pick = [jnp.where(source == part * per + s, 1.0, 0.0).astype(BF16) for s in range(per)]
-    spread_ref[...] = jnp.dot(jnp.concatenate(pick, axis=0), mine_ref[...], preferred_element_type=F32)
+    spread = jnp.dot(jnp.concatenate(pick, axis=0), mine_ref[...], preferred_element_type=F32)
+    spread_ref[:, :WIDE] = spread
+    valid = spread[:, 2 * LANE + VALID : 2 * LANE + VALID + 1]
+    spread_ref[:, WIDE:] = jnp.broadcast_to(valid, (per * lines, LANE))
     store_sums(per, sums_ref, 0, stacked(per, lines, spread_ref, mine_ref))
     copies[0].wait()
     keep = jnp.concatenate(column_of(mask_ref[...].astype(F32)), axis=0)
     keep_ref[...] = jnp.broadcast_to(keep, keep_ref.shape)
-    copies[1].wait()
 
 
 def pass_kernel(lines, *refs):
@@ -278,8 +282,8 @@
 
 
 def over_count(rows):
-    scale = 1.0 / jnp.maximum(rows[2][:, VALID : VALID + 1], 1.0)
-    return packed(*(row * scale for row in rows)).astype(BF16)
+    scale = 1.0 / jnp.maximum(rows[3], 1.0)
+    return packed(*(row * scale for row in rows[:3])).astype(BF16)
 
 
 def early_kernel(per, seg, grps, tiles, names, basis_ref, spread_ref, mine_ref, *refs):
@@ -296,7 +300,7 @@
             fit = (half + 2 * b) == place
             fits.append(fit if there is None else fit & there)
         for s in range(per):
-            rows = [jnp.zeros((8, LANE), F32)] * 3
+            rows = [jnp.zeros((8, LANE), F32)] * 4
             for fit, piece in zip(fits, sums):
                 rows = [jnp.where(fit, new, row) for new, row in zip(piece[s], rows)]
             at = (s * blocks + b) * 8
@@ -362,18 +366,18 @@
         lag_basis = jnp.asarray(lag_table(samples))
         payload = pltpu.VMEM((lines, WIDE), BF16)
         sent = [(3, d) for d in range(1, grps)] + [(1, 0)] + [(2, d) for d in reversed(range(grps))]
-        soon = [(0, d) for d in range(1, grps)] + [(1, 0)] + [(2, d) for d in range(1, grps)]
-        late = [(2, 0)] + [(1, d) for d in range(1, grps)]
-        inputs = [boundary_rows, boundary_count, validity, traces.reshape(lines, samples), jnp.asarray(factors)]
-        mine, *rest = pl.pallas_call(
+        soon = [(0, d) for d in range(1, grps)] + [(1, 0)]
+        late = [(2, d) for d in reversed(range(grps))] + [(1, d) for d in range(1, grps)]
+        inputs = [boundary_rows, boundary_count, validity, traces.reshape(lines, samples), jnp.asarray(factors), lag_basis]
+        mine, *rest, basis = pl.pallas_call(
             lambda *refs: spectra_kernel(
                 per, seg, samples, [way for way, _ in sent], starts, stretches, *refs
             ),
             out_shape=(payload,) + tuple(
                 pltpu.VMEM(((1 + way // 3) * lines, WIDE), BF16) for way, _ in sent
-            ),
+            ) + (pltpu.VMEM(lag_basis.shape, BF16),),
             in_specs=[hbm] * len(inputs),
-            out_specs=(vmem,) * (1 + len(sent)),
+            out_specs=(vmem,) * (2 + len(sent)),
             scratch_shapes=[
                 pltpu.SMEM(boundary_rows.shape, jnp.int32),
                 pltpu.SMEM(boundary_count.shape, jnp.int32),
@@ -382,27 +386,26 @@
                 pltpu.VMEM(factors.shape, F32),
                 pltpu.VMEM((per, seg, WIDE), F32),
                 pltpu.VMEM((3, lines, LANE), F32),
-                pltpu.SemaphoreType.DMA((5,)),
+                pltpu.SemaphoreType.DMA((6,)),
             ],
             compiler_params=pltpu.CompilerParams(vmem_limit_bytes=32 << 20),
             name="spectra",
         )(*[placed(x, pltpu.HBM) for x in inputs])
         came = {(way, by): exchange(array, way % 3, by) for (way, by), array in zip(sent, rest)}
         rows = per * columns
-        basis, keep, spread, first = pl.pallas_call(
+        keep, spread, first = pl.pallas_call(
             lambda *refs: ready_kernel(per, seg, *refs),
             out_shape=(
-                pltpu.VMEM(lag_basis.shape, BF16),
                 pltpu.VMEM((rows, LANE), F32),
-                pltpu.VMEM((per * lines, WIDE), F32),
-                pltpu.VMEM((per * 8, WIDE), F32),
+                pltpu.VMEM((per * lines, WIDE + LANE), F32),
+                pltpu.VMEM((per * 8, WIDE + LANE), F32),
             ),
-            in_specs=[hbm, hbm, vmem],
-            out_specs=(vmem,) * 4,
+            in_specs=[hbm, vmem],
+            out_specs=(vmem,) * 3,
             scratch_shapes=[pltpu.VMEM(pair_mask.shape, jnp.int32), pltpu.SemaphoreType.DMA((2,))],
             compiler_params=pltpu.CompilerParams(vmem_limit_bytes=32 << 20),
             name="ready",
-        )(placed(pair_mask, pltpu.HBM), placed(lag_basis, pltpu.HBM), placed(mine, pltpu.VMEM))
+        )(placed(pair_mask, pltpu.HBM), placed(mine, pltpu.VMEM))
         both = [came[3, d] for d in range(1, grps)]
         for d in range(1, grps):
             came[0, d] = came[3, d]

time: 11.7 us -> 11.2 us (0.957)
  Pallas kernels: 5.49 us -> 4.68 us
  waiting for transfers between devices: 0.98 us -> 1.34 us
    pallas_call x1, Pallas kernels: 1.63 us -> 0.88 us  [on_device(): pl.pallas_call(lambda *refs: ready_kernel(per, seg, *refs), out_shape=(pl...]
    ppermute x5, waiting for transfers between devices: 0.98 us -> 1.34 us  [exchange(): return lax.ppermute(array, axes, pairs)]
  transfers between devices with their start and end apart: 5 -> 5, of which waited for: 1 -> 2; matrix products, arithmetic and copies ran while one was open for 0% -> 0% of each run, Pallas kernels for 20% -> 13%
where the time goes in v8:
time: 11.2 us; the launch traced here: 11 us
  starting transfers between devices  4.93 us (44%)
  Pallas kernels  4.68 us (42%)
  waiting for transfers between devices  1.34 us (12%)
    ppermute x5, starting transfers between devices, exchange(): return lax.ppermute(array, axes, pairs)  4.93 us
    pallas_call x1, Pallas kernels, on_device(): pl.pallas_call(lambda *refs: spectra_kernel(per, seg, samples, [way for w...  1.88 us
    ppermute x5, waiting for transfers between devices, exchange(): return lax.ppermute(array, axes, pairs)  1.34 us
    pallas_call x1, Pallas kernels, on_device(): pl.pallas_call(lambda *refs: lags_kernel(per, seg, grps, tiles, late, *re...  1.34 us
    pallas_call x1, Pallas kernels, on_device(): pl.pallas_call(lambda *refs: ready_kernel(per, seg, *refs), out_shape=(pl...  0.88 us
    pallas_call x1, Pallas kernels, on_device(): pl.pallas_call(lambda *refs: early_kernel(per, seg, grps, tiles, soon, *r...  0.58 us
  transfers between devices with their start and end apart: 5, of which 2 were waited for; matrix products, arithmetic and copies ran while one was open for 0% of the time, Pallas kernels for 13%

profile of v8, /device:TPU:3, one launch (start us, length us, event | category | flops | bytes accessed | tf_op | source)
XLA Modules:
  0.0 11.0 jit_solution(9663328835923627121)
XLA Ops:
  0.0 1.9 %spectra.1 = (bf16[64,384]{1,0:T(8,128)(2,1)S(1)}, bf16[128,384]{1,0:T(8,128)(2,1)S(1)}, bf16[64,384]{1,0:T(8,128)(2,1)S(1)}, bf16[64,384]{1,0:T(8,128)(2,1)S(1)...) custom-call(s32[1,2,4]{2,1,0:T(2,128)} %refs_0_.2, s32[1,2]{1,0:T(1,128)} %refs_1_.1, s32[4,16]{1,0:T(4,128)} %refs_2_.1, ...), custom_call_target="tpu_custom_call" | custom-call | tf_op jit(solution)/shard_map/spectra/pallas_call | solution.py:372
  1.9 1.3 %collective-permute-start = (bf16[128,384]{1,0:T(8,128)(2,1)S(1)}, bf16[128,384]{1,0:T(8,128)(2,1)S(1)}, u32[]{:S(2)}, u32[]{:S(2)}) collective-permute-start(bf16[128,384]{1,0:T(8,128)(2,1)S(1)} %get-tuple-element.19), channel_id=1, source_target_pairs={{0,1},{1,0},{2,3},{3,2},{4,5},{5,4},{6,7},{7,6},{8,9},{9,8},{10,11... | collective-permute-start | bytes 294920 | tf_op jit(solution)/shard_map/ppermute | solution.py:359
  3.2 1.0 %collective-permute-start.1 = (bf16[64,384]{1,0:T(8,128)(2,1)S(1)}, bf16[64,384]{1,0:T(8,128)(2,1)S(1)}, u32[]{:S(2)}, u32[]{:S(2)}) collective-permute-start(bf16[64,384]{1,0:T(8,128)(2,1)S(1)} %get-tuple-element.20), channel_id=1, source_target_pairs={{0,2},{1,3},{2,0},{3,1},{4,6},{5,7},{6,4},{7,5},{8,10},{9,11},{10,... | collective-permute-start | bytes 147464 | tf_op jit(solution)/shard_map/ppermute | solution.py:359
  4.2 1.1 %collective-permute-start.2 = (bf16[64,384]{1,0:T(8,128)(2,1)S(1)}, bf16[64,384]{1,0:T(8,128)(2,1)S(1)}, u32[]{:S(2)}, u32[]{:S(2)}) collective-permute-start(bf16[64,384]{1,0:T(8,128)(2,1)S(1)} %get-tuple-element.21), channel_id=1, source_target_pairs={{0,1},{1,0},{2,5},{3,4},{4,3},{5,2},{6,9},{7,8},{8,7},{9,6},{10,13... | collective-permute-start | bytes 147464 | tf_op jit(solution)/shard_map/ppermute | solution.py:359
  5.3 1.5 %collective-permute-start.3 = (bf16[64,384]{1,0:T(8,128)(2,1)S(1)}, bf16[64,384]{1,0:T(8,128)(2,1)S(1)}, u32[]{:S(2)}, u32[]{:S(2)}) collective-permute-start(bf16[64,384]{1,0:T(8,128)(2,1)S(1)} %get-tuple-element.22), channel_id=1, source_target_pairs={{0,1},{1,0},{2,4},{3,5},{4,2},{5,3},{6,8},{7,9},{8,6},{9,7},{10,12... | collective-permute-start | bytes 147464 | tf_op jit(solution)/shard_map/ppermute | solution.py:359
  6.7 0.9 %ready.1 = (f32[96,128]{1,0:T(8,128)S(1)}, f32[256,512]{1,0:T(8,128)S(1)}, f32[32,512]{1,0:T(8,128)S(1)}) custom-call(s32[4,24]{1,0:T(4,128)} %refs_0_.3, bf16[64,384]{1,0:T(8,128)(2,1)S(1)} %get-tuple-element.15.refs_1_), custom_call_target="tpu_custom_call" | custom-call | tf_op jit(solution)/shard_map/ready/pallas_call | solution.py:396
  7.6 0.0 collective-permute-done.refs_3_.refs_0_
  7.7 0.1 collective-permute-start.4
  7.7 0.0 collective-permute-done.1.refs_4_
  7.7 0.6 %early.1.refs_3_ = f32[96,2001]{1,0:T(8,128)S(1)} custom-call(bf16[384,2001]{1,0:T(8,128)(2,1)S(1)} %get-tuple-element.14.refs_0_, f32[256,512]{1,0:T(8,128)S(1)} %get-tuple-element.17.refs_1_.refs_2_, f32[32,512]{1,0:T(8,128)S(1)} %get-tuple-element.18.refs_2_._, bf16[128,384]{1,0:T(8,128)(2,1)S(1)} %collective-permute-done.refs_3_.refs_0_, ...), custom_call_target="tpu_custom_call" | custom-call | tf_op jit(solution)/shard_map/early/pallas_call | solution.py:423
  8.3 1.1 %collective-permute-done.2.refs_4_ = bf16[64,384]{1,0:T(8,128)(2,1)S(1)} collective-permute-done((bf16[64,384]{1,0:T(8,128)(2,1)S(1)}, bf16[64,384]{1,0:T(8,128)(2,1)S(1)}, u32[]{:S(2)}, u32[]{:S(2)}) %collective-permute-start.2) | collective-permute-done | bytes 49184 | tf_op jit(solution)/shard_map/ppermute | solution.py:359
  9.5 0.2 %collective-permute-done.3.refs_5_ = bf16[64,384]{1,0:T(8,128)(2,1)S(1)} collective-permute-done((bf16[64,384]{1,0:T(8,128)(2,1)S(1)}, bf16[64,384]{1,0:T(8,128)(2,1)S(1)}, u32[]{:S(2)}, u32[]{:S(2)}) %collective-permute-start.3) | collective-permute-done | bytes 49184 | tf_op jit(solution)/shard_map/ppermute | solution.py:359
  9.7 0.0 collective-permute-done.4.refs_6_
  9.7 1.3 %lags.1 = bf16[4,24,2001]{2,1,0:T(8,128)(2,1)} custom-call(bf16[384,2001]{1,0:T(8,128)(2,1)S(1)} %get-tuple-element.14.refs_0_, f32[96,128]{1,0:T(8,128)S(1)} %get-tuple-element.16.refs_1_, f32[256,512]{1,0:T(8,128)S(1)} %get-tuple-element.17.refs_1_.refs_2_, f32[96,2001]{1,0:T(8,128)S(1)} %early.1.refs_3_, ...), custom_call_target="tpu_custom_call" | custom-call | tf_op jit(solution)/shard_map/lags/pallas_call | solution.py:432
  (1 shorter events, 0.0 us)
Async XLA Ops:
  1.9 5.7 %collective-permute-start = (bf16[128,384]{1,0:T(8,128)(2,1)S(1)}, bf16[128,384]{1,0:T(8,128)(2,1)S(1)}, u32[]{:S(2)}, u32[]{:S(2)}) collective-permute-start(bf16[128,384]{1,0:T(8,128)(2,1)S(1)} %get-tuple-element.19), channel_id=1, source_target_pairs={{0,1},{1,0},{2,3},{3,2},{4,5},{5,4},{6,7},{7,6},{8,9},{9,8},{10,11... | collective-permute-start | bytes 294920 | tf_op jit(solution)/shard_map/ppermute | solution.py:359
  3.2 4.5 %collective-permute-start.1 = (bf16[64,384]{1,0:T(8,128)(2,1)S(1)}, bf16[64,384]{1,0:T(8,128)(2,1)S(1)}, u32[]{:S(2)}, u32[]{:S(2)}) collective-permute-start(bf16[64,384]{1,0:T(8,128)(2,1)S(1)} %get-tuple-element.20), channel_id=1, source_target_pairs={{0,2},{1,3},{2,0},{3,1},{4,6},{5,7},{6,4},{7,5},{8,10},{9,11},{10,... | collective-permute-start | bytes 147464 | tf_op jit(solution)/shard_map/ppermute | solution.py:359
  4.2 5.3 %collective-permute-start.2 = (bf16[64,384]{1,0:T(8,128)(2,1)S(1)}, bf16[64,384]{1,0:T(8,128)(2,1)S(1)}, u32[]{:S(2)}, u32[]{:S(2)}) collective-permute-start(bf16[64,384]{1,0:T(8,128)(2,1)S(1)} %get-tuple-element.21), channel_id=1, source_target_pairs={{0,1},{1,0},{2,5},{3,4},{4,3},{5,2},{6,9},{7,8},{8,7},{9,6},{10,13... | collective-permute-start | bytes 147464 | tf_op jit(solution)/shard_map/ppermute | solution.py:359
  5.3 4.4 %collective-permute-start.3 = (bf16[64,384]{1,0:T(8,128)(2,1)S(1)}, bf16[64,384]{1,0:T(8,128)(2,1)S(1)}, u32[]{:S(2)}, u32[]{:S(2)}) collective-permute-start(bf16[64,384]{1,0:T(8,128)(2,1)S(1)} %get-tuple-element.22), channel_id=1, source_target_pairs={{0,1},{1,0},{2,4},{3,5},{4,2},{5,3},{6,8},{7,9},{8,6},{9,7},{10,12... | collective-permute-start | bytes 147464 | tf_op jit(solution)/shard_map/ppermute | solution.py:359
  7.7 2.0 %collective-permute-start.4 = (bf16[64,384]{1,0:T(8,128)(2,1)S(1)}, bf16[64,384]{1,0:T(8,128)(2,1)S(1)}, u32[]{:S(2)}, u32[]{:S(2)}) collective-permute-start(bf16[64,384]{1,0:T(8,128)(2,1)S(1)} %pass.1), channel_id=1, source_target_pairs={{0,2},{1,3},{2,0},{3,1},{4,6},{5,7},{6,4},{7,5},{8,10},{9,11},{10,... | collective-permute-start | bytes 147464 | tf_op jit(solution)/shard_map/ppermute | solution.py:359

commit v9 on v8

--- a/solution.py
+++ b/solution.py
@@ -16,6 +16,7 @@
 HALF = 64
 LAST = ((0, 1), (1, 0))
 VALID = 16
+SLOT = 24
 WIDE = 3 * LANE
 LAG_STEP = 4 * LANE
 STEP = 2 * LANE
@@ -108,14 +109,14 @@
 
 
 def spectra_kernel(
-    per, seg, samples, ways, starts, stretches, rows_hbm, count_hbm, valid_hbm, traces_hbm, factors_hbm, basis_hbm,
+    per, seg, samples, ways, starts, stretches, rows_hbm, count_hbm, valid_hbm, traces_hbm, factors_hbm, basis_hbm, mask_hbm,
     *refs,
 ):
-    mine_ref, *outs, basis_ref, rows_ref, count_ref, valid_ref, traces, factors, white_ref, order_ref, sems = refs
+    mine_ref, *outs, basis_ref, mask_ref, rows_ref, count_ref, valid_ref, traces, factors, white_ref, order_ref, sems = refs
     lines = per * seg
     pairs = [
         (factors_hbm, factors), (traces_hbm, traces),
-        (rows_hbm, rows_ref), (count_hbm, count_ref), (valid_hbm, valid_ref), (basis_hbm, basis_ref),
+        (rows_hbm, rows_ref), (count_hbm, count_ref), (valid_hbm, valid_ref), (basis_hbm, basis_ref), (mask_hbm, mask_ref),
     ]
     copies = [pltpu.make_async_copy(src, dst, sems.at[i]) for i, (src, dst) in enumerate(pairs)]
     for copy in copies:
@@ -137,6 +138,11 @@
 
     for copy in copies[2:5]:
         copy.wait()
+    station, _ = divided(iota((lines, LANE), 0), seg)
+    extra = jnp.zeros((lines, LANE), F32)
+    for j in range(per):
+        listed = (station == rows_ref[0, odd, j]) & (j < count_ref[0, odd])
+        extra = jnp.where((iota((lines, LANE), 1) == SLOT + j) & listed, 1.0, extra)
     usable = jnp.concatenate(column_of(valid_ref[...].astype(F32)), axis=0)
 
     copies[0].wait()
@@ -178,7 +184,7 @@
     level = level + jnp.dot(p_low, window, preferred_element_type=F32)
     factor = usable / jnp.sqrt(level * (1.0 / (2 * NBIN)) + 1e-06)
     tail = tail * factor[:, LANE:]
-    tail = jnp.where(iota((lines, LANE), 1) == VALID, usable, tail)
+    tail = jnp.where(iota((lines, LANE), 1) == VALID, usable, tail) + extra
     white = jnp.concatenate([real * factor[:, :LANE], imag * factor[:, :LANE], tail], axis=1)
     white_ref[...] = white.reshape(per, seg, WIDE)
 
@@ -196,8 +202,9 @@
     own, near, far = ordered(None), ordered(odd), ordered(1 - odd)
     mine_ref[...] = own
     for ref, way in zip(outs, ways):
-        ref[...] = (own, near, far, jnp.concatenate([own, near], axis=0))[way]
-    copies[5].wait()
+        ref[...] = (own, near, far, own)[way]
+    for copy in copies[5:]:
+        copy.wait()
 
 
 def stacked(per, lines, spread, ref):
@@ -245,30 +252,24 @@
     return [[row[:, k * LANE : (k + 1) * LANE] for k in range(4)] for row in rows]
 
 
-def ready_kernel(per, seg, mask_hbm, mine_ref, keep_ref, spread_ref, sums_ref, mask_ref, sems):
-    copies = [
-        pltpu.make_async_copy(mask_hbm, mask_ref, sems.at[0]),
-    ]
-    for copy in copies:
-        copy.start()
+def ready_kernel(per, seg, mine_ref, spread_ref, sums_ref):
     lines = per * seg
     part, _ = divided(iota((lines, lines), 0), per)
     source = iota((lines, lines), 1)
     pick = [jnp.where(source == part * per + s, 1.0, 0.0).astype(BF16) for s in range(per)]
     spread = jnp.dot(jnp.concatenate(pick, axis=0), mine_ref[...], preferred_element_type=F32)
-    spread_ref[:, :WIDE] = spread
+    spread_ref[:, : 2 * LANE] = spread[:, : 2 * LANE]
+    tail = spread[:, 2 * LANE :]
+    spread_ref[:, 2 * LANE : WIDE] = jnp.where(holds_tail(iota(tail.shape, 1)), tail, 0.0)
     valid = spread[:, 2 * LANE + VALID : 2 * LANE + VALID + 1]
     spread_ref[:, WIDE:] = jnp.broadcast_to(valid, (per * lines, LANE))
     store_sums(per, sums_ref, 0, stacked(per, lines, spread_ref, mine_ref))
-    copies[0].wait()
-    keep = jnp.concatenate(column_of(mask_ref[...].astype(F32)), axis=0)
-    keep_ref[...] = jnp.broadcast_to(keep, keep_ref.shape)
-
-
-def pass_kernel(lines, *refs):
+
+
+def pass_kernel(_, near_ref, *refs):
     half = len(refs) // 2
-    for src, dst in zip(refs[:half], refs[half:]):
-        dst[...] = src[lines:, :]
+    for src, dst in zip((near_ref, *refs[:half]), refs[half:]):
+        dst[...] = src[...]
 
 
 def place_of(name, grps, tiles):
@@ -286,10 +287,20 @@
     return packed(*(row * scale for row in rows[:3])).astype(BF16)
 
 
-def early_kernel(per, seg, grps, tiles, names, basis_ref, spread_ref, mine_ref, *refs):
-    series_ref = refs[-1]
+def early_kernel(per, seg, grps, tiles, names, mask_ref, basis_ref, spread_ref, mine_ref, *refs):
+    *came, series_ref, keep_ref, near_ref = refs
+    keep = jnp.concatenate(column_of(mask_ref[...].astype(F32)), axis=0)
+    keep_ref[...] = jnp.broadcast_to(keep, keep_ref.shape)
+    lines = per * seg
+    _, slot = divided(iota((LANE, lines), 1), per)
+    to_slots = jnp.where(iota((LANE, lines), 0) == SLOT + slot, 1.0, 0.0).astype(BF16)
+    same = divided(iota((lines, lines), 0), per)[0] == divided(iota((lines, lines), 1), per)[0]
     sums = [load_sums(per, mine_ref, 0)]
-    sums += [stacked(per, per * seg, spread_ref, ref) for ref in refs[:-1]]
+    for i, ref in enumerate(came):
+        listed = jnp.dot(ref[:, 2 * LANE :], to_slots, preferred_element_type=F32)
+        listed = jnp.where(same, listed, 0.0).astype(BF16)
+        near_ref[i] = lax.dot_general(listed, ref[...], (((0,), (0,)), ((), ())), preferred_element_type=F32)
+        sums.append(stacked(per, lines, spread_ref, near_ref.at[i]))
     places = [place_of(name, grps, tiles) for name in ((0, 0), *names)]
     half = iota((8, LANE), 0) >> 2
     blocks = 3 * grps // 2
@@ -309,9 +320,9 @@
 
 
 def lags_kernel(per, seg, grps, tiles, names, basis_ref, keep_ref, spread_ref, series_ref, *refs):
-    out_ref, result, sems = refs[-3:]
+    *came, out_ref, result, sems = refs
     left = []
-    for ref in refs[:-3]:
+    for ref in came:
         left += [over_count(rows) for rows in stacked(per, per * seg, spread_ref, ref)]
     left = jnp.concatenate(left, axis=0)
     places = [place_of(name, grps, tiles) for name in names]
@@ -358,6 +369,15 @@
                 pairs.append((t * grps + g, goal))
         return lax.ppermute(array, axes, pairs)
 
+    def call(kernel, name, inputs, **kw):
+        return pl.pallas_call(
+            kernel,
+            in_specs=[vmem] * len(inputs),
+            compiler_params=pltpu.CompilerParams(vmem_limit_bytes=32 << 20),
+            name=name,
+            **kw,
+        )(*[placed(x, pltpu.VMEM) for x in inputs])
+
     def on_device(traces, validity, boundary_rows, boundary_count, pair_mask):
         per, seg, samples = traces.shape
         lines = per * seg
@@ -365,19 +385,18 @@
         factors, starts, stretches = fourier_tables(samples)
         lag_basis = jnp.asarray(lag_table(samples))
         payload = pltpu.VMEM((lines, WIDE), BF16)
-        sent = [(3, d) for d in range(1, grps)] + [(1, 0)] + [(2, d) for d in reversed(range(grps))]
-        soon = [(0, d) for d in range(1, grps)] + [(1, 0)]
-        late = [(2, d) for d in reversed(range(grps))] + [(1, d) for d in range(1, grps)]
-        inputs = [boundary_rows, boundary_count, validity, traces.reshape(lines, samples), jnp.asarray(factors), lag_basis]
-        mine, *rest, basis = pl.pallas_call(
+        sent = [(3, d) for d in range(1, grps)] + [(2, d) for d in reversed(range(grps))]
+        soon = [(1, d) for d in range(1, grps)]
+        late = [(2, d) for d in reversed(range(grps))] + [(1, 0)] + [(0, d) for d in range(1, grps)]
+        inputs = [boundary_rows, boundary_count, validity, traces.reshape(lines, samples), jnp.asarray(factors), lag_basis, pair_mask]
+        mine, near, *rest, basis, mask = pl.pallas_call(
             lambda *refs: spectra_kernel(
-                per, seg, samples, [way for way, _ in sent], starts, stretches, *refs
+                per, seg, samples, [1] + [way for way, _ in sent], starts, stretches, *refs
             ),
-            out_shape=(payload,) + tuple(
-                pltpu.VMEM(((1 + way // 3) * lines, WIDE), BF16) for way, _ in sent
-            ) + (pltpu.VMEM(lag_basis.shape, BF16),),
+            out_shape=(payload,) * (2 + len(sent))
+            + (pltpu.VMEM(lag_basis.shape, BF16), pltpu.VMEM(pair_mask.shape, jnp.int32)),
             in_specs=[hbm] * len(inputs),
-            out_specs=(vmem,) * (2 + len(sent)),
+            out_specs=(vmem,) * (4 + len(sent)),
             scratch_shapes=[
                 pltpu.SMEM(boundary_rows.shape, jnp.int32),
                 pltpu.SMEM(boundary_count.shape, jnp.int32),
@@ -386,61 +405,51 @@
                 pltpu.VMEM(factors.shape, F32),
                 pltpu.VMEM((per, seg, WIDE), F32),
                 pltpu.VMEM((3, lines, LANE), F32),
-                pltpu.SemaphoreType.DMA((6,)),
+                pltpu.SemaphoreType.DMA((7,)),
             ],
             compiler_params=pltpu.CompilerParams(vmem_limit_bytes=32 << 20),
             name="spectra",
         )(*[placed(x, pltpu.HBM) for x in inputs])
-        came = {(way, by): exchange(array, way % 3, by) for (way, by), array in zip(sent, rest)}
+        came = [exchange(array, min(way, 4 - way), by) for (way, by), array in zip(sent, rest)]
+        aside, far = came[: grps - 1], came[grps - 1 :]
         rows = per * columns
-        keep, spread, first = pl.pallas_call(
+        spread, first = call(
             lambda *refs: ready_kernel(per, seg, *refs),
+            "ready",
+            [mine],
             out_shape=(
-                pltpu.VMEM((rows, LANE), F32),
                 pltpu.VMEM((per * lines, WIDE + LANE), F32),
                 pltpu.VMEM((per * 8, WIDE + LANE), F32),
             ),
-            in_specs=[hbm, vmem],
-            out_specs=(vmem,) * 3,
-            scratch_shapes=[pltpu.VMEM(pair_mask.shape, jnp.int32), pltpu.SemaphoreType.DMA((2,))],
-            compiler_params=pltpu.CompilerParams(vmem_limit_bytes=32 << 20),
-            name="ready",
-        )(placed(pair_mask, pltpu.HBM), placed(mine, pltpu.VMEM))
-        both = [came[3, d] for d in range(1, grps)]
-        for d in range(1, grps):
-            came[0, d] = came[3, d]
-        if both:
-            passed = pl.pallas_call(
-                lambda _, *refs: pass_kernel(lines, *refs),
-                out_shape=(payload,) * len(both),
-                in_specs=[vmem] * (1 + len(both)),
-                out_specs=(vmem,) * len(both),
-                name="pass",
-            )(*[placed(x, pltpu.VMEM) for x in (first, *both)])
-            for d, array in enumerate(passed):
-                came[1, d + 1] = exchange(array, 1, 0)
-        inputs = [placed(x, pltpu.VMEM) for x in (basis, spread, first, *(came[name] for name in soon))]
-        series = pl.pallas_call(
+            out_specs=(vmem,) * 2,
+        )
+        passed = call(
+            pass_kernel,
+            "pass",
+            [first, near, *aside],
+            out_shape=(payload,) * grps,
+            out_specs=(vmem,) * grps,
+        )
+        passed = [exchange(array, 1, 0) for array in passed]
+        series, keep = call(
             lambda *refs: early_kernel(per, seg, grps, tiles, soon, *refs),
-            out_shape=pltpu.VMEM((rows, LAGS), F32),
-            in_specs=[vmem] * len(inputs),
-            out_specs=vmem,
-            compiler_params=pltpu.CompilerParams(vmem_limit_bytes=32 << 20),
-            name="early",
-        )(*inputs)
-        inputs = [placed(x, pltpu.VMEM) for x in (basis, keep, spread, series, *(came[name] for name in late))]
-        return pl.pallas_call(
+            "early",
+            [mask, basis, spread, first, *aside],
+            out_shape=(pltpu.VMEM((rows, LAGS), F32), pltpu.VMEM((rows, LANE), F32)),
+            out_specs=(vmem,) * 2,
+            scratch_shapes=[pltpu.VMEM((max(len(soon), 1), lines, WIDE), F32)],
+        )
+        return call(
             lambda *refs: lags_kernel(per, seg, grps, tiles, late, *refs),
+            "lags",
+            [basis, keep, spread, series, *far, *passed],
             out_shape=jax.ShapeDtypeStruct((per, columns, LAGS), BF16),
-            in_specs=[vmem] * len(inputs),
             out_specs=hbm,
             scratch_shapes=[
                 pltpu.VMEM((per, columns, LAGS), BF16),
                 pltpu.SemaphoreType.DMA((pl.cdiv(LAGS, LAG_STEP),)),
             ],
-            compiler_params=pltpu.CompilerParams(vmem_limit_bytes=32 << 20),
-            name="lags",
-        )(*inputs)
+        )
 
     return jax.shard_map(
         on_device,

time: 11.2 us -> 10.9 us (0.973)
  Pallas kernels: 4.68 us -> 4.45 us
  waiting for transfers between devices: 1.34 us -> 1.19 us
    pallas_call x5, Pallas kernels: 4.68 us -> 4.45 us  [the longest x4 2.56 us: call(): pl.pallas_call(kernel, in_specs=[vmem] * len(inputs), compiler_params=plt...]
    ppermute x5, waiting for transfers between devices: 1.34 us -> 1.19 us  [exchange(): return lax.ppermute(array, axes, pairs)]
  transfers between devices with their start and end apart: 5 -> 5, of which waited for: 2 -> 2; matrix products, arithmetic and copies ran while one was open for 0% -> 0% of each run, Pallas kernels for 13% -> 10%
where the time goes in v9:
time: 10.9 us; the launch traced here: 10.7 us
  starting transfers between devices  5.03 us (46%)
  Pallas kernels  4.45 us (41%)
  waiting for transfers between devices  1.19 us (11%)
    ppermute x5, starting transfers between devices, exchange(): return lax.ppermute(array, axes, pairs)  5.03 us
    pallas_call x4, Pallas kernels, call(): pl.pallas_call(kernel, in_specs=[vmem] * len(inputs), compiler_params=plt...  2.56 us
    pallas_call x1, Pallas kernels, on_device(): pl.pallas_call(lambda *refs: spectra_kernel(per, seg, samples, [1] + [way...  1.89 us
    ppermute x5, waiting for transfers between devices, exchange(): return lax.ppermute(array, axes, pairs)  1.19 us
  transfers between devices with their start and end apart: 5, of which 2 were waited for; matrix products, arithmetic and copies ran while one was open for 0% of the time, Pallas kernels for 10%

profile of v9, /device:TPU:3, one launch (start us, length us, event | category | flops | bytes accessed | tf_op | source)
XLA Modules:
  0.0 10.7 jit_solution(15827245769284159152)
XLA Ops:
  0.0 1.9 %spectra.1 = (bf16[64,384]{1,0:T(8,128)(2,1)S(1)}, bf16[64,384]{1,0:T(8,128)(2,1)S(1)}, bf16[64,384]{1,0:T(8,128)(2,1)S(1)}, bf16[64,384]{1,0:T(8,128)(2,1)S(1)}...) custom-call(s32[1,2,4]{2,1,0:T(2,128)} %refs_0_.1, s32[1,2]{1,0:T(1,128)} %refs_1_.1, ...), custom_call_target="tpu_custom_call" | custom-call | tf_op jit(solution)/shard_map/spectra/pallas_call | solution.py:392
  1.9 1.9 %collective-permute-start = (bf16[64,384]{1,0:T(8,128)(2,1)S(1)}, bf16[64,384]{1,0:T(8,128)(2,1)S(1)}, u32[]{:S(2)}, u32[]{:S(2)}) collective-permute-start(bf16[64,384]{1,0:T(8,128)(2,1)S(1)} %get-tuple-element.23), channel_id=1, source_target_pairs={{0,3},{1,2},{2,1},{3,0},{4,7},{5,6},{6,5},{7,4},{8,11},{9,10},{10,... | collective-permute-start | bytes 147464 | tf_op jit(solution)/shard_map/ppermute | solution.py:370
  3.8 1.1 %collective-permute-start.1 = (bf16[64,384]{1,0:T(8,128)(2,1)S(1)}, bf16[64,384]{1,0:T(8,128)(2,1)S(1)}, u32[]{:S(2)}, u32[]{:S(2)}) collective-permute-start(bf16[64,384]{1,0:T(8,128)(2,1)S(1)} %get-tuple-element.26), channel_id=1, source_target_pairs={{0,1},{1,0},{2,5},{3,4},{4,3},{5,2},{6,9},{7,8},{8,7},{9,6},{10,13... | collective-permute-start | bytes 147464 | tf_op jit(solution)/shard_map/ppermute | solution.py:370
  4.8 1.5 %collective-permute-start.2 = (bf16[64,384]{1,0:T(8,128)(2,1)S(1)}, bf16[64,384]{1,0:T(8,128)(2,1)S(1)}, u32[]{:S(2)}, u32[]{:S(2)}) collective-permute-start(bf16[64,384]{1,0:T(8,128)(2,1)S(1)} %get-tuple-element.27), channel_id=1, source_target_pairs={{0,1},{1,0},{2,4},{3,5},{4,2},{5,3},{6,8},{7,9},{8,6},{9,7},{10,12... | collective-permute-start | bytes 147464 | tf_op jit(solution)/shard_map/ppermute | solution.py:370
  6.4 0.3 %ready.1 = (f32[256,512]{1,0:T(8,128)S(1)}, f32[32,512]{1,0:T(8,128)S(1)}) custom-call(bf16[64,384]{1,0:T(8,128)(2,1)S(1)} %get-tuple-element.20.refs_0_), custom_call_target="tpu_custom_call" | custom-call | tf_op jit(solution)/shard_map/ready/pallas_call | solution.py:373
  6.6 0.0 collective-permute-done.refs_4_.refs_0_
  6.7 0.1 collective-permute-start.3
  6.7 0.5 %collective-permute-start.4 = (bf16[64,384]{1,0:T(8,128)(2,1)S(1)}, bf16[64,384]{1,0:T(8,128)(2,1)S(1)}, u32[]{:S(2)}, u32[]{:S(2)}) collective-permute-start(bf16[64,384]{1,0:T(8,128)(2,1)S(1)} %get-tuple-element.30), channel_id=1, source_target_pairs={{0,2},{1,3},{2,0},{3,1},{4,6},{5,7},{6,4},{7,5},{8,10},{9,11},{10,... | collective-permute-start | bytes 147464 | tf_op jit(solution)/shard_map/ppermute | solution.py:370
  7.2 0.8 %early.1 = (f32[96,2001]{1,0:T(8,128)S(1)}, f32[96,128]{1,0:T(8,128)S(1)}) custom-call(s32[4,24]{1,0:T(4,128)S(1)} %get-tuple-element.19.refs_0_, bf16[384,2001]{1,0:T(8,128)(2,1)S(1)} %get-tuple-element.18.refs_1_.refs_0_, f32[256,512]{1,0:T(8,128)S(1)} %get-tuple-element.21.refs_2_, f32[32,512]{1,0:T(8,128)S(1)} %get-tuple-element.22.refs_3_._, ...), custom_call_target="tpu_custom_call" | custom-call | tf_op jit(solution)/shard_map/early/pallas_call | solution.py:373
  8.1 1.0 %collective-permute-done.1.refs_4_ = bf16[64,384]{1,0:T(8,128)(2,1)S(1)} collective-permute-done((bf16[64,384]{1,0:T(8,128)(2,1)S(1)}, bf16[64,384]{1,0:T(8,128)(2,1)S(1)}, u32[]{:S(2)}, u32[]{:S(2)}) %collective-permute-start.1) | collective-permute-done | bytes 49184 | tf_op jit(solution)/shard_map/ppermute | solution.py:370
  9.1 0.2 %collective-permute-done.2.refs_5_ = bf16[64,384]{1,0:T(8,128)(2,1)S(1)} collective-permute-done((bf16[64,384]{1,0:T(8,128)(2,1)S(1)}, bf16[64,384]{1,0:T(8,128)(2,1)S(1)}, u32[]{:S(2)}, u32[]{:S(2)}) %collective-permute-start.2) | collective-permute-done | bytes 49184 | tf_op jit(solution)/shard_map/ppermute | solution.py:370
  9.2 0.0 collective-permute-done.3.refs_6_
  9.2 0.0 collective-permute-done.4.refs_7_
  9.2 1.5 %lags.1 = bf16[4,24,2001]{2,1,0:T(8,128)(2,1)} custom-call(bf16[384,2001]{1,0:T(8,128)(2,1)S(1)} %get-tuple-element.18.refs_1_.refs_0_, f32[96,128]{1,0:T(8,128)S(1)} %get-tuple-element.24.refs_1_, f32[256,512]{1,0:T(8,128)S(1)} %get-tuple-element.21.refs_2_, f32[96,2001]{1,0:T(8,128)S(1)} %get-tuple-element.25.refs_3_, ...), custom_call_target="tpu_custom_call" | custom-call | tf_op jit(solution)/shard_map/lags/pallas_call | solution.py:373
  (1 shorter events, 0.0 us)
Async XLA Ops:
  1.9 4.7 %collective-permute-start = (bf16[64,384]{1,0:T(8,128)(2,1)S(1)}, bf16[64,384]{1,0:T(8,128)(2,1)S(1)}, u32[]{:S(2)}, u32[]{:S(2)}) collective-permute-start(bf16[64,384]{1,0:T(8,128)(2,1)S(1)} %get-tuple-element.23), channel_id=1, source_target_pairs={{0,3},{1,2},{2,1},{3,0},{4,7},{5,6},{6,5},{7,4},{8,11},{9,10},{10,... | collective-permute-start | bytes 147464 | tf_op jit(solution)/shard_map/ppermute | solution.py:370
  3.8 5.3 %collective-permute-start.1 = (bf16[64,384]{1,0:T(8,128)(2,1)S(1)}, bf16[64,384]{1,0:T(8,128)(2,1)S(1)}, u32[]{:S(2)}, u32[]{:S(2)}) collective-permute-start(bf16[64,384]{1,0:T(8,128)(2,1)S(1)} %get-tuple-element.26), channel_id=1, source_target_pairs={{0,1},{1,0},{2,5},{3,4},{4,3},{5,2},{6,9},{7,8},{8,7},{9,6},{10,13... | collective-permute-start | bytes 147464 | tf_op jit(solution)/shard_map/ppermute | solution.py:370
  4.8 4.4 %collective-permute-start.2 = (bf16[64,384]{1,0:T(8,128)(2,1)S(1)}, bf16[64,384]{1,0:T(8,128)(2,1)S(1)}, u32[]{:S(2)}, u32[]{:S(2)}) collective-permute-start(bf16[64,384]{1,0:T(8,128)(2,1)S(1)} %get-tuple-element.27), channel_id=1, source_target_pairs={{0,1},{1,0},{2,4},{3,5},{4,2},{5,3},{6,8},{7,9},{8,6},{9,7},{10,12... | collective-permute-start | bytes 147464 | tf_op jit(solution)/shard_map/ppermute | solution.py:370
  6.7 2.6 %collective-permute-start.3 = (bf16[64,384]{1,0:T(8,128)(2,1)S(1)}, bf16[64,384]{1,0:T(8,128)(2,1)S(1)}, u32[]{:S(2)}, u32[]{:S(2)}) collective-permute-start(bf16[64,384]{1,0:T(8,128)(2,1)S(1)} %get-tuple-element.29), channel_id=1, source_target_pairs={{0,2},{1,3},{2,0},{3,1},{4,6},{5,7},{6,4},{7,5},{8,10},{9,11},{10,... | collective-permute-start | bytes 147464 | tf_op jit(solution)/shard_map/ppermute | solution.py:370
  6.7 2.5 %collective-permute-start.4 = (bf16[64,384]{1,0:T(8,128)(2,1)S(1)}, bf16[64,384]{1,0:T(8,128)(2,1)S(1)}, u32[]{:S(2)}, u32[]{:S(2)}) collective-permute-start(bf16[64,384]{1,0:T(8,128)(2,1)S(1)} %get-tuple-element.30), channel_id=1, source_target_pairs={{0,2},{1,3},{2,0},{3,1},{4,6},{5,7},{6,4},{7,5},{8,10},{9,11},{10,... | collective-permute-start | bytes 147464 | tf_op jit(solution)/shard_map/ppermute | solution.py:370

commit v10 on v9

--- a/solution.py
+++ b/solution.py
@@ -15,6 +15,7 @@
 TAIL = NBIN - LANE
 HALF = 64
 LAST = ((0, 1), (1, 0))
+TOGETHER = 2
 VALID = 16
 SLOT = 24
 WIDE = 3 * LANE
@@ -207,36 +208,41 @@
         copy.wait()
 
 
-def stacked(per, lines, spread, ref):
-    sums = [[None] * 5 for _ in range(per)]
-
-    def add(s, i, value):
-        sums[s][i] = value if sums[s][i] is None else sums[s][i] + value
+def stacked(per, lines, spread, refs):
+    sums = [[[None] * 5 for _ in range(per)] for _ in refs]
+
+    def add(total, i, value):
+        total[i] = value if total[i] is None else total[i] + value
 
     for at in range(0, lines, 16):
-        both = ref[at : at + 16, :].astype(F32)
+        both = [ref[at : at + 16, :].astype(F32) for ref in refs]
         for half in range(2):
-            one = both[8 * half : 8 * half + 8]
-            c_re, c_im, c_tail = one[:, :LANE], one[:, LANE : 2 * LANE], one[:, 2 * LANE :]
-            c_turn = pltpu.roll(c_tail, HALF, 1)
-            c_valid = jnp.broadcast_to(c_tail[:, VALID : VALID + 1], c_tail.shape)
+            columns = []
+            for x in both:
+                one = x[8 * half : 8 * half + 8]
+                c_re, c_im, c_tail = one[:, :LANE], one[:, LANE : 2 * LANE], one[:, 2 * LANE :]
+                c_valid = jnp.broadcast_to(c_tail[:, VALID : VALID + 1], c_tail.shape)
+                columns.append((c_re, c_im, c_tail, pltpu.roll(c_tail, HALF, 1), c_valid))
             for s in range(per):
                 here = s * lines + at + 8 * half
                 left = spread[here : here + 8, :]
                 l_re, l_im, l_tail, l_valid = (left[:, k * LANE : (k + 1) * LANE] for k in range(4))
-                add(s, 0, l_re * c_re + l_im * c_im)
-                add(s, 1, l_im * c_re - l_re * c_im)
-                add(s, 2, l_tail * c_tail)
-                add(s, 3, l_tail * c_turn)
-                add(s, 4, l_valid * c_valid)
+                for total, (c_re, c_im, c_tail, c_turn, c_valid) in zip(sums, columns):
+                    add(total[s], 0, l_re * c_re + l_im * c_im)
+                    add(total[s], 1, l_im * c_re - l_re * c_im)
+                    add(total[s], 2, l_tail * c_tail)
+                    add(total[s], 3, l_tail * c_turn)
+                    add(total[s], 4, l_valid * c_valid)
     low_lanes = iota((8, LANE), 1) < HALF
     out = []
-    for s in range(per):
-        straight, turned = sums[s][2], sums[s][3]
-        straight = straight + pltpu.roll(straight, HALF, 1)
-        turned = turned - pltpu.roll(turned, HALF, 1)
-        all_lanes = [sums[s][0], sums[s][1], jnp.where(low_lanes, straight, turned), sums[s][4]]
-        out.append([v + pltpu.roll(v, 4, 0) for v in all_lanes])
+    for total in sums:
+        piece = []
+        for re, im, straight, turned, count in total:
+            straight = straight + pltpu.roll(straight, HALF, 1)
+            turned = turned - pltpu.roll(turned, HALF, 1)
+            all_lanes = [re, im, jnp.where(low_lanes, straight, turned), count]
+            piece.append([v + pltpu.roll(v, 4, 0) for v in all_lanes])
+        out.append(piece)
     return out
 
 
@@ -263,7 +269,7 @@
     spread_ref[:, 2 * LANE : WIDE] = jnp.where(holds_tail(iota(tail.shape, 1)), tail, 0.0)
     valid = spread[:, 2 * LANE + VALID : 2 * LANE + VALID + 1]
     spread_ref[:, WIDE:] = jnp.broadcast_to(valid, (per * lines, LANE))
-    store_sums(per, sums_ref, 0, stacked(per, lines, spread_ref, mine_ref))
+    store_sums(per, sums_ref, 0, stacked(per, lines, spread_ref, [mine_ref])[0])
 
 
 def pass_kernel(_, near_ref, *refs):
@@ -284,11 +290,25 @@
 
 def over_count(rows):
     scale = 1.0 / jnp.maximum(rows[3], 1.0)
-    return packed(*(row * scale for row in rows[:3])).astype(BF16)
-
-
-def early_kernel(per, seg, grps, tiles, names, mask_ref, basis_ref, spread_ref, mine_ref, *refs):
-    *came, series_ref, keep_ref, near_ref = refs
+    return packed(*(row * scale for row in rows[:3]))
+
+
+def put(names, grps, tiles, per, pieces, rows):
+    places = [place_of(name, grps, tiles) for name in names]
+    half = iota((8, WIDE), 0) >> 2
+    blocks = 3 * grps // 2
+    for b in range(blocks):
+        for (place, there), piece in zip(places, pieces):
+            fit = (half + 2 * b) == place
+            fit = fit if there is None else fit & there
+            for s in range(per):
+                at = s * blocks + b
+                rows[at] = jnp.where(fit, piece[s], rows[at])
+    return rows
+
+
+def early_kernel(per, seg, grps, tiles, names, mask_ref, spread_ref, mine_ref, *refs):
+    *came, rows_ref, keep_ref, near_ref = refs
     keep = jnp.concatenate(column_of(mask_ref[...].astype(F32)), axis=0)
     keep_ref[...] = jnp.broadcast_to(keep, keep_ref.shape)
     lines = per * seg
@@ -300,49 +320,41 @@
         listed = jnp.dot(ref[:, 2 * LANE :], to_slots, preferred_element_type=F32)
         listed = jnp.where(same, listed, 0.0).astype(BF16)
         near_ref[i] = lax.dot_general(listed, ref[...], (((0,), (0,)), ((), ())), preferred_element_type=F32)
-        sums.append(stacked(per, lines, spread_ref, near_ref.at[i]))
-    places = [place_of(name, grps, tiles) for name in ((0, 0), *names)]
-    half = iota((8, LANE), 0) >> 2
-    blocks = 3 * grps // 2
-    left = [None] * (per * blocks)
-    for b in range(blocks):
-        fits = []
-        for place, there in places:
-            fit = (half + 2 * b) == place
-            fits.append(fit if there is None else fit & there)
-        for s in range(per):
-            rows = [jnp.zeros((8, LANE), F32)] * 4
-            for fit, piece in zip(fits, sums):
-                rows = [jnp.where(fit, new, row) for new, row in zip(piece[s], rows)]
-            at = (s * blocks + b) * 8
-            left[at // 8] = over_count(rows)
-    series_ref[...] = jnp.dot(jnp.concatenate(left, axis=0), basis_ref[...], preferred_element_type=F32)
-
-
-def lags_kernel(per, seg, grps, tiles, names, basis_ref, keep_ref, spread_ref, series_ref, *refs):
+        sums += stacked(per, lines, spread_ref, [near_ref.at[i]])
+    pieces = [[over_count(rows) for rows in piece] for piece in sums]
+    rows = [jnp.zeros((8, WIDE), F32)] * (rows_ref.shape[0] // 8)
+    rows_ref[...] = jnp.concatenate(put(((0, 0), *names), grps, tiles, per, pieces, rows), axis=0)
+
+
+def middle_kernel(per, seg, grps, tiles, names, spread_ref, early_ref, *refs):
+    *came, rows_ref = refs
+    pieces = []
+    for i in range(0, len(came), TOGETHER):
+        for piece in stacked(per, per * seg, spread_ref, came[i : i + TOGETHER]):
+            pieces.append([over_count(rows) for rows in piece])
+    rows = [early_ref[at : at + 8, :] for at in range(0, early_ref.shape[0], 8)]
+    rows_ref[...] = jnp.concatenate(put(names, grps, tiles, per, pieces, rows), axis=0)
+
+
+def lags_kernel(per, seg, grps, tiles, names, basis_ref, keep_ref, spread_ref, rows_ref, *refs):
     *came, out_ref, result, sems = refs
-    left = []
-    for ref in came:
-        left += [over_count(rows) for rows in stacked(per, per * seg, spread_ref, ref)]
-    left = jnp.concatenate(left, axis=0)
-    places = [place_of(name, grps, tiles) for name in names]
-    blocks = 3 * grps // 2
+    pieces = []
+    for i in range(0, len(came), TOGETHER):
+        for piece in stacked(per, per * seg, spread_ref, came[i : i + TOGETHER]):
+            pieces.append([over_count(rows) for rows in piece])
+    total = rows_ref.shape[0]
+    rows = [rows_ref[at : at + 8, :] for at in range(0, total, 8)]
+    rows = put(names, grps, tiles, per, pieces, rows)
+    keep = [keep_ref[at : at + 8, :] for at in range(0, total, 8)]
+    left = [row * jnp.concatenate([k, k, k], axis=1) for row, k in zip(rows, keep)]
+    left = jnp.concatenate(left, axis=0).astype(BF16)
+    columns = total // per
     copies = []
     for i, lo in enumerate(range(0, LAGS, LAG_STEP)):
         hi = min(lo + LAG_STEP, LAGS)
-        late = jnp.dot(left, basis_ref[:, lo:hi], preferred_element_type=F32)
-        half = iota((8, hi - lo), 0) >> 2
+        series = jnp.dot(left, basis_ref[:, lo:hi], preferred_element_type=F32).astype(BF16)
         for s in range(per):
-            rows = []
-            for b in range(blocks):
-                at = (s * blocks + b) * 8
-                row = series_ref[at : at + 8, lo:hi]
-                for p, (place, there) in enumerate(places):
-                    fit = (half + 2 * b) == place
-                    fit = fit if there is None else fit & there
-                    row = jnp.where(fit, late[(p * per + s) * 8 : (p * per + s) * 8 + 8], row)
-                rows.append(row * keep_ref[at : at + 8, :1])
-            result[s, :, lo:hi] = jnp.concatenate(rows, axis=0).astype(BF16)
+            result[s, :, lo:hi] = series[s * columns : (s + 1) * columns]
         here = (slice(None), slice(None), slice(lo, hi))
         copies.append(pltpu.make_async_copy(result.at[here], out_ref.at[here], sems.at[i]))
         copies[-1].start()
@@ -431,18 +443,26 @@
             out_specs=(vmem,) * grps,
         )
         passed = [exchange(array, 1, 0) for array in passed]
-        series, keep = call(
+        early, keep = call(
             lambda *refs: early_kernel(per, seg, grps, tiles, soon, *refs),
             "early",
-            [mask, basis, spread, first, *aside],
-            out_shape=(pltpu.VMEM((rows, LAGS), F32), pltpu.VMEM((rows, LANE), F32)),
+            [mask, spread, first, *aside],
+            out_shape=(pltpu.VMEM((rows, WIDE), F32), pltpu.VMEM((rows, LANE), F32)),
             out_specs=(vmem,) * 2,
             scratch_shapes=[pltpu.VMEM((max(len(soon), 1), lines, WIDE), F32)],
+            cost_estimate=pl.CostEstimate(flops=100000000000, transcendentals=0, bytes_accessed=1000000000),
+        )
+        early = call(
+            lambda *refs: middle_kernel(per, seg, grps, tiles, late[grps:], *refs),
+            "middle",
+            [spread, early, *passed],
+            out_shape=pltpu.VMEM((rows, WIDE), F32),
+            out_specs=vmem,
         )
         return call(
-            lambda *refs: lags_kernel(per, seg, grps, tiles, late, *refs),
+            lambda *refs: lags_kernel(per, seg, grps, tiles, late[:grps], *refs),
             "lags",
-            [basis, keep, spread, series, *far, *passed],
+            [basis, keep, spread, early, *far],
             out_shape=jax.ShapeDtypeStruct((per, columns, LAGS), BF16),
             out_specs=hbm,
             scratch_shapes=[

time: 10.9 us -> 10.6 us (0.972)
  Pallas kernels: 4.45 us -> 4.12 us
    pallas_call x4 -> x5, Pallas kernels: 2.56 us -> 2.23 us  [call(): pl.pallas_call(kernel, in_specs=[vmem] * len(inputs), compiler_params=plt...]
  transfers between devices with their start and end apart: 5 -> 5, of which waited for: 2 -> 4; matrix products, arithmetic and copies ran while one was open for 0% -> 0% of each run, Pallas kernels for 10% -> 9%
where the time goes in v10:
time: 10.6 us; the launch traced here: 10.5 us
  starting transfers between devices  5.03 us (47%)
  Pallas kernels  4.12 us (39%)
  waiting for transfers between devices  1.29 us (12%)
    ppermute x5, starting transfers between devices, exchange(): return lax.ppermute(array, axes, pairs)  5.03 us
    pallas_call x5, Pallas kernels, call(): pl.pallas_call(kernel, in_specs=[vmem] * len(inputs), compiler_params=plt...  2.23 us
    pallas_call x1, Pallas kernels, on_device(): pl.pallas_call(lambda *refs: spectra_kernel(per, seg, samples, [1] + [way...  1.89 us
    ppermute x5, waiting for transfers between devices, exchange(): return lax.ppermute(array, axes, pairs)  1.29 us
  transfers between devices with their start and end apart: 5, of which 4 were waited for; matrix products, arithmetic and copies ran while one was open for 0% of the time, Pallas kernels for 9%

profile of v10, /device:TPU:3, one launch (start us, length us, event | category | flops | bytes accessed | tf_op | source)
XLA Modules:
  0.0 10.5 jit_solution(15994005828432285800)
XLA Ops:
  0.0 1.9 %spectra.1 = (bf16[64,384]{1,0:T(8,128)(2,1)S(1)}, bf16[64,384]{1,0:T(8,128)(2,1)S(1)}, bf16[64,384]{1,0:T(8,128)(2,1)S(1)}, bf16[64,384]{1,0:T(8,128)(2,1)S(1)}...) custom-call(s32[1,2,4]{2,1,0:T(2,128)} %refs_0_.1, s32[1,2]{1,0:T(1,128)} %refs_1_.1, ...), custom_call_target="tpu_custom_call" | custom-call | tf_op jit(solution)/shard_map/spectra/pallas_call | solution.py:404
  1.9 1.9 %collective-permute-start = (bf16[64,384]{1,0:T(8,128)(2,1)S(1)}, bf16[64,384]{1,0:T(8,128)(2,1)S(1)}, u32[]{:S(2)}, u32[]{:S(2)}) collective-permute-start(bf16[64,384]{1,0:T(8,128)(2,1)S(1)} %get-tuple-element.23), channel_id=1, source_target_pairs={{0,3},{1,2},{2,1},{3,0},{4,7},{5,6},{6,5},{7,4},{8,11},{9,10},{10,... | collective-permute-start | bytes 147464 | tf_op jit(solution)/shard_map/ppermute | solution.py:382
  3.8 1.1 %collective-permute-start.3 = (bf16[64,384]{1,0:T(8,128)(2,1)S(1)}, bf16[64,384]{1,0:T(8,128)(2,1)S(1)}, u32[]{:S(2)}, u32[]{:S(2)}) collective-permute-start(bf16[64,384]{1,0:T(8,128)(2,1)S(1)} %get-tuple-element.29), channel_id=1, source_target_pairs={{0,1},{1,0},{2,5},{3,4},{4,3},{5,2},{6,9},{7,8},{8,7},{9,6},{10,13... | collective-permute-start | bytes 147464 | tf_op jit(solution)/shard_map/ppermute | solution.py:382
  4.8 1.5 %collective-permute-start.4 = (bf16[64,384]{1,0:T(8,128)(2,1)S(1)}, bf16[64,384]{1,0:T(8,128)(2,1)S(1)}, u32[]{:S(2)}, u32[]{:S(2)}) collective-permute-start(bf16[64,384]{1,0:T(8,128)(2,1)S(1)} %get-tuple-element.30), channel_id=1, source_target_pairs={{0,1},{1,0},{2,4},{3,5},{4,2},{5,3},{6,8},{7,9},{8,6},{9,7},{10,12... | collective-permute-start | bytes 147464 | tf_op jit(solution)/shard_map/ppermute | solution.py:382
  6.4 0.3 %ready.1 = (f32[256,512]{1,0:T(8,128)S(1)}, f32[32,512]{1,0:T(8,128)S(1)}) custom-call(bf16[64,384]{1,0:T(8,128)(2,1)S(1)} %get-tuple-element.20.refs_0_), custom_call_target="tpu_custom_call" | custom-call | tf_op jit(solution)/shard_map/ready/pallas_call | solution.py:385
  6.6 0.0 collective-permute-done.refs_3_.refs_0_
  6.7 0.1 collective-permute-start.1
  6.7 0.5 %collective-permute-start.2 = (bf16[64,384]{1,0:T(8,128)(2,1)S(1)}, bf16[64,384]{1,0:T(8,128)(2,1)S(1)}, u32[]{:S(2)}, u32[]{:S(2)}) collective-permute-start(bf16[64,384]{1,0:T(8,128)(2,1)S(1)} %get-tuple-element.28), channel_id=1, source_target_pairs={{0,2},{1,3},{2,0},{3,1},{4,6},{5,7},{6,4},{7,5},{8,10},{9,11},{10,... | collective-permute-start | bytes 147464 | tf_op jit(solution)/shard_map/ppermute | solution.py:382
  7.2 0.5 %early.1 = (f32[96,384]{1,0:T(8,128)S(1)}, f32[96,128]{1,0:T(8,128)S(1)}) custom-call(s32[4,24]{1,0:T(4,128)S(1)} %get-tuple-element.19.refs_0_, f32[256,512]{1,0:T(8,128)S(1)} %get-tuple-element.21.refs_1_.refs_0_.refs_2_, f32[32,512]{1,0:T(8,128)S(1)} %get-tuple-element.22.refs_2_._, bf16[64,384]{1,0:T(8,128)(2,1)S(1)} %collective-permute-done.refs_3_.refs_0_), custom_call_target="tpu_custom_call" | custom-call | flops 99999997952 | bytes 1000000000 | tf_op jit(solution)/shard_map/early/pallas_call | solution.py:385
  7.7 0.2 %collective-permute-done.1.refs_2_ = bf16[64,384]{1,0:T(8,128)(2,1)S(1)} collective-permute-done((bf16[64,384]{1,0:T(8,128)(2,1)S(1)}, bf16[64,384]{1,0:T(8,128)(2,1)S(1)}, u32[]{:S(2)}, u32[]{:S(2)}) %collective-permute-start.1) | collective-permute-done | bytes 49184 | tf_op jit(solution)/shard_map/ppermute | solution.py:382
  8.0 0.2 %collective-permute-done.2.refs_3_ = bf16[64,384]{1,0:T(8,128)(2,1)S(1)} collective-permute-done((bf16[64,384]{1,0:T(8,128)(2,1)S(1)}, bf16[64,384]{1,0:T(8,128)(2,1)S(1)}, u32[]{:S(2)}, u32[]{:S(2)}) %collective-permute-start.2) | collective-permute-done | bytes 49184 | tf_op jit(solution)/shard_map/ppermute | solution.py:382
  8.1 0.2 %middle.1.refs_3_ = f32[96,384]{1,0:T(8,128)S(1)} custom-call(f32[256,512]{1,0:T(8,128)S(1)} %get-tuple-element.21.refs_1_.refs_0_.refs_2_, f32[96,384]{1,0:T(8,128)S(1)} %get-tuple-element.25.refs_1_, bf16[64,384]{1,0:T(8,128)(2,1)S(1)} %collective-permute-done.1.refs_2_, bf16[64,384]{1,0:T(8,128)(2,1)S(1)} %collective-permute-done.2.refs_3_), custom_call_target="tpu_custom_call" | custom-call | tf_op jit(solution)/shard_map/middle/pallas_call | solution.py:385
  8.3 0.7 %collective-permute-done.3.refs_4_ = bf16[64,384]{1,0:T(8,128)(2,1)S(1)} collective-permute-done((bf16[64,384]{1,0:T(8,128)(2,1)S(1)}, bf16[64,384]{1,0:T(8,128)(2,1)S(1)}, u32[]{:S(2)}, u32[]{:S(2)}) %collective-permute-start.3) | collective-permute-done | bytes 49184 | tf_op jit(solution)/shard_map/ppermute | solution.py:382
  9.1 0.2 %collective-permute-done.4.refs_5_ = bf16[64,384]{1,0:T(8,128)(2,1)S(1)} collective-permute-done((bf16[64,384]{1,0:T(8,128)(2,1)S(1)}, bf16[64,384]{1,0:T(8,128)(2,1)S(1)}, u32[]{:S(2)}, u32[]{:S(2)}) %collective-permute-start.4) | collective-permute-done | bytes 49184 | tf_op jit(solution)/shard_map/ppermute | solution.py:382
  9.2 1.2 %lags.1 = bf16[4,24,2001]{2,1,0:T(8,128)(2,1)} custom-call(bf16[384,2001]{1,0:T(8,128)(2,1)S(1)} %get-tuple-element.18.refs_0_, f32[96,128]{1,0:T(8,128)S(1)} %get-tuple-element.24.refs_1_, f32[256,512]{1,0:T(8,128)S(1)} %get-tuple-element.21.refs_1_.refs_0_.refs_2_, f32[96,384]{1,0:T(8,128)S(1)} %middle.1.refs_3_, ...), custom_call_target="tpu_custom_call" | custom-call | tf_op jit(solution)/shard_map/lags/pallas_call | solution.py:385
  (1 shorter events, 0.0 us)
Async XLA Ops:
  1.9 4.7 %collective-permute-start = (bf16[64,384]{1,0:T(8,128)(2,1)S(1)}, bf16[64,384]{1,0:T(8,128)(2,1)S(1)}, u32[]{:S(2)}, u32[]{:S(2)}) collective-permute-start(bf16[64,384]{1,0:T(8,128)(2,1)S(1)} %get-tuple-element.23), channel_id=1, source_target_pairs={{0,3},{1,2},{2,1},{3,0},{4,7},{5,6},{6,5},{7,4},{8,11},{9,10},{10,... | collective-permute-start | bytes 147464 | tf_op jit(solution)/shard_map/ppermute | solution.py:382
  3.8 5.3 %collective-permute-start.3 = (bf16[64,384]{1,0:T(8,128)(2,1)S(1)}, bf16[64,384]{1,0:T(8,128)(2,1)S(1)}, u32[]{:S(2)}, u32[]{:S(2)}) collective-permute-start(bf16[64,384]{1,0:T(8,128)(2,1)S(1)} %get-tuple-element.29), channel_id=1, source_target_pairs={{0,1},{1,0},{2,5},{3,4},{4,3},{5,2},{6,9},{7,8},{8,7},{9,6},{10,13... | collective-permute-start | bytes 147464 | tf_op jit(solution)/shard_map/ppermute | solution.py:382
  4.8 4.4 %collective-permute-start.4 = (bf16[64,384]{1,0:T(8,128)(2,1)S(1)}, bf16[64,384]{1,0:T(8,128)(2,1)S(1)}, u32[]{:S(2)}, u32[]{:S(2)}) collective-permute-start(bf16[64,384]{1,0:T(8,128)(2,1)S(1)} %get-tuple-element.30), channel_id=1, source_target_pairs={{0,1},{1,0},{2,4},{3,5},{4,2},{5,3},{6,8},{7,9},{8,6},{9,7},{10,12... | collective-permute-start | bytes 147464 | tf_op jit(solution)/shard_map/ppermute | solution.py:382
  6.7 1.3 %collective-permute-start.1 = (bf16[64,384]{1,0:T(8,128)(2,1)S(1)}, bf16[64,384]{1,0:T(8,128)(2,1)S(1)}, u32[]{:S(2)}, u32[]{:S(2)}) collective-permute-start(bf16[64,384]{1,0:T(8,128)(2,1)S(1)} %get-tuple-element.27), channel_id=1, source_target_pairs={{0,2},{1,3},{2,0},{3,1},{4,6},{5,7},{6,4},{7,5},{8,10},{9,11},{10,... | collective-permute-start | bytes 147464 | tf_op jit(solution)/shard_map/ppermute | solution.py:382
  6.7 1.4 %collective-permute-start.2 = (bf16[64,384]{1,0:T(8,128)(2,1)S(1)}, bf16[64,384]{1,0:T(8,128)(2,1)S(1)}, u32[]{:S(2)}, u32[]{:S(2)}) collective-permute-start(bf16[64,384]{1,0:T(8,128)(2,1)S(1)} %get-tuple-element.28), channel_id=1, source_target_pairs={{0,2},{1,3},{2,0},{3,1},{4,6},{5,7},{6,4},{7,5},{8,10},{9,11},{10,... | collective-permute-start | bytes 147464 | tf_op jit(solution)/shard_map/ppermute | solution.py:382

commit v11 on v10

--- a/solution.py
+++ b/solution.py
@@ -326,35 +326,53 @@
     rows_ref[...] = jnp.concatenate(put(((0, 0), *names), grps, tiles, per, pieces, rows), axis=0)
 
 
-def middle_kernel(per, seg, grps, tiles, names, spread_ref, early_ref, *refs):
-    *came, rows_ref = refs
-    pieces = []
-    for i in range(0, len(came), TOGETHER):
-        for piece in stacked(per, per * seg, spread_ref, came[i : i + TOGETHER]):
-            pieces.append([over_count(rows) for rows in piece])
+def middle_kernel(per, seg, grps, tiles, names, basis_ref, keep_ref, spread_ref, early_ref, *refs):
+    *came, series_ref = refs
+    pieces = [[over_count(rows) for rows in piece] for piece in stacked(per, per * seg, spread_ref, came)]
     rows = [early_ref[at : at + 8, :] for at in range(0, early_ref.shape[0], 8)]
-    rows_ref[...] = jnp.concatenate(put(names, grps, tiles, per, pieces, rows), axis=0)
-
-
-def lags_kernel(per, seg, grps, tiles, names, basis_ref, keep_ref, spread_ref, rows_ref, *refs):
+    rows = put(names, grps, tiles, per, pieces, rows)
+    left = [masked(row, keep_ref[8 * i : 8 * i + 8, :]) for i, row in enumerate(rows)]
+    left = jnp.concatenate(left, axis=0).astype(BF16)
+    series_ref[...] = jnp.dot(left, basis_ref[...], preferred_element_type=F32)
+
+
+def masked(row, keep):
+    return row * jnp.concatenate([keep] * (WIDE // LANE), axis=1)
+
+
+def lags_kernel(per, seg, grps, tiles, names, basis_ref, keep_ref, spread_ref, series_ref, *refs):
     *came, out_ref, result, sems = refs
-    pieces = []
-    for i in range(0, len(came), TOGETHER):
-        for piece in stacked(per, per * seg, spread_ref, came[i : i + TOGETHER]):
-            pieces.append([over_count(rows) for rows in piece])
-    total = rows_ref.shape[0]
-    rows = [rows_ref[at : at + 8, :] for at in range(0, total, 8)]
-    rows = put(names, grps, tiles, per, pieces, rows)
-    keep = [keep_ref[at : at + 8, :] for at in range(0, total, 8)]
-    left = [row * jnp.concatenate([k, k, k], axis=1) for row, k in zip(rows, keep)]
+    blocks = 3 * grps // 2
+    half = iota((8, WIDE), 0) >> 2
+    left, places = [], []
+    for i in range(0, grps, 2):
+        one, two = stacked(per, per * seg, spread_ref, came[i : i + 2])
+        (first, there), (second, _) = (place_of(name, grps, tiles) for name in names[i : i + 2])
+        places.append((first, second, there))
+        for s in range(per):
+            row = jnp.where(half == (first & 1), over_count(one[s]), over_count(two[s]))
+            keep = jnp.zeros((8, LANE), F32)
+            for b in range(blocks):
+                at = (s * blocks + b) * 8
+                here = (half[:, :LANE] + 2 * b == first) | (half[:, :LANE] + 2 * b == second)
+                keep = jnp.where(here, keep_ref[at : at + 8, :], keep)
+            left.append(masked(row, keep))
     left = jnp.concatenate(left, axis=0).astype(BF16)
-    columns = total // per
     copies = []
     for i, lo in enumerate(range(0, LAGS, LAG_STEP)):
         hi = min(lo + LAG_STEP, LAGS)
-        series = jnp.dot(left, basis_ref[:, lo:hi], preferred_element_type=F32).astype(BF16)
+        late = jnp.dot(left, basis_ref[:, lo:hi], preferred_element_type=F32)
+        half = iota((8, hi - lo), 0) >> 2
         for s in range(per):
-            result[s, :, lo:hi] = series[s * columns : (s + 1) * columns]
+            rows = []
+            for b in range(blocks):
+                at = (s * blocks + b) * 8
+                row = series_ref[at : at + 8, lo:hi]
+                for p, (first, second, there) in enumerate(places):
+                    here = ((half + 2 * b == first) | (half + 2 * b == second)) & there
+                    row = jnp.where(here, late[(p * per + s) * 8 : (p * per + s) * 8 + 8], row)
+                rows.append(row)
+            result[s, :, lo:hi] = jnp.concatenate(rows, axis=0).astype(BF16)
         here = (slice(None), slice(None), slice(lo, hi))
         copies.append(pltpu.make_async_copy(result.at[here], out_ref.at[here], sems.at[i]))
         copies[-1].start()
@@ -452,17 +470,17 @@
             scratch_shapes=[pltpu.VMEM((max(len(soon), 1), lines, WIDE), F32)],
             cost_estimate=pl.CostEstimate(flops=100000000000, transcendentals=0, bytes_accessed=1000000000),
         )
-        early = call(
+        series = call(
             lambda *refs: middle_kernel(per, seg, grps, tiles, late[grps:], *refs),
             "middle",
-            [spread, early, *passed],
-            out_shape=pltpu.VMEM((rows, WIDE), F32),
+            [basis, keep, spread, early, *passed],
+            out_shape=pltpu.VMEM((rows, LAGS), F32),
             out_specs=vmem,
         )
         return call(
             lambda *refs: lags_kernel(per, seg, grps, tiles, late[:grps], *refs),
             "lags",
-            [basis, keep, spread, early, *far],
+            [basis, keep, spread, series, *far],
             out_shape=jax.ShapeDtypeStruct((per, columns, LAGS), BF16),
             out_specs=hbm,
             scratch_shapes=[

time: 10.6 us -> 10.6 us (level)
  waiting for transfers between devices: 1.29 us -> 0.95 us
  Pallas kernels: 4.12 us -> 4.41 us
    ppermute x5, waiting for transfers between devices: 1.29 us -> 0.95 us  [exchange(): return lax.ppermute(array, axes, pairs)]
    pallas_call x5, Pallas kernels: 2.23 us -> 2.52 us  [call(): pl.pallas_call(kernel, in_specs=[vmem] * len(inputs), compiler_params=plt...]
  transfers between devices with their start and end apart: 5 -> 5, of which waited for: 4 -> 4; matrix products, arithmetic and copies ran while one was open for 0% -> 0% of each run, Pallas kernels for 9% -> 13%
where the time goes in v11:
time: 10.6 us; the launch traced here: 10.4 us
  starting transfers between devices  5.03 us (47%)
  Pallas kernels  4.41 us (42%)
  waiting for transfers between devices  0.95 us (9%)
    ppermute x5, starting transfers between devices, exchange(): return lax.ppermute(array, axes, pairs)  5.03 us
    pallas_call x5, Pallas kernels, call(): pl.pallas_call(kernel, in_specs=[vmem] * len(inputs), compiler_params=plt...  2.52 us
    pallas_call x1, Pallas kernels, on_device(): pl.pallas_call(lambda *refs: spectra_kernel(per, seg, samples, [1] + [way...  1.89 us
    ppermute x5, waiting for transfers between devices, exchange(): return lax.ppermute(array, axes, pairs)  0.95 us
  transfers between devices with their start and end apart: 5, of which 4 were waited for; matrix products, arithmetic and copies ran while one was open for 0% of the time, Pallas kernels for 13%

profile of v11, /device:TPU:3, one launch (start us, length us, event | category | flops | bytes accessed | tf_op | source)
XLA Modules:
  0.0 10.4 jit_solution(7634157327864342599)
XLA Ops:
  0.0 1.9 %spectra.1 = (bf16[64,384]{1,0:T(8,128)(2,1)S(1)}, bf16[64,384]{1,0:T(8,128)(2,1)S(1)}, bf16[64,384]{1,0:T(8,128)(2,1)S(1)}, bf16[64,384]{1,0:T(8,128)(2,1)S(1)}...) custom-call(s32[1,2,4]{2,1,0:T(2,128)} %refs_0_.1, s32[1,2]{1,0:T(1,128)} %refs_1_.1, ...), custom_call_target="tpu_custom_call" | custom-call | tf_op jit(solution)/shard_map/spectra/pallas_call | solution.py:422
  1.9 1.9 %collective-permute-start = (bf16[64,384]{1,0:T(8,128)(2,1)S(1)}, bf16[64,384]{1,0:T(8,128)(2,1)S(1)}, u32[]{:S(2)}, u32[]{:S(2)}) collective-permute-start(bf16[64,384]{1,0:T(8,128)(2,1)S(1)} %get-tuple-element.23), channel_id=1, source_target_pairs={{0,3},{1,2},{2,1},{3,0},{4,7},{5,6},{6,5},{7,4},{8,11},{9,10},{10,... | collective-permute-start | bytes 147464 | tf_op jit(solution)/shard_map/ppermute | solution.py:400
  3.8 1.1 %collective-permute-start.3 = (bf16[64,384]{1,0:T(8,128)(2,1)S(1)}, bf16[64,384]{1,0:T(8,128)(2,1)S(1)}, u32[]{:S(2)}, u32[]{:S(2)}) collective-permute-start(bf16[64,384]{1,0:T(8,128)(2,1)S(1)} %get-tuple-element.29), channel_id=1, source_target_pairs={{0,1},{1,0},{2,5},{3,4},{4,3},{5,2},{6,9},{7,8},{8,7},{9,6},{10,13... | collective-permute-start | bytes 147464 | tf_op jit(solution)/shard_map/ppermute | solution.py:400
  4.8 1.5 %collective-permute-start.4 = (bf16[64,384]{1,0:T(8,128)(2,1)S(1)}, bf16[64,384]{1,0:T(8,128)(2,1)S(1)}, u32[]{:S(2)}, u32[]{:S(2)}) collective-permute-start(bf16[64,384]{1,0:T(8,128)(2,1)S(1)} %get-tuple-element.30), channel_id=1, source_target_pairs={{0,1},{1,0},{2,4},{3,5},{4,2},{5,3},{6,8},{7,9},{8,6},{9,7},{10,12... | collective-permute-start | bytes 147464 | tf_op jit(solution)/shard_map/ppermute | solution.py:400
  6.4 0.3 %ready.1 = (f32[256,512]{1,0:T(8,128)S(1)}, f32[32,512]{1,0:T(8,128)S(1)}) custom-call(bf16[64,384]{1,0:T(8,128)(2,1)S(1)} %get-tuple-element.20.refs_0_), custom_call_target="tpu_custom_call" | custom-call | tf_op jit(solution)/shard_map/ready/pallas_call | solution.py:403
  6.6 0.0 collective-permute-done.refs_3_.refs_0_
  6.7 0.1 collective-permute-start.1
  6.7 0.5 %collective-permute-start.2 = (bf16[64,384]{1,0:T(8,128)(2,1)S(1)}, bf16[64,384]{1,0:T(8,128)(2,1)S(1)}, u32[]{:S(2)}, u32[]{:S(2)}) collective-permute-start(bf16[64,384]{1,0:T(8,128)(2,1)S(1)} %get-tuple-element.28), channel_id=1, source_target_pairs={{0,2},{1,3},{2,0},{3,1},{4,6},{5,7},{6,4},{7,5},{8,10},{9,11},{10,... | collective-permute-start | bytes 147464 | tf_op jit(solution)/shard_map/ppermute | solution.py:400
  7.2 0.5 %early.1 = (f32[96,384]{1,0:T(8,128)S(1)}, f32[96,128]{1,0:T(8,128)S(1)}) custom-call(s32[4,24]{1,0:T(4,128)S(1)} %get-tuple-element.19.refs_0_, f32[256,512]{1,0:T(8,128)S(1)} %get-tuple-element.21.refs_1_.refs_2_, f32[32,512]{1,0:T(8,128)S(1)} %get-tuple-element.22.refs_2_._, bf16[64,384]{1,0:T(8,128)(2,1)S(1)} %collective-permute-done.refs_3_.refs_0_), custom_call_target="tpu_custom_call" | custom-call | flops 99999997952 | bytes 1000000000 | tf_op jit(solution)/shard_map/early/pallas_call | solution.py:403
  7.7 0.2 %collective-permute-done.1.refs_4_ = bf16[64,384]{1,0:T(8,128)(2,1)S(1)} collective-permute-done((bf16[64,384]{1,0:T(8,128)(2,1)S(1)}, bf16[64,384]{1,0:T(8,128)(2,1)S(1)}, u32[]{:S(2)}, u32[]{:S(2)}) %collective-permute-start.1) | collective-permute-done | bytes 49184 | tf_op jit(solution)/shard_map/ppermute | solution.py:400
  8.0 0.2 %collective-permute-done.2.refs_5_ = bf16[64,384]{1,0:T(8,128)(2,1)S(1)} collective-permute-done((bf16[64,384]{1,0:T(8,128)(2,1)S(1)}, bf16[64,384]{1,0:T(8,128)(2,1)S(1)}, u32[]{:S(2)}, u32[]{:S(2)}) %collective-permute-start.2) | collective-permute-done | bytes 49184 | tf_op jit(solution)/shard_map/ppermute | solution.py:400
  8.1 0.6 %middle.1.refs_3_ = f32[96,2001]{1,0:T(8,128)S(1)} custom-call(bf16[384,2001]{1,0:T(8,128)(2,1)S(1)} %get-tuple-element.18.refs_0_, f32[96,128]{1,0:T(8,128)S(1)} %get-tuple-element.24.refs_1_, f32[256,512]{1,0:T(8,128)S(1)} %get-tuple-element.21.refs_1_.refs_2_, f32[96,384]{1,0:T(8,128)S(1)} %get-tuple-element.25.refs_3_, ...), custom_call_target="tpu_custom_call" | custom-call | tf_op jit(solution)/shard_map/middle/pallas_call | solution.py:403
  8.7 0.4 %collective-permute-done.3.refs_4_ = bf16[64,384]{1,0:T(8,128)(2,1)S(1)} collective-permute-done((bf16[64,384]{1,0:T(8,128)(2,1)S(1)}, bf16[64,384]{1,0:T(8,128)(2,1)S(1)}, u32[]{:S(2)}, u32[]{:S(2)}) %collective-permute-start.3) | collective-permute-done | bytes 49184 | tf_op jit(solution)/shard_map/ppermute | solution.py:400
  9.1 0.2 %collective-permute-done.4.refs_5_ = bf16[64,384]{1,0:T(8,128)(2,1)S(1)} collective-permute-done((bf16[64,384]{1,0:T(8,128)(2,1)S(1)}, bf16[64,384]{1,0:T(8,128)(2,1)S(1)}, u32[]{:S(2)}, u32[]{:S(2)}) %collective-permute-start.4) | collective-permute-done | bytes 49184 | tf_op jit(solution)/shard_map/ppermute | solution.py:400
  9.2 1.2 %lags.1 = bf16[4,24,2001]{2,1,0:T(8,128)(2,1)} custom-call(bf16[384,2001]{1,0:T(8,128)(2,1)S(1)} %get-tuple-element.18.refs_0_, f32[96,128]{1,0:T(8,128)S(1)} %get-tuple-element.24.refs_1_, f32[256,512]{1,0:T(8,128)S(1)} %get-tuple-element.21.refs_1_.refs_2_, f32[96,2001]{1,0:T(8,128)S(1)} %middle.1.refs_3_, ...), custom_call_target="tpu_custom_call" | custom-call | tf_op jit(solution)/shard_map/lags/pallas_call | solution.py:403
  (1 shorter events, 0.0 us)
Async XLA Ops:
  1.9 4.7 %collective-permute-start = (bf16[64,384]{1,0:T(8,128)(2,1)S(1)}, bf16[64,384]{1,0:T(8,128)(2,1)S(1)}, u32[]{:S(2)}, u32[]{:S(2)}) collective-permute-start(bf16[64,384]{1,0:T(8,128)(2,1)S(1)} %get-tuple-element.23), channel_id=1, source_target_pairs={{0,3},{1,2},{2,1},{3,0},{4,7},{5,6},{6,5},{7,4},{8,11},{9,10},{10,... | collective-permute-start | bytes 147464 | tf_op jit(solution)/shard_map/ppermute | solution.py:400
  3.8 5.3 %collective-permute-start.3 = (bf16[64,384]{1,0:T(8,128)(2,1)S(1)}, bf16[64,384]{1,0:T(8,128)(2,1)S(1)}, u32[]{:S(2)}, u32[]{:S(2)}) collective-permute-start(bf16[64,384]{1,0:T(8,128)(2,1)S(1)} %get-tuple-element.29), channel_id=1, source_target_pairs={{0,1},{1,0},{2,5},{3,4},{4,3},{5,2},{6,9},{7,8},{8,7},{9,6},{10,13... | collective-permute-start | bytes 147464 | tf_op jit(solution)/shard_map/ppermute | solution.py:400
  4.8 4.4 %collective-permute-start.4 = (bf16[64,384]{1,0:T(8,128)(2,1)S(1)}, bf16[64,384]{1,0:T(8,128)(2,1)S(1)}, u32[]{:S(2)}, u32[]{:S(2)}) collective-permute-start(bf16[64,384]{1,0:T(8,128)(2,1)S(1)} %get-tuple-element.30), channel_id=1, source_target_pairs={{0,1},{1,0},{2,4},{3,5},{4,2},{5,3},{6,8},{7,9},{8,6},{9,7},{10,12... | collective-permute-start | bytes 147464 | tf_op jit(solution)/shard_map/ppermute | solution.py:400
  6.7 1.3 %collective-permute-start.1 = (bf16[64,384]{1,0:T(8,128)(2,1)S(1)}, bf16[64,384]{1,0:T(8,128)(2,1)S(1)}, u32[]{:S(2)}, u32[]{:S(2)}) collective-permute-start(bf16[64,384]{1,0:T(8,128)(2,1)S(1)} %get-tuple-element.27), channel_id=1, source_target_pairs={{0,2},{1,3},{2,0},{3,1},{4,6},{5,7},{6,4},{7,5},{8,10},{9,11},{10,... | collective-permute-start | bytes 147464 | tf_op jit(solution)/shard_map/ppermute | solution.py:400
  6.7 1.4 %collective-permute-start.2 = (bf16[64,384]{1,0:T(8,128)(2,1)S(1)}, bf16[64,384]{1,0:T(8,128)(2,1)S(1)}, u32[]{:S(2)}, u32[]{:S(2)}) collective-permute-start(bf16[64,384]{1,0:T(8,128)(2,1)S(1)} %get-tuple-element.28), channel_id=1, source_target_pairs={{0,2},{1,3},{2,0},{3,1},{4,6},{5,7},{6,4},{7,5},{8,10},{9,11},{10,... | collective-permute-start | bytes 147464 | tf_op jit(solution)/shard_map/ppermute | solution.py:400

commit v12 on v11

--- a/solution.py
+++ b/solution.py
@@ -41,34 +41,58 @@
     return out
 
 
-def fourier_tables(samples):
-    bins = np.arange(1, NBIN + 1)
-    turn = np.pi / samples
+def round_to(rows):
+    return -(-rows // 8) * 8
+
+
+def fourier_rows(samples):
     stretches = -(-samples // STEP)
-
-    def angles(number):
-        return np.mod(number[:, None] * bins[None, :], 2 * samples) * turn
-
-    whole = angles(np.arange(stretches) * STEP)
-    coarse = angles(np.arange(STEP // FINE) * FINE)
-    fine = angles(np.arange(FINE))
-    number = np.arange(stretches * STEP)
-    taper = np.where(number < samples, 0.5 - 0.5 * np.cos(number * (2.0 * np.pi / samples)), 0.0)
-    parts = [
-        in_lanes(np.cos(whole), np.cos(whole)),
-        in_lanes(np.sin(whole), -np.sin(whole)),
-        np.pad(taper.reshape(stretches, STEP), ((0, 0), (0, WIDE - STEP))),
-        in_lanes(np.cos(coarse), -np.sin(coarse)),
-        in_lanes(-np.sin(coarse), -np.cos(coarse)),
-        in_lanes(np.cos(fine), np.cos(fine)),
-        in_lanes(np.sin(fine), np.sin(fine)),
-    ]
-    starts, rows = [], 0
-    for i, part in enumerate(parts):
-        parts[i] = np.pad(part, ((0, -len(part) % 8), (0, 0)))
-        starts.append(rows)
-        rows += len(parts[i])
-    return np.concatenate(parts).astype(np.float32), starts, stretches
+    sizes = [round_to(stretches)] * 3 + [STEP // FINE] * 2 + [FINE] * 2
+    return [sum(sizes[:i]) for i in range(len(sizes) + 1)], stretches
+
+
+def cos_sin(number, points):
+    number = number - points * jnp.floor((number + 0.5) * (1.0 / points))
+    turn = jnp.floor(number * (4.0 / points) + 0.5)
+    angle = (number - turn * (points / 4)) * (2.0 * np.pi / points)
+    square = angle * angle
+    sine = 1.0 / 120 + square * (-1.0 / 5040 + square * (1.0 / 362880))
+    sine = angle + angle * square * (-1.0 / 6 + square * sine)
+    cosine = 1.0 / 24 + square * (-1.0 / 720 + square * (1.0 / 40320))
+    cosine = 1.0 + square * (-0.5 + square * cosine)
+    odd = (turn == 1) | (turn == 3)
+    cosine, sine = jnp.where(odd, sine, cosine), jnp.where(odd, cosine, sine)
+    cosine = jnp.where((turn == 1) | (turn == 2), -cosine, cosine)
+    return cosine, jnp.where((turn == 2) | (turn == 3), -sine, sine)
+
+
+def fill_factors(factors, starts, samples):
+    points = 2 * samples
+
+    def of(rows, step):
+        lane = iota((rows, WIDE), 1)
+        tail = lane & (HALF - 1)
+        known = (lane < 2 * LANE) | (tail < TAIL)
+        imag = ((lane >= LANE) & (lane < 2 * LANE)) | (lane >= 2 * LANE + HALF)
+        bins = jnp.where(lane < 2 * LANE, lane & (LANE - 1), LANE + tail) + 1
+        cosine, sine = cos_sin((iota((rows, WIDE), 0) * step * bins).astype(F32), points)
+        return cosine, sine, imag, known
+
+    def put_rows(i, rows):
+        factors[starts[i] : starts[i + 1], :] = rows
+
+    cosine, sine, imag, _ = of(starts[1] - starts[0], STEP)
+    put_rows(0, cosine)
+    put_rows(1, jnp.where(imag, -sine, sine))
+    rows = starts[3] - starts[2]
+    number = iota((rows, WIDE), 0) * STEP + iota((rows, WIDE), 1)
+    put_rows(2, 0.5 - 0.5 * cos_sin((2 * number).astype(F32), points)[0])
+    cosine, sine, imag, known = of(STEP // FINE, FINE)
+    put_rows(3, jnp.where(known, jnp.where(imag, -sine, cosine), 0.0))
+    put_rows(4, jnp.where(known, jnp.where(imag, -cosine, -sine), 0.0))
+    cosine, sine, _, _ = of(FINE, 1)
+    put_rows(5, cosine)
+    put_rows(6, sine)
 
 
 def lag_table(samples):
@@ -110,13 +134,13 @@
 
 
 def spectra_kernel(
-    per, seg, samples, ways, starts, stretches, rows_hbm, count_hbm, valid_hbm, traces_hbm, factors_hbm, basis_hbm, mask_hbm,
+    per, seg, samples, ways, starts, stretches, rows_hbm, count_hbm, valid_hbm, traces_hbm, basis_hbm, mask_hbm,
     *refs,
 ):
-    mine_ref, *outs, basis_ref, mask_ref, rows_ref, count_ref, valid_ref, traces, factors, white_ref, order_ref, sems = refs
+    mine_ref, *outs, basis_ref, mask_ref, rows_ref, count_ref, valid_ref, traces, factors, table, window, white_ref, order_ref, sems = refs
     lines = per * seg
     pairs = [
-        (factors_hbm, factors), (traces_hbm, traces),
+        (traces_hbm, traces),
         (rows_hbm, rows_ref), (count_hbm, count_ref), (valid_hbm, valid_ref), (basis_hbm, basis_ref), (mask_hbm, mask_ref),
     ]
     copies = [pltpu.make_async_copy(src, dst, sems.at[i]) for i, (src, dst) in enumerate(pairs)]
@@ -135,9 +159,20 @@
     known_in, bin_in = bin_of(col)
     known_out, bin_out = bin_of(row)
     near_bins = jnp.abs(bin_in - bin_out) <= 4
-    window = jnp.where(known_in & known_out, jnp.where(near_bins, 17.0, 1.0), 0.0).astype(BF16)
-
-    for copy in copies[2:5]:
+    window[...] = jnp.where(known_in & known_out, jnp.where(near_bins, 17.0, 1.0), 0.0).astype(BF16)
+
+    fill_factors(factors, starts, samples)
+    turn_at, swap_at, taper_at, coarse_at, cross_at, fine_at, other_at = starts[:-1]
+    fine, other = factors[fine_at : fine_at + FINE, :], factors[other_at : other_at + FINE, :]
+    for i in range(STEP // FINE):
+        rows = factors[coarse_at + i : coarse_at + i + 1, :] * fine
+        rows = rows + factors[cross_at + i : cross_at + i + 1, :] * other
+        high = rows.astype(BF16)
+        low = (rows - high.astype(F32)).astype(BF16)
+        for k, part in enumerate((high, high, low)):
+            table[k * STEP + i * FINE : k * STEP + (i + 1) * FINE, :] = part
+
+    for copy in copies[1:4]:
         copy.wait()
     station, _ = divided(iota((lines, LANE), 0), seg)
     extra = jnp.zeros((lines, LANE), F32)
@@ -147,17 +182,6 @@
     usable = jnp.concatenate(column_of(valid_ref[...].astype(F32)), axis=0)
 
     copies[0].wait()
-    turn_at, swap_at, taper_at, coarse_at, cross_at, fine_at, other_at = starts
-    fine, other = factors[fine_at : fine_at + FINE, :], factors[other_at : other_at + FINE, :]
-    high, low = [], []
-    for i in range(STEP // FINE):
-        rows = factors[coarse_at + i : coarse_at + i + 1, :] * fine
-        rows = rows + factors[cross_at + i : cross_at + i + 1, :] * other
-        high.append(rows.astype(BF16))
-        low.append((rows - high[-1].astype(F32)).astype(BF16))
-    table = jnp.concatenate([*high, *high, *low], axis=0)
-
-    copies[1].wait()
     left = []
     for j in range(stretches):
         at = j * STEP
@@ -168,7 +192,7 @@
         x_high = x.astype(BF16)
         x_low = (x - x_high.astype(F32)).astype(BF16)
         left.append(jnp.concatenate([x_high, x_low, x_high], axis=1))
-    parts = jnp.dot(jnp.concatenate(left, axis=0), table, preferred_element_type=F32)
+    parts = jnp.dot(jnp.concatenate(left, axis=0), table[...], preferred_element_type=F32)
     real, imag, tail = (parts[:lines, k * LANE : (k + 1) * LANE] for k in range(3))
     for j in range(1, stretches):
         p_re, p_im, p_tail = (parts[j * lines : (j + 1) * lines, k * LANE : (k + 1) * LANE] for k in range(3))
@@ -181,8 +205,8 @@
     power = jnp.concatenate([real * real + imag * imag, tail * tail], axis=1)
     p_high = power.astype(BF16)
     p_low = (power - p_high.astype(F32)).astype(BF16)
-    level = jnp.dot(p_high, window, preferred_element_type=F32)
-    level = level + jnp.dot(p_low, window, preferred_element_type=F32)
+    level = jnp.dot(p_high, window[...], preferred_element_type=F32)
+    level = level + jnp.dot(p_low, window[...], preferred_element_type=F32)
     factor = usable / jnp.sqrt(level * (1.0 / (2 * NBIN)) + 1e-06)
     tail = tail * factor[:, LANE:]
     tail = jnp.where(iota((lines, LANE), 1) == VALID, usable, tail) + extra
@@ -204,7 +228,7 @@
     mine_ref[...] = own
     for ref, way in zip(outs, ways):
         ref[...] = (own, near, far, own)[way]
-    for copy in copies[5:]:
+    for copy in copies[4:]:
         copy.wait()
 
 
@@ -412,13 +436,13 @@
         per, seg, samples = traces.shape
         lines = per * seg
         columns = pair_mask.shape[1]
-        factors, starts, stretches = fourier_tables(samples)
+        starts, stretches = fourier_rows(samples)
         lag_basis = jnp.asarray(lag_table(samples))
         payload = pltpu.VMEM((lines, WIDE), BF16)
         sent = [(3, d) for d in range(1, grps)] + [(2, d) for d in reversed(range(grps))]
         soon = [(1, d) for d in range(1, grps)]
         late = [(2, d) for d in reversed(range(grps))] + [(1, 0)] + [(0, d) for d in range(1, grps)]
-        inputs = [boundary_rows, boundary_count, validity, traces.reshape(lines, samples), jnp.asarray(factors), lag_basis, pair_mask]
+        inputs = [boundary_rows, boundary_count, validity, traces.reshape(lines, samples), lag_basis, pair_mask]
         mine, near, *rest, basis, mask = pl.pallas_call(
             lambda *refs: spectra_kernel(
                 per, seg, samples, [1] + [way for way, _ in sent], starts, stretches, *refs
@@ -432,10 +456,12 @@
                 pltpu.SMEM(boundary_count.shape, jnp.int32),
                 pltpu.VMEM(validity.shape, jnp.int32),
                 pltpu.VMEM((lines, samples), F32),
-                pltpu.VMEM(factors.shape, F32),
+                pltpu.VMEM((starts[-1], WIDE), F32),
+                pltpu.VMEM((3 * STEP, WIDE), BF16),
+                pltpu.VMEM((2 * LANE, 2 * LANE), BF16),
                 pltpu.VMEM((per, seg, WIDE), F32),
                 pltpu.VMEM((3, lines, LANE), F32),
-                pltpu.SemaphoreType.DMA((7,)),
+                pltpu.SemaphoreType.DMA((6,)),
             ],
             compiler_params=pltpu.CompilerParams(vmem_limit_bytes=32 << 20),
             name="spectra",

time: 10.6 us -> 10.5 us (level)
  no operation moved by 1% of the time
where the time goes in v12:
time: 10.5 us; the launch traced here: 10.4 us
  starting transfers between devices  5.03 us (48%)
  Pallas kernels  4.33 us (41%)
  waiting for transfers between devices  0.95 us (9%)
    ppermute x5, starting transfers between devices, exchange(): return lax.ppermute(array, axes, pairs)  5.03 us
    pallas_call x5, Pallas kernels, call(): pl.pallas_call(kernel, in_specs=[vmem] * len(inputs), compiler_params=plt...  2.52 us
    pallas_call x1, Pallas kernels, on_device(): pl.pallas_call(lambda *refs: spectra_kernel(per, seg, samples, [1] + [way...  1.81 us
    ppermute x5, waiting for transfers between devices, exchange(): return lax.ppermute(array, axes, pairs)  0.95 us
  transfers between devices with their start and end apart: 5, of which 4 were waited for; matrix products, arithmetic and copies ran while one was open for 0% of the time, Pallas kernels for 13%

profile of v12, /device:TPU:3, one launch (start us, length us, event | category | flops | bytes accessed | tf_op | source)
XLA Modules:
  0.0 10.4 jit_solution(13668143433509389699)
XLA Ops:
  0.0 1.8 %spectra.1 = (bf16[64,384]{1,0:T(8,128)(2,1)S(1)}, bf16[64,384]{1,0:T(8,128)(2,1)S(1)}, bf16[64,384]{1,0:T(8,128)(2,1)S(1)}, bf16[64,384]{1,0:T(8,128)(2,1)S(1)}...) custom-call(s32[1,2,4]{2,1,0:T(2,128)} %refs_0_.1, s32[1,2]{1,0:T(1,128)} %refs_1_.1, ...), custom_call_target="tpu_custom_call" | custom-call | tf_op jit(solution)/shard_map/spectra/pallas_call | solution.py:446
  1.8 1.9 %collective-permute-start = (bf16[64,384]{1,0:T(8,128)(2,1)S(1)}, bf16[64,384]{1,0:T(8,128)(2,1)S(1)}, u32[]{:S(2)}, u32[]{:S(2)}) collective-permute-start(bf16[64,384]{1,0:T(8,128)(2,1)S(1)} %get-tuple-element.23), channel_id=1, source_target_pairs={{0,3},{1,2},{2,1},{3,0},{4,7},{5,6},{6,5},{7,4},{8,11},{9,10},{10,... | collective-permute-start | bytes 147464 | tf_op jit(solution)/shard_map/ppermute | solution.py:424
  3.7 1.1 %collective-permute-start.3 = (bf16[64,384]{1,0:T(8,128)(2,1)S(1)}, bf16[64,384]{1,0:T(8,128)(2,1)S(1)}, u32[]{:S(2)}, u32[]{:S(2)}) collective-permute-start(bf16[64,384]{1,0:T(8,128)(2,1)S(1)} %get-tuple-element.29), channel_id=1, source_target_pairs={{0,1},{1,0},{2,5},{3,4},{4,3},{5,2},{6,9},{7,8},{8,7},{9,6},{10,13... | collective-permute-start | bytes 147464 | tf_op jit(solution)/shard_map/ppermute | solution.py:424
  4.7 1.5 %collective-permute-start.4 = (bf16[64,384]{1,0:T(8,128)(2,1)S(1)}, bf16[64,384]{1,0:T(8,128)(2,1)S(1)}, u32[]{:S(2)}, u32[]{:S(2)}) collective-permute-start(bf16[64,384]{1,0:T(8,128)(2,1)S(1)} %get-tuple-element.30), channel_id=1, source_target_pairs={{0,1},{1,0},{2,4},{3,5},{4,2},{5,3},{6,8},{7,9},{8,6},{9,7},{10,12... | collective-permute-start | bytes 147464 | tf_op jit(solution)/shard_map/ppermute | solution.py:424
  6.3 0.3 %ready.1 = (f32[256,512]{1,0:T(8,128)S(1)}, f32[32,512]{1,0:T(8,128)S(1)}) custom-call(bf16[64,384]{1,0:T(8,128)(2,1)S(1)} %get-tuple-element.20.refs_0_), custom_call_target="tpu_custom_call" | custom-call | tf_op jit(solution)/shard_map/ready/pallas_call | solution.py:427
  6.6 0.0 collective-permute-done.refs_3_.refs_0_
  6.6 0.1 collective-permute-start.1
  6.7 0.5 %collective-permute-start.2 = (bf16[64,384]{1,0:T(8,128)(2,1)S(1)}, bf16[64,384]{1,0:T(8,128)(2,1)S(1)}, u32[]{:S(2)}, u32[]{:S(2)}) collective-permute-start(bf16[64,384]{1,0:T(8,128)(2,1)S(1)} %get-tuple-element.28), channel_id=1, source_target_pairs={{0,2},{1,3},{2,0},{3,1},{4,6},{5,7},{6,4},{7,5},{8,10},{9,11},{10,... | collective-permute-start | bytes 147464 | tf_op jit(solution)/shard_map/ppermute | solution.py:424
  7.2 0.5 %early.1 = (f32[96,384]{1,0:T(8,128)S(1)}, f32[96,128]{1,0:T(8,128)S(1)}) custom-call(s32[4,24]{1,0:T(4,128)S(1)} %get-tuple-element.19.refs_0_, f32[256,512]{1,0:T(8,128)S(1)} %get-tuple-element.21.refs_1_.refs_2_, f32[32,512]{1,0:T(8,128)S(1)} %get-tuple-element.22.refs_2_._, bf16[64,384]{1,0:T(8,128)(2,1)S(1)} %collective-permute-done.refs_3_.refs_0_), custom_call_target="tpu_custom_call" | custom-call | flops 99999997952 | bytes 1000000000 | tf_op jit(solution)/shard_map/early/pallas_call | solution.py:427
  7.6 0.2 %collective-permute-done.1.refs_4_ = bf16[64,384]{1,0:T(8,128)(2,1)S(1)} collective-permute-done((bf16[64,384]{1,0:T(8,128)(2,1)S(1)}, bf16[64,384]{1,0:T(8,128)(2,1)S(1)}, u32[]{:S(2)}, u32[]{:S(2)}) %collective-permute-start.1) | collective-permute-done | bytes 49184 | tf_op jit(solution)/shard_map/ppermute | solution.py:424
  7.9 0.2 %collective-permute-done.2.refs_5_ = bf16[64,384]{1,0:T(8,128)(2,1)S(1)} collective-permute-done((bf16[64,384]{1,0:T(8,128)(2,1)S(1)}, bf16[64,384]{1,0:T(8,128)(2,1)S(1)}, u32[]{:S(2)}, u32[]{:S(2)}) %collective-permute-start.2) | collective-permute-done | bytes 49184 | tf_op jit(solution)/shard_map/ppermute | solution.py:424
  8.0 0.6 %middle.1.refs_3_ = f32[96,2001]{1,0:T(8,128)S(1)} custom-call(bf16[384,2001]{1,0:T(8,128)(2,1)S(1)} %get-tuple-element.18.refs_0_, f32[96,128]{1,0:T(8,128)S(1)} %get-tuple-element.24.refs_1_, f32[256,512]{1,0:T(8,128)S(1)} %get-tuple-element.21.refs_1_.refs_2_, f32[96,384]{1,0:T(8,128)S(1)} %get-tuple-element.25.refs_3_, ...), custom_call_target="tpu_custom_call" | custom-call | tf_op jit(solution)/shard_map/middle/pallas_call | solution.py:427
  8.6 0.4 %collective-permute-done.3.refs_4_ = bf16[64,384]{1,0:T(8,128)(2,1)S(1)} collective-permute-done((bf16[64,384]{1,0:T(8,128)(2,1)S(1)}, bf16[64,384]{1,0:T(8,128)(2,1)S(1)}, u32[]{:S(2)}, u32[]{:S(2)}) %collective-permute-start.3) | collective-permute-done | bytes 49184 | tf_op jit(solution)/shard_map/ppermute | solution.py:424
  9.0 0.2 %collective-permute-done.4.refs_5_ = bf16[64,384]{1,0:T(8,128)(2,1)S(1)} collective-permute-done((bf16[64,384]{1,0:T(8,128)(2,1)S(1)}, bf16[64,384]{1,0:T(8,128)(2,1)S(1)}, u32[]{:S(2)}, u32[]{:S(2)}) %collective-permute-start.4) | collective-permute-done | bytes 49184 | tf_op jit(solution)/shard_map/ppermute | solution.py:424
  9.2 1.2 %lags.1 = bf16[4,24,2001]{2,1,0:T(8,128)(2,1)} custom-call(bf16[384,2001]{1,0:T(8,128)(2,1)S(1)} %get-tuple-element.18.refs_0_, f32[96,128]{1,0:T(8,128)S(1)} %get-tuple-element.24.refs_1_, f32[256,512]{1,0:T(8,128)S(1)} %get-tuple-element.21.refs_1_.refs_2_, f32[96,2001]{1,0:T(8,128)S(1)} %middle.1.refs_3_, ...), custom_call_target="tpu_custom_call" | custom-call | tf_op jit(solution)/shard_map/lags/pallas_call | solution.py:427
  (1 shorter events, 0.0 us)
Async XLA Ops:
  1.8 4.7 %collective-permute-start = (bf16[64,384]{1,0:T(8,128)(2,1)S(1)}, bf16[64,384]{1,0:T(8,128)(2,1)S(1)}, u32[]{:S(2)}, u32[]{:S(2)}) collective-permute-start(bf16[64,384]{1,0:T(8,128)(2,1)S(1)} %get-tuple-element.23), channel_id=1, source_target_pairs={{0,3},{1,2},{2,1},{3,0},{4,7},{5,6},{6,5},{7,4},{8,11},{9,10},{10,... | collective-permute-start | bytes 147464 | tf_op jit(solution)/shard_map/ppermute | solution.py:424
  3.7 5.3 %collective-permute-start.3 = (bf16[64,384]{1,0:T(8,128)(2,1)S(1)}, bf16[64,384]{1,0:T(8,128)(2,1)S(1)}, u32[]{:S(2)}, u32[]{:S(2)}) collective-permute-start(bf16[64,384]{1,0:T(8,128)(2,1)S(1)} %get-tuple-element.29), channel_id=1, source_target_pairs={{0,1},{1,0},{2,5},{3,4},{4,3},{5,2},{6,9},{7,8},{8,7},{9,6},{10,13... | collective-permute-start | bytes 147464 | tf_op jit(solution)/shard_map/ppermute | solution.py:424
  4.7 4.4 %collective-permute-start.4 = (bf16[64,384]{1,0:T(8,128)(2,1)S(1)}, bf16[64,384]{1,0:T(8,128)(2,1)S(1)}, u32[]{:S(2)}, u32[]{:S(2)}) collective-permute-start(bf16[64,384]{1,0:T(8,128)(2,1)S(1)} %get-tuple-element.30), channel_id=1, source_target_pairs={{0,1},{1,0},{2,4},{3,5},{4,2},{5,3},{6,8},{7,9},{8,6},{9,7},{10,12... | collective-permute-start | bytes 147464 | tf_op jit(solution)/shard_map/ppermute | solution.py:424
  6.6 1.3 %collective-permute-start.1 = (bf16[64,384]{1,0:T(8,128)(2,1)S(1)}, bf16[64,384]{1,0:T(8,128)(2,1)S(1)}, u32[]{:S(2)}, u32[]{:S(2)}) collective-permute-start(bf16[64,384]{1,0:T(8,128)(2,1)S(1)} %get-tuple-element.27), channel_id=1, source_target_pairs={{0,2},{1,3},{2,0},{3,1},{4,6},{5,7},{6,4},{7,5},{8,10},{9,11},{10,... | collective-permute-start | bytes 147464 | tf_op jit(solution)/shard_map/ppermute | solution.py:424
  6.7 1.4 %collective-permute-start.2 = (bf16[64,384]{1,0:T(8,128)(2,1)S(1)}, bf16[64,384]{1,0:T(8,128)(2,1)S(1)}, u32[]{:S(2)}, u32[]{:S(2)}) collective-permute-start(bf16[64,384]{1,0:T(8,128)(2,1)S(1)} %get-tuple-element.28), channel_id=1, source_target_pairs={{0,2},{1,3},{2,0},{3,1},{4,6},{5,7},{6,4},{7,5},{8,10},{9,11},{10,... | collective-permute-start | bytes 147464 | tf_op jit(solution)/shard_map/ppermute | solution.py:424

commit v13 on v12

--- a/solution.py
+++ b/solution.py
@@ -19,8 +19,8 @@
 VALID = 16
 SLOT = 24
 WIDE = 3 * LANE
-LAG_STEP = 4 * LANE
-STEP = 2 * LANE
+LAG_STEP = 6 * LANE
+STEP = 4 * LANE
 FINE = 16
 F32 = jnp.float32
 BF16 = jnp.bfloat16
@@ -47,7 +47,7 @@
 
 def fourier_rows(samples):
     stretches = -(-samples // STEP)
-    sizes = [round_to(stretches)] * 3 + [STEP // FINE] * 2 + [FINE] * 2
+    sizes = [round_to(stretches)] * 2 + [round_to(stretches * STEP // LANE)] + [STEP // FINE] * 2 + [FINE] * 2
     return [sum(sizes[:i]) for i in range(len(sizes) + 1)], stretches
 
 
@@ -85,7 +85,7 @@
     put_rows(0, cosine)
     put_rows(1, jnp.where(imag, -sine, sine))
     rows = starts[3] - starts[2]
-    number = iota((rows, WIDE), 0) * STEP + iota((rows, WIDE), 1)
+    number = iota((rows, WIDE), 0) * LANE + iota((rows, WIDE), 1)
     put_rows(2, 0.5 - 0.5 * cos_sin((2 * number).astype(F32), points)[0])
     cosine, sine, imag, known = of(STEP // FINE, FINE)
     put_rows(3, jnp.where(known, jnp.where(imag, -sine, cosine), 0.0))
@@ -148,8 +148,8 @@
         copy.start()
 
     odd = lax.rem(lax.axis_index("tile"), 2)
-    col = iota((STEP, STEP), 0)
-    row = iota((STEP, STEP), 1)
+    col = iota((2 * LANE, 2 * LANE), 0)
+    row = iota((2 * LANE, 2 * LANE), 1)
 
     def bin_of(lane):
         tail = lane & (HALF - 1)
@@ -188,7 +188,9 @@
         x = traces[:, at : min(at + STEP, samples)]
         if at + STEP > samples:
             x = jnp.concatenate([x, jnp.zeros((lines, at + STEP - samples), F32)], axis=1)
-        x = x * factors[taper_at + j : taper_at + j + 1, :STEP]
+        first = taper_at + at // LANE
+        taper = [factors[first + i : first + i + 1, :LANE] for i in range(STEP // LANE)]
+        x = x * jnp.concatenate(taper, axis=1)
         x_high = x.astype(BF16)
         x_low = (x - x_high.astype(F32)).astype(BF16)
         left.append(jnp.concatenate([x_high, x_low, x_high], axis=1))

time: 10.5 us -> 10.5 us (level)
  no operation moved by 1% of the time
where the time goes in v13:
time: 10.5 us; the launch traced here: 10.3 us
  starting transfers between devices  5.02 us (48%)
  Pallas kernels  4.31 us (41%)
  waiting for transfers between devices  0.97 us (9%)
    ppermute x5, starting transfers between devices, exchange(): return lax.ppermute(array, axes, pairs)  5.02 us
    pallas_call x5, Pallas kernels, call(): pl.pallas_call(kernel, in_specs=[vmem] * len(inputs), compiler_params=plt...  2.51 us
    pallas_call x1, Pallas kernels, on_device(): pl.pallas_call(lambda *refs: spectra_kernel(per, seg, samples, [1] + [way...  1.8 us
    ppermute x5, waiting for transfers between devices, exchange(): return lax.ppermute(array, axes, pairs)  0.97 us
  transfers between devices with their start and end apart: 5, of which 4 were waited for; matrix products, arithmetic and copies ran while one was open for 0% of the time, Pallas kernels for 13%

profile of v13, /device:TPU:3, one launch (start us, length us, event | category | flops | bytes accessed | tf_op | source)
XLA Modules:
  0.0 10.3 jit_solution(14124917607541104939)
XLA Ops:
  0.0 1.8 %spectra.1 = (bf16[64,384]{1,0:T(8,128)(2,1)S(1)}, bf16[64,384]{1,0:T(8,128)(2,1)S(1)}, bf16[64,384]{1,0:T(8,128)(2,1)S(1)}, bf16[64,384]{1,0:T(8,128)(2,1)S(1)}...) custom-call(s32[1,2,4]{2,1,0:T(2,128)} %refs_0_.1, s32[1,2]{1,0:T(1,128)} %refs_1_.1, ...), custom_call_target="tpu_custom_call" | custom-call | tf_op jit(solution)/shard_map/spectra/pallas_call | solution.py:448
  1.8 1.9 %collective-permute-start = (bf16[64,384]{1,0:T(8,128)(2,1)S(1)}, bf16[64,384]{1,0:T(8,128)(2,1)S(1)}, u32[]{:S(2)}, u32[]{:S(2)}) collective-permute-start(bf16[64,384]{1,0:T(8,128)(2,1)S(1)} %get-tuple-element.23), channel_id=1, source_target_pairs={{0,3},{1,2},{2,1},{3,0},{4,7},{5,6},{6,5},{7,4},{8,11},{9,10},{10,... | collective-permute-start | bytes 147464 | tf_op jit(solution)/shard_map/ppermute | solution.py:426
  3.7 1.1 %collective-permute-start.3 = (bf16[64,384]{1,0:T(8,128)(2,1)S(1)}, bf16[64,384]{1,0:T(8,128)(2,1)S(1)}, u32[]{:S(2)}, u32[]{:S(2)}) collective-permute-start(bf16[64,384]{1,0:T(8,128)(2,1)S(1)} %get-tuple-element.29), channel_id=1, source_target_pairs={{0,1},{1,0},{2,5},{3,4},{4,3},{5,2},{6,9},{7,8},{8,7},{9,6},{10,13... | collective-permute-start | bytes 147464 | tf_op jit(solution)/shard_map/ppermute | solution.py:426
  4.7 1.5 %collective-permute-start.4 = (bf16[64,384]{1,0:T(8,128)(2,1)S(1)}, bf16[64,384]{1,0:T(8,128)(2,1)S(1)}, u32[]{:S(2)}, u32[]{:S(2)}) collective-permute-start(bf16[64,384]{1,0:T(8,128)(2,1)S(1)} %get-tuple-element.30), channel_id=1, source_target_pairs={{0,1},{1,0},{2,4},{3,5},{4,2},{5,3},{6,8},{7,9},{8,6},{9,7},{10,12... | collective-permute-start | bytes 147464 | tf_op jit(solution)/shard_map/ppermute | solution.py:426
  6.3 0.3 %ready.1 = (f32[256,512]{1,0:T(8,128)S(1)}, f32[32,512]{1,0:T(8,128)S(1)}) custom-call(bf16[64,384]{1,0:T(8,128)(2,1)S(1)} %get-tuple-element.20.refs_0_), custom_call_target="tpu_custom_call" | custom-call | tf_op jit(solution)/shard_map/ready/pallas_call | solution.py:429
  6.5 0.0 collective-permute-done.refs_3_.refs_0_
  6.6 0.1 collective-permute-start.1
  6.6 0.5 %collective-permute-start.2 = (bf16[64,384]{1,0:T(8,128)(2,1)S(1)}, bf16[64,384]{1,0:T(8,128)(2,1)S(1)}, u32[]{:S(2)}, u32[]{:S(2)}) collective-permute-start(bf16[64,384]{1,0:T(8,128)(2,1)S(1)} %get-tuple-element.28), channel_id=1, source_target_pairs={{0,2},{1,3},{2,0},{3,1},{4,6},{5,7},{6,4},{7,5},{8,10},{9,11},{10,... | collective-permute-start | bytes 147464 | tf_op jit(solution)/shard_map/ppermute | solution.py:426
  7.1 0.5 %early.1 = (f32[96,384]{1,0:T(8,128)S(1)}, f32[96,128]{1,0:T(8,128)S(1)}) custom-call(s32[4,24]{1,0:T(4,128)S(1)} %get-tuple-element.19.refs_0_, f32[256,512]{1,0:T(8,128)S(1)} %get-tuple-element.21.refs_1_.refs_2_, f32[32,512]{1,0:T(8,128)S(1)} %get-tuple-element.22.refs_2_._, bf16[64,384]{1,0:T(8,128)(2,1)S(1)} %collective-permute-done.refs_3_.refs_0_), custom_call_target="tpu_custom_call" | custom-call | flops 99999997952 | bytes 1000000000 | tf_op jit(solution)/shard_map/early/pallas_call | solution.py:429
  7.6 0.2 %collective-permute-done.1.refs_4_ = bf16[64,384]{1,0:T(8,128)(2,1)S(1)} collective-permute-done((bf16[64,384]{1,0:T(8,128)(2,1)S(1)}, bf16[64,384]{1,0:T(8,128)(2,1)S(1)}, u32[]{:S(2)}, u32[]{:S(2)}) %collective-permute-start.1) | collective-permute-done | bytes 49184 | tf_op jit(solution)/shard_map/ppermute | solution.py:426
  7.9 0.2 %collective-permute-done.2.refs_5_ = bf16[64,384]{1,0:T(8,128)(2,1)S(1)} collective-permute-done((bf16[64,384]{1,0:T(8,128)(2,1)S(1)}, bf16[64,384]{1,0:T(8,128)(2,1)S(1)}, u32[]{:S(2)}, u32[]{:S(2)}) %collective-permute-start.2) | collective-permute-done | bytes 49184 | tf_op jit(solution)/shard_map/ppermute | solution.py:426
  8.0 0.6 %middle.1.refs_3_ = f32[96,2001]{1,0:T(8,128)S(1)} custom-call(bf16[384,2001]{1,0:T(8,128)(2,1)S(1)} %get-tuple-element.18.refs_0_, f32[96,128]{1,0:T(8,128)S(1)} %get-tuple-element.24.refs_1_, f32[256,512]{1,0:T(8,128)S(1)} %get-tuple-element.21.refs_1_.refs_2_, f32[96,384]{1,0:T(8,128)S(1)} %get-tuple-element.25.refs_3_, ...), custom_call_target="tpu_custom_call" | custom-call | tf_op jit(solution)/shard_map/middle/pallas_call | solution.py:429
  8.6 0.4 %collective-permute-done.3.refs_4_ = bf16[64,384]{1,0:T(8,128)(2,1)S(1)} collective-permute-done((bf16[64,384]{1,0:T(8,128)(2,1)S(1)}, bf16[64,384]{1,0:T(8,128)(2,1)S(1)}, u32[]{:S(2)}, u32[]{:S(2)}) %collective-permute-start.3) | collective-permute-done | bytes 49184 | tf_op jit(solution)/shard_map/ppermute | solution.py:426
  9.0 0.2 %collective-permute-done.4.refs_5_ = bf16[64,384]{1,0:T(8,128)(2,1)S(1)} collective-permute-done((bf16[64,384]{1,0:T(8,128)(2,1)S(1)}, bf16[64,384]{1,0:T(8,128)(2,1)S(1)}, u32[]{:S(2)}, u32[]{:S(2)}) %collective-permute-start.4) | collective-permute-done | bytes 49184 | tf_op jit(solution)/shard_map/ppermute | solution.py:426
  9.2 1.2 %lags.1 = bf16[4,24,2001]{2,1,0:T(8,128)(2,1)} custom-call(bf16[384,2001]{1,0:T(8,128)(2,1)S(1)} %get-tuple-element.18.refs_0_, f32[96,128]{1,0:T(8,128)S(1)} %get-tuple-element.24.refs_1_, f32[256,512]{1,0:T(8,128)S(1)} %get-tuple-element.21.refs_1_.refs_2_, f32[96,2001]{1,0:T(8,128)S(1)} %middle.1.refs_3_, ...), custom_call_target="tpu_custom_call" | custom-call | tf_op jit(solution)/shard_map/lags/pallas_call | solution.py:429
  (1 shorter events, 0.0 us)
Async XLA Ops:
  1.8 4.7 %collective-permute-start = (bf16[64,384]{1,0:T(8,128)(2,1)S(1)}, bf16[64,384]{1,0:T(8,128)(2,1)S(1)}, u32[]{:S(2)}, u32[]{:S(2)}) collective-permute-start(bf16[64,384]{1,0:T(8,128)(2,1)S(1)} %get-tuple-element.23), channel_id=1, source_target_pairs={{0,3},{1,2},{2,1},{3,0},{4,7},{5,6},{6,5},{7,4},{8,11},{9,10},{10,... | collective-permute-start | bytes 147464 | tf_op jit(solution)/shard_map/ppermute | solution.py:426
  3.7 5.3 %collective-permute-start.3 = (bf16[64,384]{1,0:T(8,128)(2,1)S(1)}, bf16[64,384]{1,0:T(8,128)(2,1)S(1)}, u32[]{:S(2)}, u32[]{:S(2)}) collective-permute-start(bf16[64,384]{1,0:T(8,128)(2,1)S(1)} %get-tuple-element.29), channel_id=1, source_target_pairs={{0,1},{1,0},{2,5},{3,4},{4,3},{5,2},{6,9},{7,8},{8,7},{9,6},{10,13... | collective-permute-start | bytes 147464 | tf_op jit(solution)/shard_map/ppermute | solution.py:426
  4.7 4.4 %collective-permute-start.4 = (bf16[64,384]{1,0:T(8,128)(2,1)S(1)}, bf16[64,384]{1,0:T(8,128)(2,1)S(1)}, u32[]{:S(2)}, u32[]{:S(2)}) collective-permute-start(bf16[64,384]{1,0:T(8,128)(2,1)S(1)} %get-tuple-element.30), channel_id=1, source_target_pairs={{0,1},{1,0},{2,4},{3,5},{4,2},{5,3},{6,8},{7,9},{8,6},{9,7},{10,12... | collective-permute-start | bytes 147464 | tf_op jit(solution)/shard_map/ppermute | solution.py:426
  6.6 1.3 %collective-permute-start.1 = (bf16[64,384]{1,0:T(8,128)(2,1)S(1)}, bf16[64,384]{1,0:T(8,128)(2,1)S(1)}, u32[]{:S(2)}, u32[]{:S(2)}) collective-permute-start(bf16[64,384]{1,0:T(8,128)(2,1)S(1)} %get-tuple-element.27), channel_id=1, source_target_pairs={{0,2},{1,3},{2,0},{3,1},{4,6},{5,7},{6,4},{7,5},{8,10},{9,11},{10,... | collective-permute-start | bytes 147464 | tf_op jit(solution)/shard_map/ppermute | solution.py:426
  6.6 1.4 %collective-permute-start.2 = (bf16[64,384]{1,0:T(8,128)(2,1)S(1)}, bf16[64,384]{1,0:T(8,128)(2,1)S(1)}, u32[]{:S(2)}, u32[]{:S(2)}) collective-permute-start(bf16[64,384]{1,0:T(8,128)(2,1)S(1)} %get-tuple-element.28), channel_id=1, source_target_pairs={{0,2},{1,3},{2,0},{3,1},{4,6},{5,7},{6,4},{7,5},{8,10},{9,11},{10,... | collective-permute-start | bytes 147464 | tf_op jit(solution)/shard_map/ppermute | solution.py:426
